TPU v7x, 32 devices: a whole 2x2x4 slice. The times are simulated.
32 devices in a mesh: tm: 8 (over z, y), patch: 4 (over x, core).
Axes of the slice: x: 2, y: 2, z: 4, core: 2. Of those that a mesh axis runs over, the one named last changes fastest.
Arguments:
- latents: bfloat16 [1024, 1024], replicated, may hold values from -6 to 6
- tokens: bfloat16 [65536, 1024], P(('tm', 'patch')), may hold values from -300 to 300, as said below
- w_query: bfloat16 [1024, 1024], replicated, may hold values from -0.1875 to 0.1875
- w_key: bfloat16 [1024, 1024], replicated, may hold values from -0.1875 to 0.1875
- w_value: bfloat16 [1024, 1024], replicated, may hold values from -0.1875 to 0.1875
- w_out: bfloat16 [1024, 1024], P(None, 'patch'), may hold values from -0.1875 to 0.1875
Outputs:
- resampled: bfloat16 [1024, 1024], P('tm', 'patch')
Inputs may be any that keep to these rules, and one draw needn't show every extreme that they name: `tokens`: token features; a few rows may be far larger than the rest.
All inputs are finite; a program needn't handle non-finite values.
Results may differ from a plain program's by a relative error of at most 0.006.
The roundings to bfloat16 on the way count: a program that leaves them out, or rounds other values in their place, can miss the bound.
Values may be sent and summed in bfloat16 or wider, within the bound.
No kernel may reach another device: no remote copies, remote signals or barrier semaphores. Data moves between devices by JAX's collectives and lax.ppermute only.
A program may use at most 192 MiB of HBM per device.

v0:
```python
import math

import jax
import jax.numpy as jnp
from jax import lax
from jax.sharding import PartitionSpec as P

H = 8


def block_part(query, block, w_key, w_value):
    head_size = query.shape[1] // H
    keys = jnp.dot(block, w_key, preferred_element_type=jnp.float32).astype(jnp.bfloat16)
    vals = jnp.dot(block, w_value, preferred_element_type=jnp.float32).astype(jnp.bfloat16)
    scale = 1.0 / math.sqrt(head_size)
    peaks, totals, parts = ([], [], [])
    for head in range(H):
        cols = slice(head * head_size, (head + 1) * head_size)
        score = jnp.dot(query[:, cols], keys[:, cols].T, preferred_element_type=jnp.float32) * scale
        top = jnp.max(score, axis=1)
        weight = jnp.exp(score - top[:, None]).astype(jnp.bfloat16)
        peaks.append(top)
        totals.append(jnp.sum(weight.astype(jnp.float32), axis=1))
        parts.append(jnp.dot(weight, vals[:, cols], preferred_element_type=jnp.float32))
    return (jnp.stack(peaks, axis=1), jnp.stack(totals, axis=1), jnp.concatenate(parts, axis=1))


def finish(merged, total):
    head_size = merged.shape[1] // H
    attended = merged / jnp.repeat(total, head_size, axis=1)
    return (
        attended * lax.rsqrt(jnp.mean(attended * attended, axis=1, keepdims=True) + 1e-06)
    ).astype(jnp.bfloat16)


def per_device(latents, tokens, w_query, w_key, w_value, w_out):
    head_size = latents.shape[1] // H
    query = jnp.dot(latents, w_query, preferred_element_type=jnp.float32).astype(jnp.bfloat16)
    peaks, totals, parts = block_part(query, tokens, w_key, w_value)
    peak = lax.pmax(peaks.astype(jnp.bfloat16), ("tm", "patch")).astype(peaks.dtype)
    factor = jnp.exp(peaks - peak)
    scaled = parts * jnp.repeat(factor, head_size, axis=1)
    own_rows, own_total = (
        lax.psum_scatter(scaled, ("tm", "patch"), scatter_dimension=0, tiled=True),
        lax.psum_scatter(totals * factor, ("tm", "patch"), scatter_dimension=0, tiled=True),
    )
    normed = lax.all_gather(finish(own_rows, own_total), "patch", axis=0, tiled=True)
    return jnp.dot(normed, w_out, preferred_element_type=jnp.float32).astype(jnp.bfloat16)


def solution(mesh):
    return jax.shard_map(
        per_device,
        mesh=mesh,
        in_specs=(P(), P(("tm", "patch"), None), P(), P(), P(), P(None, "patch")),
        out_specs=P("tm", "patch"),
        check_vma=False,
    )
```

profile of v0, /device:TPU:0, one launch (start us, length us, event | category | flops | bytes accessed | tf_op | source)
XLA Modules:
  0.0 410.4 jit_solution(9795586393636509564)
XLA Ops:
  6.5 0.0 copy-start
  6.5 0.0 reduce-scatter.9.cloned.1.call-start
  6.5 1.6 copy-done
  8.1 7.6 %convolution_convert_fusion.1 = bf16[2048,1024]{1,0:T(8,128)(2,1)S(1)} fusion(bf16[2048,1024]{1,0:T(8,128)(2,1)} %param.7, bf16[1024,1024]{1,0:T(8,128)(2,1)S(1)} %copy-done), kind=kOutput, calls=%fused_computation.26 | convolution fusion | flops 4297064448 | bytes 10485760 | tf_op jit(solution)/shard_map/dot_general | solution.py:13
  15.7 0.0 copy-done.4
  15.8 2.3 convolution_convert_fusion.2
  18.1 4.5 %multiply_reduce_fusion.7 = (f32[1024]{0:T(1024)S(1)}, f32[1024,2048]{1,0:T(8,128)}) fusion(bf16[2048,1024]{1,0:T(8,128)(2,1)S(1)} %convolution_convert_fusion.1, bf16[1024,1024]{1,0:T(8,128)(2,1)S(1)} %convolution_convert_fusion.2), kind=kOutput, calls=%fused_computation.23 | convolution fusion | flops 541064192 | bytes 9179136 | tf_op jit(solution)/shard_map/dot_general | solution.py:19
  22.6 4.5 %multiply_reduce_fusion.6 = (f32[1024]{0:T(1024)S(1)}, f32[1024,2048]{1,0:T(8,128)}) fusion(bf16[2048,1024]{1,0:T(8,128)(2,1)S(1)} %convolution_convert_fusion.1, bf16[1024,1024]{1,0:T(8,128)(2,1)S(1)} %convolution_convert_fusion.2), kind=kOutput, calls=%fused_computation.22 | convolution fusion | flops 541064192 | bytes 9179136 | tf_op jit(solution)/shard_map/dot_general | solution.py:19
  27.1 4.5 %multiply_reduce_fusion.5 = (f32[1024]{0:T(1024)S(1)}, f32[1024,2048]{1,0:T(8,128)}) fusion(bf16[2048,1024]{1,0:T(8,128)(2,1)S(1)} %convolution_convert_fusion.1, bf16[1024,1024]{1,0:T(8,128)(2,1)S(1)} %convolution_convert_fusion.2), kind=kOutput, calls=%fused_computation.21 | convolution fusion | flops 541064192 | bytes 9179136 | tf_op jit(solution)/shard_map/dot_general | solution.py:19
  31.5 4.5 %multiply_reduce_fusion.4 = (f32[1024]{0:T(1024)S(1)}, f32[1024,2048]{1,0:T(8,128)}) fusion(bf16[2048,1024]{1,0:T(8,128)(2,1)S(1)} %convolution_convert_fusion.1, bf16[1024,1024]{1,0:T(8,128)(2,1)S(1)} %convolution_convert_fusion.2), kind=kOutput, calls=%fused_computation.20 | convolution fusion | flops 541064192 | bytes 9179136 | tf_op jit(solution)/shard_map/dot_general | solution.py:19
  36.0 4.5 %multiply_reduce_fusion.3 = (f32[1024]{0:T(1024)S(1)}, f32[1024,2048]{1,0:T(8,128)}) fusion(bf16[2048,1024]{1,0:T(8,128)(2,1)S(1)} %convolution_convert_fusion.1, bf16[1024,1024]{1,0:T(8,128)(2,1)S(1)} %convolution_convert_fusion.2), kind=kOutput, calls=%fused_computation.19 | convolution fusion | flops 541064192 | bytes 9179136 | tf_op jit(solution)/shard_map/dot_general | solution.py:19
  40.5 4.5 %multiply_reduce_fusion.2 = (f32[1024]{0:T(1024)S(1)}, f32[1024,2048]{1,0:T(8,128)}) fusion(bf16[2048,1024]{1,0:T(8,128)(2,1)S(1)} %convolution_convert_fusion.1, bf16[1024,1024]{1,0:T(8,128)(2,1)S(1)} %convolution_convert_fusion.2), kind=kOutput, calls=%fused_computation.18 | convolution fusion | flops 541064192 | bytes 9179136 | tf_op jit(solution)/shard_map/dot_general | solution.py:19
  44.9 4.5 %multiply_reduce_fusion.1 = (f32[1024]{0:T(1024)S(1)}, f32[1024,2048]{1,0:T(8,128)}) fusion(bf16[2048,1024]{1,0:T(8,128)(2,1)S(1)} %convolution_convert_fusion.1, bf16[1024,1024]{1,0:T(8,128)(2,1)S(1)} %convolution_convert_fusion.2), kind=kOutput, calls=%fused_computation.17 | convolution fusion | flops 541064192 | bytes 9179136 | tf_op jit(solution)/shard_map/dot_general | solution.py:19
  49.4 4.5 %multiply_reduce_fusion = (f32[1024]{0:T(1024)S(1)}, f32[1024,2048]{1,0:T(8,128)}) fusion(bf16[2048,1024]{1,0:T(8,128)(2,1)S(1)} %convolution_convert_fusion.1, bf16[1024,1024]{1,0:T(8,128)(2,1)S(1)} %convolution_convert_fusion.2), kind=kOutput, calls=%fused_computation.16 | convolution fusion | flops 541064192 | bytes 9179136 | tf_op jit(solution)/shard_map/dot_general | solution.py:19
  53.9 0.1 stack.38
  54.0 42.2 %pmax.7 = bf16[1024,8]{0,1:T(8,128)(2,1)S(1)} all-reduce(bf16[1024,8]{0,1:T(8,128)(2,1)S(1)} %convert_element_type.80), channel_id=1, replica_groups=mesh['tm'=8,'patch'=4] {'tm','patch'}, use_global_device_ids=true, to_apply=%region_8.0 | all-reduce | flops 8192 | bytes 32768 | tf_op jit(solution)/shard_map/pmax | solution.py:40
  96.1 4.5 %convert_reduce_fusion.6 = f32[1024]{0:T(1024)S(1)} fusion(f32[1024]{0:T(1024)S(1)} %get-tuple-element.9, f32[1024,2048]{1,0:T(8,128)} %get-tuple-element.10), kind=kLoop, calls=%fused_computation.6 | loop fusion | flops 10484736 | bytes 8396800 | tf_op jit(solution)/shard_map/reduce_sum | solution.py:23
  100.6 0.0 slice-start.13
  100.6 0.0 slice-start.8
  100.7 4.5 %convert_reduce_fusion.5 = f32[1024]{0:T(1024)S(1)} fusion(f32[1024]{0:T(1024)S(1)} %get-tuple-element.11, f32[1024,2048]{1,0:T(8,128)} %get-tuple-element.12), kind=kLoop, calls=%fused_computation.5 | loop fusion | flops 10484736 | bytes 8396800 | tf_op jit(solution)/shard_map/reduce_sum | solution.py:23
  105.1 0.0 slice-start.9
  105.2 4.7 %convert_reduce_fusion.4 = f32[1024]{0:T(1024)S(1)} fusion(f32[1024]{0:T(1024)S(1)} %get-tuple-element.13, f32[1024,2048]{1,0:T(8,128)} %get-tuple-element.14), kind=kLoop, calls=%fused_computation.4 | loop fusion | flops 10484736 | bytes 8396800 | tf_op jit(solution)/shard_map/reduce_sum | solution.py:23
  109.8 0.0 slice-start.4
  109.9 0.0 slice-start.18
  109.9 1.9 convert_reduce_fusion.3
  111.8 0.0 slice-start.5
  111.9 0.0 slice-start
  111.9 1.9 convert_reduce_fusion.2
  113.8 0.0 slice-done.4
  113.8 0.8 slice-done.5
  114.7 1.9 convert_reduce_fusion.1
  116.6 0.5 slice-done.1
  117.1 1.9 convert_reduce_fusion
  119.0 1.9 convert_reduce_fusion.7
  121.0 0.1 stack.47
  121.1 1.0 copy.10
  122.1 0.0 reduce-scatter.9.cloned.1.call-update
  122.1 0.3 reduce-scatter.7.cloned.1.call-start
  122.4 7.4 %convolution_convert_fusion = bf16[2048,1024]{1,0:T(8,128)(2,1)S(1)} fusion(bf16[2048,1024]{1,0:T(8,128)(2,1)} %param.7, bf16[1024,1024]{1,0:T(8,128)(2,1)} %param.10), kind=kOutput, calls=%fused_computation.25 | convolution fusion | flops 4297064448 | bytes 10485760 | tf_op jit(solution)/shard_map/dot_general | solution.py:14
  129.8 0.0 slice-start.16
  129.8 7.4 %convolution_dynamic-update-slice_fusion.7 = f32[1024,1024]{0,1:T(8,128)} fusion(bf16[2048,1024]{1,0:T(8,128)(2,1)S(1)} %convolution_convert_fusion, f32[1024,2048]{1,0:T(8,128)} %get-tuple-element.8, f32[1024]{0:T(1024)S(1)} %get-tuple-element.7), kind=kOutput, calls=%fused_computation.35 | convolution fusion | flops 543162368 | bytes 9441280 | tf_op jit(solution)/shard_map/dot_general | solution.py:24
  137.2 6.0 %convolution_dynamic-update-slice_fusion.6 = f32[1024,1024]{0,1:T(8,128)} fusion(f32[1024,1024]{0,1:T(8,128)} %convolution_dynamic-update-slice_fusion.7, bf16[2048,1024]{1,0:T(8,128)(2,1)S(1)} %convolution_convert_fusion, f32[1024,2048]{1,0:T(8,128)} %get-tuple-element.10, f32[1024]{0:T(1024)S(1)} %get-tuple-element.9), kind=kOutput, calls=%fused_computation.34 | convolution fusion | flops 543162368 | bytes 9441280 | tf_op jit(solution)/shard_map/dot_general | solution.py:24
  143.3 6.1 %convolution_dynamic-update-slice_fusion.5 = f32[1024,1024]{0,1:T(8,128)} fusion(f32[1024,1024]{0,1:T(8,128)} %convolution_dynamic-update-slice_fusion.6, bf16[2048,1024]{1,0:T(8,128)(2,1)S(1)} %convolution_convert_fusion, f32[1024,2048]{1,0:T(8,128)} %get-tuple-element.12, f32[1024]{0:T(1024)S(1)} %get-tuple-element.11), kind=kOutput, calls=%fused_computation.33 | convolution fusion | flops 543162368 | bytes 9441280 | tf_op jit(solution)/shard_map/dot_general | solution.py:24
  149.3 0.0 slice-start.11
  149.4 0.0 slice-start.6
  149.4 2.6 convolution_dynamic-update-slice_fusion.4
  151.9 0.0 slice-done.15
  151.9 4.0 convolution_dynamic-update-slice_fusion.3
  155.9 3.8 convolution_dynamic-update-slice_fusion.2
  159.7 0.0 slice-done.7
  159.7 3.7 convolution_dynamic-update-slice_fusion.1
  163.5 3.6 convolution_dynamic-update-slice_fusion
  167.1 5.2 %bitcast_multiply_fusion = f32[1024,1024]{0,1:T(8,128)} fusion(f32[1024,1024]{0,1:T(8,128)} %convolution_dynamic-update-slice_fusion, f32[1024,8]{0,1:T(8,128)S(1)} %get-tuple-element.6), kind=kLoop, calls=%fused_computation.24 | loop fusion | flops 1048576 | bytes 8421376 | tf_op jit(solution)/shard_map/mul | solution.py:42
  172.3 5.4 %copy.8 = f32[1024,1024]{1,0:T(8,128)} copy(f32[1024,1024]{0,1:T(8,128)} %bitcast_multiply_fusion) | data formatting | bytes 8388608
  177.7 0.0 reduce-scatter.7.cloned.1.call-update
  177.7 78.1 %reduce-scatter.9.cloned.1.call-done = f32[32,8]{1,0:T(8,128)} async-done(((f32[1024,8]{1,0:T(8,128)}), f32[32,8]{1,0:T(8,128)}) %reduce-scatter.9.cloned.1.call-update) | async-done | bytes 1040
  255.8 0.8 copy.11
  256.6 138.6 %reduce-scatter.7.cloned.1.call-done = f32[32,1024]{1,0:T(8,128)} async-done(((f32[1024,1024]{1,0:T(8,128)}), f32[32,1024]{1,0:T(8,128)}) %reduce-scatter.7.cloned.1.call-update) | async-done | bytes 131088
  395.2 1.1 copy.9
  396.3 0.2 multiply_reduce_fusion.8
  396.4 0.1 multiply_convert_fusion
  396.5 0.1 copy.7
  396.6 5.8 %all_gather.3 = bf16[128,1024]{1,0:T(8,128)(2,1)S(1)} all-gather(bf16[32,1024]{1,0:T(8,128)(2,1)S(1)} %copy.7), channel_id=1, replica_groups=mesh['tm'=8,'patch'=4] {'patch'}, dimensions={0}, use_global_device_ids=true | all-gather | bytes 327680 | tf_op jit(solution)/shard_map/all_gather | solution.py:47
  402.4 0.9 convolution_convert_fusion.3
  (47 shorter events, 0.1 us)
Async XLA Ops:
  6.5 1.6 copy-start
  6.5 249.3 %reduce-scatter.9.cloned.1.call-start = ((), (), s32[]{:S(2)}) async-start(), calls=%async_computation.3 | async-start | bytes 540672
  8.1 7.6 %copy-start.4 = (bf16[1024,1024]{1,0:T(8,128)(2,1)S(1)}, bf16[1024,1024]{1,0:T(8,128)(2,1)}, u32[]{:S(2)}) copy-start(bf16[1024,1024]{1,0:T(8,128)(2,1)} %param.6) | copy-start | bytes 6291460
  8.1 7.6 %copy-start.5 = (bf16[1024,1024]{1,0:T(8,128)(2,1)S(1)}, bf16[1024,1024]{1,0:T(8,128)(2,1)}, u32[]{:S(2)}) copy-start(bf16[1024,1024]{1,0:T(8,128)(2,1)} %param.8) | copy-start | bytes 6291460
  96.1 13.7 %slice-start.12 = ((s8[8388608]{0:T(1024)(128)(4,1)}), s8[4194304]{0:T(1024)(128)(4,1)S(1)}, s32[]{:S(2)}) async-start(s8[8388608]{0:T(1024)(128)(4,1)} %bitcast.46), calls=%async_computation.16 | async-start | bytes 8388608
  100.6 9.2 %slice-start.13 = ((s8[8388608]{0:T(1024)(128)(4,1)}), s8[4194304]{0:T(1024)(128)(4,1)S(1)}, s32[]{:S(2)}) async-start(s8[8388608]{0:T(1024)(128)(4,1)} %bitcast.46), calls=%async_computation.17 | async-start | bytes 8388608
  100.6 11.2 %slice-start.8 = ((s8[8388608]{0:T(1024)(128)(4,1)}), s8[4194304]{0:T(1024)(128)(4,1)S(1)}, s32[]{:S(2)}) async-start(s8[8388608]{0:T(1024)(128)(4,1)} %bitcast.42), calls=%async_computation.12 | async-start | bytes 8388608
  105.1 6.7 %slice-start.9 = ((s8[8388608]{0:T(1024)(128)(4,1)}), s8[4194304]{0:T(1024)(128)(4,1)S(1)}, s32[]{:S(2)}) async-start(s8[8388608]{0:T(1024)(128)(4,1)} %bitcast.42), calls=%async_computation.13 | async-start | bytes 8388608
  109.8 4.0 slice-start.4
  109.9 9.1 %slice-start.18 = ((s8[8388608]{0:T(1024)(128)(4,1)}), s8[4194304]{0:T(1024)(128)(4,1)S(1)}, s32[]{:S(2)}) async-start(s8[8388608]{0:T(1024)(128)(4,1)} %bitcast.52), calls=%async_computation.22 | async-start | bytes 8388608
  111.8 2.8 slice-start.5
  111.9 4.7 %slice-start = ((s8[8388608]{0:T(1024)(128)(4,1)}), s8[4194304]{0:T(1024)(128)(4,1)S(1)}, s32[]{:S(2)}) async-start(s8[8388608]{0:T(1024)(128)(4,1)} %bitcast.34), calls=%async_computation.4 | async-start | bytes 8388608
  114.7 2.4 slice-start.1
  114.7 4.4 %slice-start.19 = ((s8[8388608]{0:T(1024)(128)(4,1)}), s8[4194304]{0:T(1024)(128)(4,1)S(1)}, s32[]{:S(2)}) async-start(s8[8388608]{0:T(1024)(128)(4,1)} %bitcast.52), calls=%async_computation.23 | async-start | bytes 8388608
  122.1 273.0 %reduce-scatter.7.cloned.1.call-start = ((), (), s32[]{:S(2)}) async-start(), calls=%async_computation.2 | async-start | bytes 4325376
  129.8 19.5 %copy-start.2 = (bf16[2048,1024]{1,0:T(8,128)(2,1)}, bf16[2048,1024]{1,0:T(8,128)(2,1)S(1)}, u32[]{:S(2)}) copy-start(bf16[2048,1024]{1,0:T(8,128)(2,1)S(1)} %convolution_convert_fusion) | copy-start | bytes 12582916
  129.8 19.5 %slice-start.16 = ((s8[8388608]{0:T(1024)(128)(4,1)}), s8[4194304]{0:T(1024)(128)(4,1)S(1)}, s32[]{:S(2)}) async-start(s8[8388608]{0:T(1024)(128)(4,1)} %bitcast.50), calls=%async_computation.20 | async-start | bytes 8388608
  137.2 12.1 %slice-start.17 = ((s8[8388608]{0:T(1024)(128)(4,1)}), s8[4194304]{0:T(1024)(128)(4,1)S(1)}, s32[]{:S(2)}) async-start(s8[8388608]{0:T(1024)(128)(4,1)} %bitcast.50), calls=%async_computation.21 | async-start | bytes 8388608
  137.2 14.7 %slice-start.14 = ((s8[8388608]{0:T(1024)(128)(4,1)}), s8[4194304]{0:T(1024)(128)(4,1)S(1)}, s32[]{:S(2)}) async-start(s8[8388608]{0:T(1024)(128)(4,1)} %bitcast.48), calls=%async_computation.18 | async-start | bytes 8388608
  143.3 8.7 %slice-start.15 = ((s8[8388608]{0:T(1024)(128)(4,1)}), s8[4194304]{0:T(1024)(128)(4,1)S(1)}, s32[]{:S(2)}) async-start(s8[8388608]{0:T(1024)(128)(4,1)} %bitcast.48), calls=%async_computation.19 | async-start | bytes 8388608
  143.3 12.7 %slice-start.10 = ((s8[8388608]{0:T(1024)(128)(4,1)}), s8[4194304]{0:T(1024)(128)(4,1)S(1)}, s32[]{:S(2)}) async-start(s8[8388608]{0:T(1024)(128)(4,1)} %bitcast.44), calls=%async_computation.14 | async-start | bytes 8388608
  149.3 6.6 %slice-start.11 = ((s8[8388608]{0:T(1024)(128)(4,1)}), s8[4194304]{0:T(1024)(128)(4,1)S(1)}, s32[]{:S(2)}) async-start(s8[8388608]{0:T(1024)(128)(4,1)} %bitcast.44), calls=%async_computation.15 | async-start | bytes 8388608
  149.4 10.4 %slice-start.6 = ((s8[8388608]{0:T(1024)(128)(4,1)}), s8[4194304]{0:T(1024)(128)(4,1)S(1)}, s32[]{:S(2)}) async-start(s8[8388608]{0:T(1024)(128)(4,1)} %bitcast.40), calls=%async_computation.10 | async-start | bytes 8388608
  151.9 7.8 %slice-start.7 = ((s8[8388608]{0:T(1024)(128)(4,1)}), s8[4194304]{0:T(1024)(128)(4,1)S(1)}, s32[]{:S(2)}) async-start(s8[8388608]{0:T(1024)(128)(4,1)} %bitcast.40), calls=%async_computation.11 | async-start | bytes 8388608
  155.9 7.5 %slice-start.2 = ((s8[8388608]{0:T(1024)(128)(4,1)}), s8[4194304]{0:T(1024)(128)(4,1)S(1)}, s32[]{:S(2)}) async-start(s8[8388608]{0:T(1024)(128)(4,1)} %bitcast.36), calls=%async_computation.6 | async-start | bytes 8388608
  159.7 3.8 slice-start.3
  167.1 236.2 %copy-start.1 = (bf16[1024,1024]{1,0:T(8,128)(2,1)S(1)}, bf16[1024,1024]{1,0:T(8,128)(2,1)}, u32[]{:S(2)}) copy-start(bf16[1024,1024]{1,0:T(8,128)(2,1)} %param.9) | copy-start | bytes 6291460
  172.3 230.2 %copy-start.3 = (bf16[1024,256]{1,0:T(8,128)(2,1)S(1)}, bf16[1024,256]{1,0:T(8,128)(2,1)}, u32[]{:S(2)}) copy-start(bf16[1024,256]{1,0:T(8,128)(2,1)} %param.11) | copy-start | bytes 1572868
Sparse Core Ops, SparseCore 0:
  122.2 133.5 reduce-scatter.8
  258.2 136.9 reduce-scatter.6
where the time goes:
time: 413 us; the launch traced here: 410 us
  waiting for transfers between devices  217 us (53%)
  matrix products  91.2 us (22%)
  blocking collectives  47.9 us (12%)
  other arithmetic  28.7 us (7%)
  between operations  14 us (3%)
  local copies, waits for them, and re-layouts  11.6 us (3%)
    unnamed x4, waiting for transfers between devices  217 us
    pmax x1, blocking collectives, per_device(): lax.pmax(peaks.astype(jnp.bfloat16), ('tm', 'patch')).astype(peaks.dtype)  42.2 us
    dot_general x8, matrix products, block_part(): jnp.dot(weight, vals[:, cols], preferred_element_type=jnp.float32)  37.2 us
    dot_general x8, matrix products, block_part(): jnp.dot(query[:, cols], keys[:, cols].T, preferred_element_type=jnp.float32)  35.8 us
    reduce_sum x8, other arithmetic, block_part(): totals.append(jnp.sum(weight.astype(jnp.float32), axis=1))  23.3 us
    unnamed x56, local copies, waits for them, and re-layouts  11.4 us
  transfers between devices with their start and end apart: 2, of which 2 were waited for; matrix products, arithmetic and copies ran while one was open for 14% of the time, Pallas kernels for 0%

commit v1 on v0

v1 whole, which is shorter than its diff:
```python
import functools
import math

import jax
import jax.numpy as jnp
from jax import lax
from jax.experimental import pallas as pl
from jax.experimental.pallas import tpu as pltpu
from jax.sharding import PartitionSpec as P

H = 8
CORES = 2
AXES = ("tm", "patch")
VMEM = pl.BlockSpec(memory_space=pltpu.VMEM)
SMEM = pl.BlockSpec(memory_space=pltpu.SMEM)
PARAMS = pltpu.CompilerParams(vmem_limit_bytes=48 * 2**20)
EXTRA = 8


def xor_permute(value, n, step):
    return lax.ppermute(value, AXES, [(i, i ^ step) for i in range(n)])


def project_kernel(a_ref, w_ref, o_ref):
    o_ref[...] = jnp.dot(a_ref[...], w_ref[...], preferred_element_type=jnp.float32).astype(o_ref.dtype)


def project_t_kernel(a_ref, w_ref, o_ref):
    o_ref[...] = jnp.dot(a_ref[...], w_ref[...], preferred_element_type=jnp.float32).astype(o_ref.dtype).T


def project(a, w, transposed, rows=256):
    n, d = a.shape
    cols = w.shape[1]
    if transposed:
        kernel, out, spec = project_t_kernel, (cols, n), pl.BlockSpec((cols, rows), lambda i: (0, i))
    else:
        kernel, out, spec = project_kernel, (n, cols), pl.BlockSpec((rows, cols), lambda i: (i, 0))
    return pl.pallas_call(
        kernel,
        grid=(n // rows,),
        out_shape=jax.ShapeDtypeStruct(out, jnp.bfloat16),
        in_specs=[pl.BlockSpec((rows, d), lambda i: (i, 0)), pl.BlockSpec((d, cols), lambda i: (0, 0))],
        out_specs=spec,
        compiler_params=PARAMS,
        cost_estimate=pl.CostEstimate(flops=2 * n * d * cols, bytes_accessed=2 * (n * d + d * cols + n * cols), transcendentals=0),
    )(a, w)


def attend_kernel(tile, chunk, head_ref, q_ref, k_ref, v_ref, o_ref, s0, s1):
    size, latents = q_ref.shape
    tokens = k_ref.shape[0]
    n_x, n_tm, rows, block = o_ref.shape
    feats = rows - EXTRA
    coef = math.log2(math.e) / math.sqrt(size)
    slots = (s0, s1)
    ones = jnp.ones((16, chunk), jnp.bfloat16)
    row = lax.broadcasted_iota(jnp.int32, (EXTRA, tile), 0)
    peak = None
    for j in range(latents // tile + 1):
        scores, weights = j < latents // tile, j > 0
        now, before = slots[j % 2], slots[(j - 1) % 2]
        acc, top = jnp.zeros((size + 16, tile), jnp.float32), None
        for c in range(tokens // chunk):
            part = slice(c * chunk, (c + 1) * chunk)
            if scores:
                s = jnp.dot(k_ref[part, :], q_ref[:, j * tile : (j + 1) * tile], preferred_element_type=jnp.float32)
                now[part, :] = s
                high = jnp.max(s.reshape(chunk // 8, 8, tile), axis=0)
                top = high if top is None else jnp.maximum(top, high)
            if weights:
                w = jnp.exp2((before[part, :] - peak) * coef).astype(jnp.bfloat16)
                v = jnp.concatenate([v_ref[:, part], ones], axis=0)
                acc = acc + jnp.dot(v, w, preferred_element_type=jnp.float32)
        if weights:
            tail = jnp.where(row == 1, peak * coef, acc[size : size + EXTRA])
            for b in range(tile // block):
                lanes = slice(b * block, (b + 1) * block)
                tm = (j - 1) * (tile // block) + b
                for x in range(n_x):
                    o_ref[x, tm, :feats] = acc[x * feats : (x + 1) * feats, lanes]
                    o_ref[x, tm, feats:] = tail[:, lanes]
        if scores:
            peak = jnp.max(top, axis=0, keepdims=True)


def attend(head, query_t, keys, vals_t, n_x, n_tm, tile=512, chunk=1024):
    size, latents, tokens = query_t.shape[0] // H, query_t.shape[1], keys.shape[0]
    shape = (n_x, n_tm, size // n_x + EXTRA, latents // n_tm)
    return pl.pallas_call(
        functools.partial(attend_kernel, tile, chunk),
        grid_spec=pltpu.PrefetchScalarGridSpec(
            num_scalar_prefetch=1,
            grid=(1,),
            in_specs=[
                pl.BlockSpec((size, latents), lambda i, h: (h[0], 0)),
                pl.BlockSpec((tokens, size), lambda i, h: (0, h[0])),
                pl.BlockSpec((size, tokens), lambda i, h: (h[0], 0)),
            ],
            out_specs=pl.BlockSpec(shape, lambda i, h: (0, 0, 0, 0)),
            scratch_shapes=[pltpu.VMEM((tokens, tile), jnp.float32)] * 2,
        ),
        out_shape=jax.ShapeDtypeStruct(shape, jnp.float32),
        compiler_params=PARAMS,
        cost_estimate=pl.CostEstimate(
            flops=4 * tokens * latents * size, bytes_accessed=4 * math.prod(shape), transcendentals=tokens * latents
        ),
    )(head, query_t, keys, vals_t)


def merge(parts):
    feats = parts[0].shape[-2] - EXTRA
    peaks = [p[..., feats + 1 : feats + 2, :] for p in parts]
    peak = functools.reduce(jnp.maximum, peaks)
    total = sum(p * jnp.exp2(m - peak) for p, m in zip(parts, peaks))
    row = lax.broadcasted_iota(jnp.int32, total.shape, total.ndim - 2)
    return jnp.where(row == feats + 1, peak, total)


def merge_core_kernel(at_ref, own_ref, got_ref, *out_refs):
    x = at_ref[0]
    n_tm = own_ref.shape[1]
    for s, out in enumerate(out_refs):
        for t in range(n_tm):
            out[t] = merge([own_ref[x ^ s, t], got_ref[x ^ s, t]])


def merge_core(at, own, got):
    n_x = own.shape[0]
    return pl.pallas_call(
        merge_core_kernel,
        out_shape=[jax.ShapeDtypeStruct(own.shape[1:], jnp.float32)] * n_x,
        in_specs=[SMEM, VMEM, VMEM],
        out_specs=[VMEM] * n_x,
        compiler_params=PARAMS,
        cost_estimate=pl.CostEstimate(flops=own.size * 4, bytes_accessed=own.size * 12, transcendentals=0),
    )(at, own, got)


def merge_x_kernel(at_ref, *refs):
    n_tm = refs[0].shape[0]
    parts, outs = refs[:-n_tm], refs[-n_tm:]
    tm = at_ref[1]
    for s, out in enumerate(outs):
        out[...] = merge([p[tm ^ s] for p in parts])


def merge_x(at, parts):
    n_tm = parts[0].shape[0]
    return pl.pallas_call(
        merge_x_kernel,
        out_shape=[jax.ShapeDtypeStruct(parts[0].shape[1:], jnp.float32)] * n_tm,
        in_specs=[SMEM] + [VMEM] * len(parts),
        out_specs=[VMEM] * n_tm,
        compiler_params=PARAMS,
        cost_estimate=pl.CostEstimate(flops=parts[0].size * 8, bytes_accessed=parts[0].size * 12, transcendentals=0),
    )(at, *parts)


def attended_kernel(*refs):
    merged = merge([r[...] for r in refs[:-1]])
    feats = merged.shape[0] - EXTRA
    refs[-1][...] = merged[:feats] / merged[feats : feats + 1]


def attended(parts):
    rows, block = parts[0].shape
    return pl.pallas_call(
        attended_kernel,
        out_shape=jax.ShapeDtypeStruct((rows - EXTRA, block), jnp.float32),
        in_specs=[VMEM] * len(parts),
        out_specs=VMEM,
        compiler_params=PARAMS,
        cost_estimate=pl.CostEstimate(flops=rows * block * 32, bytes_accessed=rows * block * 36, transcendentals=0),
    )(*parts)


def finish_kernel(n_patch, at_ref, *refs):
    pieces, (w_ref, o_ref, normed) = refs[:-3], refs[-3:]
    feats = pieces[0].shape[0]
    width = feats * len(pieces)
    me = at_ref[2]
    squares = functools.reduce(lambda a, b: a + b, [jnp.square(p[...]) for p in pieces])
    scale = lax.rsqrt(jnp.sum(squares, axis=0, keepdims=True) * (1.0 / width) + 1e-06)
    for i, piece in enumerate(pieces):
        pair, owner = i // n_patch, me ^ (i % n_patch)
        head = CORES * pair + owner % CORES
        at = pl.multiple_of(head * (width // H) + owner // CORES * feats, feats)
        normed[pl.ds(at, feats), :] = (piece[...] * scale).astype(jnp.bfloat16)
    o_ref[...] = lax.dot_general(
        normed[...], w_ref[...], (((0,), (0,)), ((), ())), preferred_element_type=jnp.float32
    ).astype(jnp.bfloat16)


def finish(at, pieces, w_out, n_patch):
    block = pieces[0].shape[1]
    return pl.pallas_call(
        functools.partial(finish_kernel, n_patch),
        out_shape=jax.ShapeDtypeStruct((block, w_out.shape[1]), jnp.bfloat16),
        in_specs=[SMEM] + [VMEM] * (len(pieces) + 1),
        out_specs=VMEM,
        scratch_shapes=[pltpu.VMEM((w_out.shape[0], block), jnp.bfloat16)],
        compiler_params=PARAMS,
        cost_estimate=pl.CostEstimate(flops=2 * block * w_out.size, bytes_accessed=2 * w_out.size, transcendentals=0),
    )(at, *pieces, w_out)


def per_device(n_tm, n_patch, latents, tokens, w_query, w_key, w_value, w_out):
    n, n_x = n_tm * n_patch, n_patch // CORES
    tm, patch = lax.axis_index("tm"), lax.axis_index("patch")
    x, core = patch // CORES, patch % CORES
    at = jnp.stack([x, tm, patch]).astype(jnp.int32)

    query_t = project(latents, w_query, True)
    keys = project(tokens, w_key, False)
    vals_t = project(tokens, w_value, True)

    pieces = []
    for pair in range(H // CORES):
        other, own = (
            attend((CORES * pair + c).astype(jnp.int32).reshape(1), query_t, keys, vals_t, n_x, n_tm)
            for c in (1 - core, core)
        )
        kept, *sent = merge_core(at, own, xor_permute(other, n, 1))
        got = [xor_permute(v, n, CORES * (s + 1)) for s, v in enumerate(sent)]
        kept, *sent = merge_x(at, [kept, *got])
        got = [xor_permute(v, n, n_patch * (s + 1)) for s, v in enumerate(sent)]
        piece = attended([kept, *got])
        pieces += [piece] + [xor_permute(piece, n, s) for s in range(1, n_patch)]
    return finish(at, pieces, w_out, n_patch)


def solution(mesh):
    return jax.shard_map(
        functools.partial(per_device, mesh.shape["tm"], mesh.shape["patch"]),
        mesh=mesh,
        in_specs=(P(), P(("tm", "patch"), None), P(), P(), P(), P(None, "patch")),
        out_specs=P("tm", "patch"),
        check_vma=False,
    )
```

time: 413 us -> 148 us (0.36)
  waiting for transfers between devices: 217 us -> 13.1 us
  matrix products: 91.2 us -> 0 us
  Pallas kernels: 0 us -> 67.4 us
  starting transfers between devices: 0.26 us -> 63.5 us
  blocking collectives: 47.9 us -> 0 us
  other arithmetic: 28.7 us -> 0.08 us
  between operations: 14 us -> 0.25 us
  local copies, waits for them, and re-layouts: 11.6 us -> 3.19 us
    unnamed x4 -> x0, waiting for transfers between devices: 217 us -> none
    dot_general x20 -> x0, matrix products: 91.2 us -> none  [the longest x8 37.2 us: block_part(): jnp.dot(weight, vals[:, cols], preferred_element_type=jnp.float32)]
    pallas_call x0 -> x24, Pallas kernels: none -> 67.4 us  [the longest x8 34.5 us: attend(): pl.pallas_call(functools.partial(attend_kernel, tile, chunk), grid_spec=p...]
    ppermute x0 -> x48, starting transfers between devices: none -> 63.5 us  [xor_permute(): return lax.ppermute(value, AXES, [(i, i ^ step) for i in range(n)])]
    pmax x1 -> x0, blocking collectives: 42.2 us -> none  [per_device(): lax.pmax(peaks.astype(jnp.bfloat16), ('tm', 'patch')).astype(peaks.dtype)]
    reduce_sum x9 -> x0, other arithmetic: 23.4 us -> none  [the longest x8 23.3 us: block_part(): totals.append(jnp.sum(weight.astype(jnp.float32), axis=1))]
    ppermute x0 -> x48, waiting for transfers between devices: none -> 13.1 us  [xor_permute(): return lax.ppermute(value, AXES, [(i, i ^ step) for i in range(n)])]
    unnamed x56 -> x8, local copies, waits for them, and re-layouts: 11.4 us -> 3.19 us
  transfers between devices with their start and end apart: 2 -> 48, of which waited for: 2 -> 11; matrix products, arithmetic and copies ran while one was open for 14% -> 0% of each run, Pallas kernels for 0% -> 25%
where the time goes in v1:
time: 148 us; the launch traced here: 147 us
  Pallas kernels  67.4 us (46%)
  starting transfers between devices  63.5 us (43%)
  waiting for transfers between devices  13.1 us (9%)
  local copies, waits for them, and re-layouts  3.19 us (2%)
    ppermute x48, starting transfers between devices, xor_permute(): return lax.ppermute(value, AXES, [(i, i ^ step) for i in range(n)])  63.5 us
    pallas_call x8, Pallas kernels, attend(): pl.pallas_call(functools.partial(attend_kernel, tile, chunk), grid_spec=p...  34.5 us
    pallas_call x3, Pallas kernels, project(): pl.pallas_call(kernel, grid=(n // rows,), out_shape=jax.ShapeDtypeStruct(...  24 us
    ppermute x48, waiting for transfers between devices, xor_permute(): return lax.ppermute(value, AXES, [(i, i ^ step) for i in range(n)])  13.1 us
    pallas_call x4, Pallas kernels, merge_core(): pl.pallas_call(merge_core_kernel, out_shape=[jax.ShapeDtypeStruct(own.sha...  4.71 us
    unnamed x8, local copies, waits for them, and re-layouts  3.19 us
  transfers between devices with their start and end apart: 48, of which 11 were waited for; matrix products, arithmetic and copies ran while one was open for 0% of the time, Pallas kernels for 25%

profile of v1, /device:TPU:0, one launch (start us, length us, event | category | flops | bytes accessed | tf_op | source)
XLA Modules:
  0.0 147.5 jit_solution(5759445745861576964)
XLA Ops:
  0.0 1.6 %copy-done.1 = bf16[1024,1024]{1,0:T(8,128)(2,1)S(1)} copy-done((bf16[1024,1024]{1,0:T(8,128)(2,1)S(1)}, bf16[1024,1024]{1,0:T(8,128)(2,1)}, u32[]{:S(2)}) %copy-start.1) | copy-done | bytes 2097176
  1.6 9.4 %shard_map.65.k_ref = bf16[2048,1024]{1,0:T(8,128)(2,1)} custom-call(bf16[2048,1024]{1,0:T(8,128)(2,1)} %a_ref.5, bf16[1024,1024]{1,0:T(8,128)(2,1)S(1)} %copy-done.1), custom_call_target="tpu_custom_call" | custom-call | flops 4294967296 | bytes 10485760 | tf_op jit(solution)/shard_map/pallas_call | solution.py:39
  11.0 9.7 %shard_map.66.v_ref = bf16[1024,2048]{1,0:T(8,128)(2,1)} custom-call(bf16[2048,1024]{1,0:T(8,128)(2,1)} %a_ref.5, bf16[1024,1024]{1,0:T(8,128)(2,1)S(1)} %copy-done.2), custom_call_target="tpu_custom_call" | custom-call | flops 4294967296 | bytes 10485760 | tf_op jit(solution)/shard_map/pallas_call | solution.py:39
  20.7 1.6 %copy-done.3 = bf16[1024,1024]{1,0:T(8,128)(2,1)S(1)} copy-done((bf16[1024,1024]{1,0:T(8,128)(2,1)S(1)}, bf16[1024,1024]{1,0:T(8,128)(2,1)}, u32[]{:S(2)}) %copy-start.3) | copy-done | bytes 2097176
  22.3 5.0 %shard_map.64.q_ref = bf16[1024,1024]{1,0:T(8,128)(2,1)S(1)} custom-call(bf16[1024,1024]{1,0:T(8,128)(2,1)S(1)} %copy-done.3, bf16[1024,1024]{1,0:T(8,128)(2,1)} %w_ref.3), custom_call_target="tpu_custom_call" | custom-call | flops 2147483648 | bytes 6291456 | tf_op jit(solution)/shard_map/pallas_call | solution.py:39
  27.2 4.9 %shard_map.83 = f32[2,8,72,128]{3,2,1,0:T(8,128)} custom-call(s32[1]{0:T(128)} %bitcast.10.head_ref, bf16[1024,1024]{1,0:T(8,128)(2,1)S(1)} %shard_map.64.q_ref, bf16[2048,1024]{1,0:T(8,128)(2,1)} %shard_map.65.k_ref, bf16[1024,2048]{1,0:T(8,128)(2,1)} %shard_map.66.v_ref), custom_call_target="tpu_custom_call" | custom-call | flops 1073741824 | bytes 589824 | tf_op jit(solution)/shard_map/pallas_call | solution.py:90
  32.1 0.5 collective-permute-start.36
  32.6 4.9 %shard_map.78 = f32[2,8,72,128]{3,2,1,0:T(8,128)} custom-call(s32[1]{0:T(128)} %bitcast.8.head_ref, bf16[1024,1024]{1,0:T(8,128)(2,1)S(1)} %shard_map.64.q_ref, bf16[2048,1024]{1,0:T(8,128)(2,1)} %shard_map.65.k_ref, bf16[1024,2048]{1,0:T(8,128)(2,1)} %shard_map.66.v_ref), custom_call_target="tpu_custom_call" | custom-call | flops 1073741824 | bytes 589824 | tf_op jit(solution)/shard_map/pallas_call | solution.py:90
  37.6 4.1 %shard_map.73 = f32[2,8,72,128]{3,2,1,0:T(8,128)S(1)} custom-call(s32[1]{0:T(128)} %bitcast.6.head_ref, bf16[1024,1024]{1,0:T(8,128)(2,1)S(1)} %shard_map.64.q_ref, bf16[2048,1024]{1,0:T(8,128)(2,1)} %shard_map.65.k_ref, bf16[1024,2048]{1,0:T(8,128)(2,1)} %shard_map.66.v_ref), custom_call_target="tpu_custom_call" | custom-call | flops 1073741824 | bytes 589824 | tf_op jit(solution)/shard_map/pallas_call | solution.py:90
  41.6 0.5 collective-permute-start.12
  42.2 4.1 %shard_map.68 = f32[2,8,72,128]{3,2,1,0:T(8,128)S(1)} custom-call(s32[1]{0:T(128)} %bitcast.4.head_ref, bf16[1024,1024]{1,0:T(8,128)(2,1)S(1)} %shard_map.64.q_ref, bf16[2048,1024]{1,0:T(8,128)(2,1)} %shard_map.65.k_ref, bf16[1024,2048]{1,0:T(8,128)(2,1)} %shard_map.66.v_ref), custom_call_target="tpu_custom_call" | custom-call | flops 1073741824 | bytes 589824 | tf_op jit(solution)/shard_map/pallas_call | solution.py:90
  46.4 4.3 %shard_map.82.own_ref = f32[2,8,72,128]{3,2,1,0:T(8,128)S(1)} custom-call(s32[1]{0:T(128)} %bitcast.9.head_ref, bf16[1024,1024]{1,0:T(8,128)(2,1)S(1)} %shard_map.64.q_ref, bf16[2048,1024]{1,0:T(8,128)(2,1)} %shard_map.65.k_ref, bf16[1024,2048]{1,0:T(8,128)(2,1)} %shard_map.66.v_ref), custom_call_target="tpu_custom_call" | custom-call | flops 1073741824 | bytes 589824 | tf_op jit(solution)/shard_map/pallas_call | solution.py:90
  50.6 4.1 %shard_map.77.own_ref = f32[2,8,72,128]{3,2,1,0:T(8,128)S(1)} custom-call(s32[1]{0:T(128)} %bitcast.7.head_ref, bf16[1024,1024]{1,0:T(8,128)(2,1)S(1)} %shard_map.64.q_ref, bf16[2048,1024]{1,0:T(8,128)(2,1)} %shard_map.65.k_ref, bf16[1024,2048]{1,0:T(8,128)(2,1)} %shard_map.66.v_ref), custom_call_target="tpu_custom_call" | custom-call | flops 1073741824 | bytes 589824 | tf_op jit(solution)/shard_map/pallas_call | solution.py:90
  54.7 4.1 %shard_map.72.own_ref = f32[2,8,72,128]{3,2,1,0:T(8,128)S(1)} custom-call(s32[1]{0:T(128)} %bitcast.5.head_ref, bf16[1024,1024]{1,0:T(8,128)(2,1)S(1)} %shard_map.64.q_ref, bf16[2048,1024]{1,0:T(8,128)(2,1)} %shard_map.65.k_ref, bf16[1024,2048]{1,0:T(8,128)(2,1)} %shard_map.66.v_ref), custom_call_target="tpu_custom_call" | custom-call | flops 1073741824 | bytes 589824 | tf_op jit(solution)/shard_map/pallas_call | solution.py:90
  58.9 1.2 shard_map.84
  60.1 3.0 %collective-permute-start.37 = (f32[8,72,128]{2,1,0:T(8,128)S(1)}, f32[8,72,128]{2,1,0:T(8,128)S(1)}, u32[]{:S(2)}, u32[]{:S(2)}) collective-permute-start(f32[8,72,128]{2,1,0:T(8,128)S(1)} %get-tuple-element.76), channel_id=1, source_target_pairs={{0,2},{1,3},{2,0},{3,1},{4,6},{5,7},{6,4},{7,5},{8,10},{9,11},{10,... | collective-permute-start | bytes 884744 | tf_op jit(solution)/shard_map/ppermute | solution.py:21
  63.1 1.2 shard_map.79
  64.4 4.1 %shard_map.67.own_ref = f32[2,8,72,128]{3,2,1,0:T(8,128)S(1)} custom-call(s32[1]{0:T(128)} %bitcast.3.head_ref, bf16[1024,1024]{1,0:T(8,128)(2,1)S(1)} %shard_map.64.q_ref, bf16[2048,1024]{1,0:T(8,128)(2,1)} %shard_map.65.k_ref, bf16[1024,2048]{1,0:T(8,128)(2,1)} %shard_map.66.v_ref), custom_call_target="tpu_custom_call" | custom-call | flops 1073741824 | bytes 589824 | tf_op jit(solution)/shard_map/pallas_call | solution.py:90
  68.5 1.2 shard_map.74
  69.7 2.1 %collective-permute-start.13 = (f32[8,72,128]{2,1,0:T(8,128)S(1)}, f32[8,72,128]{2,1,0:T(8,128)S(1)}, u32[]{:S(2)}, u32[]{:S(2)}) collective-permute-start(f32[8,72,128]{2,1,0:T(8,128)S(1)} %get-tuple-element.56), channel_id=1, source_target_pairs={{0,2},{1,3},{2,0},{3,1},{4,6},{5,7},{6,4},{7,5},{8,10},{9,11},{10,... | collective-permute-start | bytes 884744 | tf_op jit(solution)/shard_map/ppermute | solution.py:21
  71.7 1.2 shard_map.69
  73.0 0.6 shard_map.85
  73.6 2.1 %collective-permute-start.38 = (f32[72,128]{1,0:T(8,128)S(1)}, f32[72,128]{1,0:T(8,128)S(1)}, u32[]{:S(2)}, u32[]{:S(2)}) collective-permute-start(f32[72,128]{1,0:T(8,128)S(1)} %get-tuple-element.78), channel_id=1, source_target_pairs={{0,4},{1,5},{2,6},{3,7},{4,0},{5,1},{6,2},{7,3},{8,12},{9,13},{10,... | collective-permute-start | bytes 110600 | tf_op jit(solution)/shard_map/ppermute | solution.py:21
  75.7 1.6 %collective-permute-start.39 = (f32[72,128]{1,0:T(8,128)S(1)}, f32[72,128]{1,0:T(8,128)S(1)}, u32[]{:S(2)}, u32[]{:S(2)}) collective-permute-start(f32[72,128]{1,0:T(8,128)S(1)} %get-tuple-element.79), channel_id=1, source_target_pairs={{0,8},{1,9},{2,10},{3,11},{4,12},{5,13},{6,14},{7,15},{8,0},{9,1},... | collective-permute-start | bytes 110600 | tf_op jit(solution)/shard_map/ppermute | solution.py:21
  77.3 3.0 %collective-permute-start.40 = (f32[72,128]{1,0:T(8,128)S(1)}, f32[72,128]{1,0:T(8,128)S(1)}, u32[]{:S(2)}, u32[]{:S(2)}) collective-permute-start(f32[72,128]{1,0:T(8,128)S(1)} %get-tuple-element.80), channel_id=1, source_target_pairs={{0,12},{1,13},{2,14},{3,15},{4,8},{5,9},{6,10},{7,11},{8,4},{9,5},... | collective-permute-start | bytes 110600 | tf_op jit(solution)/shard_map/ppermute | solution.py:21
  80.3 3.2 %collective-permute-done.13.refs_1_ = f32[8,72,128]{2,1,0:T(8,128)S(1)} collective-permute-done((f32[8,72,128]{2,1,0:T(8,128)S(1)}, f32[8,72,128]{2,1,0:T(8,128)S(1)}, u32[]{:S(2)}, u32[]{:S(2)}) %collective-permute-start.13) | collective-permute-done | bytes 294944 | tf_op jit(solution)/shard_map/ppermute | solution.py:21
  83.5 3.2 %collective-permute-start.41 = (f32[72,128]{1,0:T(8,128)S(1)}, f32[72,128]{1,0:T(8,128)S(1)}, u32[]{:S(2)}, u32[]{:S(2)}) collective-permute-start(f32[72,128]{1,0:T(8,128)S(1)} %get-tuple-element.81), channel_id=1, source_target_pairs={{0,16},{1,17},{2,18},{3,19},{4,20},{5,21},{6,22},{7,23},{8,24},{9,... | collective-permute-start | bytes 110600 | tf_op jit(solution)/shard_map/ppermute | solution.py:21
  86.7 2.5 %collective-permute-done.1.refs_1_ = f32[8,72,128]{2,1,0:T(8,128)S(1)} collective-permute-done((f32[8,72,128]{2,1,0:T(8,128)S(1)}, f32[8,72,128]{2,1,0:T(8,128)S(1)}, u32[]{:S(2)}, u32[]{:S(2)}) %collective-permute-start.1) | collective-permute-done | bytes 294944 | tf_op jit(solution)/shard_map/ppermute | solution.py:21
  89.3 3.8 %collective-permute-start.42 = (f32[72,128]{1,0:T(8,128)S(1)}, f32[72,128]{1,0:T(8,128)S(1)}, u32[]{:S(2)}, u32[]{:S(2)}) collective-permute-start(f32[72,128]{1,0:T(8,128)S(1)} %get-tuple-element.82), channel_id=1, source_target_pairs={{0,20},{1,21},{2,22},{3,23},{4,16},{5,17},{6,18},{7,19},{8,28},{9,... | collective-permute-start | bytes 110600 | tf_op jit(solution)/shard_map/ppermute | solution.py:21
  93.1 0.6 shard_map.80
  93.7 1.4 collective-permute-start.43
  95.1 2.4 %collective-permute-start.44 = (f32[72,128]{1,0:T(8,128)S(1)}, f32[72,128]{1,0:T(8,128)S(1)}, u32[]{:S(2)}, u32[]{:S(2)}) collective-permute-start(f32[72,128]{1,0:T(8,128)S(1)} %get-tuple-element.84), channel_id=1, source_target_pairs={{0,28},{1,29},{2,30},{3,31},{4,24},{5,25},{6,26},{7,27},{8,20},{9,... | collective-permute-start | bytes 110600 | tf_op jit(solution)/shard_map/ppermute | solution.py:21
  97.5 1.5 %collective-permute-start.26 = (f32[72,128]{1,0:T(8,128)S(1)}, f32[72,128]{1,0:T(8,128)S(1)}, u32[]{:S(2)}, u32[]{:S(2)}) collective-permute-start(f32[72,128]{1,0:T(8,128)S(1)} %get-tuple-element.68), channel_id=1, source_target_pairs={{0,4},{1,5},{2,6},{3,7},{4,0},{5,1},{6,2},{7,3},{8,12},{9,13},{10,... | collective-permute-start | bytes 110600 | tf_op jit(solution)/shard_map/ppermute | solution.py:21
  99.0 2.0 %collective-permute-start.28 = (f32[72,128]{1,0:T(8,128)S(1)}, f32[72,128]{1,0:T(8,128)S(1)}, u32[]{:S(2)}, u32[]{:S(2)}) collective-permute-start(f32[72,128]{1,0:T(8,128)S(1)} %get-tuple-element.70), channel_id=1, source_target_pairs={{0,12},{1,13},{2,14},{3,15},{4,8},{5,9},{6,10},{7,11},{8,4},{9,5},... | collective-permute-start | bytes 110600 | tf_op jit(solution)/shard_map/ppermute | solution.py:21
  101.0 0.4 collective-permute-start.29
  101.4 0.5 collective-permute-done.44.refs_7_
  101.9 3.0 %collective-permute-start.30 = (f32[72,128]{1,0:T(8,128)S(1)}, f32[72,128]{1,0:T(8,128)S(1)}, u32[]{:S(2)}, u32[]{:S(2)}) collective-permute-start(f32[72,128]{1,0:T(8,128)S(1)} %get-tuple-element.72), channel_id=1, source_target_pairs={{0,20},{1,21},{2,22},{3,23},{4,16},{5,17},{6,18},{7,19},{8,28},{9,... | collective-permute-start | bytes 110600 | tf_op jit(solution)/shard_map/ppermute | solution.py:21
  104.9 1.3 collective-permute-start.31
  106.3 0.6 shard_map.75
  106.9 2.5 %collective-permute-start.32 = (f32[72,128]{1,0:T(8,128)S(1)}, f32[72,128]{1,0:T(8,128)S(1)}, u32[]{:S(2)}, u32[]{:S(2)}) collective-permute-start(f32[72,128]{1,0:T(8,128)S(1)} %get-tuple-element.74), channel_id=1, source_target_pairs={{0,28},{1,29},{2,30},{3,31},{4,24},{5,25},{6,26},{7,27},{8,20},{9,... | collective-permute-start | bytes 110600 | tf_op jit(solution)/shard_map/ppermute | solution.py:21
  109.4 1.5 %collective-permute-start.14 = (f32[72,128]{1,0:T(8,128)S(1)}, f32[72,128]{1,0:T(8,128)S(1)}, u32[]{:S(2)}, u32[]{:S(2)}) collective-permute-start(f32[72,128]{1,0:T(8,128)S(1)} %get-tuple-element.58), channel_id=1, source_target_pairs={{0,4},{1,5},{2,6},{3,7},{4,0},{5,1},{6,2},{7,3},{8,12},{9,13},{10,... | collective-permute-start | bytes 110600 | tf_op jit(solution)/shard_map/ppermute | solution.py:21
  110.9 2.0 %collective-permute-start.16 = (f32[72,128]{1,0:T(8,128)S(1)}, f32[72,128]{1,0:T(8,128)S(1)}, u32[]{:S(2)}, u32[]{:S(2)}) collective-permute-start(f32[72,128]{1,0:T(8,128)S(1)} %get-tuple-element.60), channel_id=1, source_target_pairs={{0,12},{1,13},{2,14},{3,15},{4,8},{5,9},{6,10},{7,11},{8,4},{9,5},... | collective-permute-start | bytes 110600 | tf_op jit(solution)/shard_map/ppermute | solution.py:21
  112.9 0.8 collective-permute-done.32.refs_7_
  113.7 3.0 %collective-permute-start.18 = (f32[72,128]{1,0:T(8,128)S(1)}, f32[72,128]{1,0:T(8,128)S(1)}, u32[]{:S(2)}, u32[]{:S(2)}) collective-permute-start(f32[72,128]{1,0:T(8,128)S(1)} %get-tuple-element.62), channel_id=1, source_target_pairs={{0,20},{1,21},{2,22},{3,23},{4,16},{5,17},{6,18},{7,19},{8,28},{9,... | collective-permute-start | bytes 110600 | tf_op jit(solution)/shard_map/ppermute | solution.py:21
  116.7 1.3 collective-permute-start.19
  118.1 0.6 shard_map.70
  118.7 2.5 %collective-permute-start.20 = (f32[72,128]{1,0:T(8,128)S(1)}, f32[72,128]{1,0:T(8,128)S(1)}, u32[]{:S(2)}, u32[]{:S(2)}) collective-permute-start(f32[72,128]{1,0:T(8,128)S(1)} %get-tuple-element.64), channel_id=1, source_target_pairs={{0,28},{1,29},{2,30},{3,31},{4,24},{5,25},{6,26},{7,27},{8,20},{9,... | collective-permute-start | bytes 110600 | tf_op jit(solution)/shard_map/ppermute | solution.py:21
  121.2 1.5 %collective-permute-start.2 = (f32[72,128]{1,0:T(8,128)S(1)}, f32[72,128]{1,0:T(8,128)S(1)}, u32[]{:S(2)}, u32[]{:S(2)}) collective-permute-start(f32[72,128]{1,0:T(8,128)S(1)} %get-tuple-element.48), channel_id=1, source_target_pairs={{0,4},{1,5},{2,6},{3,7},{4,0},{5,1},{6,2},{7,3},{8,12},{9,13},{10,... | collective-permute-start | bytes 110600 | tf_op jit(solution)/shard_map/ppermute | solution.py:21
  122.7 2.0 %collective-permute-start.4 = (f32[72,128]{1,0:T(8,128)S(1)}, f32[72,128]{1,0:T(8,128)S(1)}, u32[]{:S(2)}, u32[]{:S(2)}) collective-permute-start(f32[72,128]{1,0:T(8,128)S(1)} %get-tuple-element.50), channel_id=1, source_target_pairs={{0,12},{1,13},{2,14},{3,15},{4,8},{5,9},{6,10},{7,11},{8,4},{9,5},... | collective-permute-start | bytes 110600 | tf_op jit(solution)/shard_map/ppermute | solution.py:21
  124.7 0.8 collective-permute-done.20.refs_7_
  125.5 3.0 %collective-permute-start.6 = (f32[72,128]{1,0:T(8,128)S(1)}, f32[72,128]{1,0:T(8,128)S(1)}, u32[]{:S(2)}, u32[]{:S(2)}) collective-permute-start(f32[72,128]{1,0:T(8,128)S(1)} %get-tuple-element.52), channel_id=1, source_target_pairs={{0,20},{1,21},{2,22},{3,23},{4,16},{5,17},{6,18},{7,19},{8,28},{9,... | collective-permute-start | bytes 110600 | tf_op jit(solution)/shard_map/ppermute | solution.py:21
  128.6 1.3 collective-permute-start.7
  129.9 2.4 %collective-permute-start.8 = (f32[72,128]{1,0:T(8,128)S(1)}, f32[72,128]{1,0:T(8,128)S(1)}, u32[]{:S(2)}, u32[]{:S(2)}) collective-permute-start(f32[72,128]{1,0:T(8,128)S(1)} %get-tuple-element.54), channel_id=1, source_target_pairs={{0,28},{1,29},{2,30},{3,31},{4,24},{5,25},{6,26},{7,27},{8,20},{9,... | collective-permute-start | bytes 110600 | tf_op jit(solution)/shard_map/ppermute | solution.py:21
  132.5 1.6 %collective-permute-start.46 = (f32[64,128]{1,0:T(8,128)S(1)}, f32[64,128]{1,0:T(8,128)S(1)}, u32[]{:S(2)}, u32[]{:S(2)}) collective-permute-start(f32[64,128]{1,0:T(8,128)S(1)} %shard_map.86.refs_12_), channel_id=1, source_target_pairs={{0,2},{1,3},{2,0},{3,1},{4,6},{5,7},{6,4},{7,5},{8,10},{9,11},{10,... | collective-permute-start | bytes 98312 | tf_op jit(solution)/shard_map/ppermute | solution.py:21
  134.2 0.4 collective-permute-start.47
  134.9 1.7 %collective-permute-done.8.refs_7_ = f32[72,128]{1,0:T(8,128)S(1)} collective-permute-done((f32[72,128]{1,0:T(8,128)S(1)}, f32[72,128]{1,0:T(8,128)S(1)}, u32[]{:S(2)}, u32[]{:S(2)}) %collective-permute-start.8) | collective-permute-done | bytes 36896 | tf_op jit(solution)/shard_map/ppermute | solution.py:21
  136.6 1.5 %collective-permute-start.34 = (f32[64,128]{1,0:T(8,128)S(1)}, f32[64,128]{1,0:T(8,128)S(1)}, u32[]{:S(2)}, u32[]{:S(2)}) collective-permute-start(f32[64,128]{1,0:T(8,128)S(1)} %shard_map.81.refs_8_), channel_id=1, source_target_pairs={{0,2},{1,3},{2,0},{3,1},{4,6},{5,7},{6,4},{7,5},{8,10},{9,11},{10,... | collective-permute-start | bytes 98312 | tf_op jit(solution)/shard_map/ppermute | solution.py:21
  138.1 0.6 collective-permute-start.21
  138.8 1.6 %collective-permute-start.22 = (f32[64,128]{1,0:T(8,128)S(1)}, f32[64,128]{1,0:T(8,128)S(1)}, u32[]{:S(2)}, u32[]{:S(2)}) collective-permute-start(f32[64,128]{1,0:T(8,128)S(1)} %shard_map.76.refs_4_), channel_id=1, source_target_pairs={{0,2},{1,3},{2,0},{3,1},{4,6},{5,7},{6,4},{7,5},{8,10},{9,11},{10,... | collective-permute-start | bytes 98312 | tf_op jit(solution)/shard_map/ppermute | solution.py:21
  140.5 1.8 %collective-permute-start.10 = (f32[64,128]{1,0:T(8,128)S(1)}, f32[64,128]{1,0:T(8,128)S(1)}, u32[]{:S(2)}, u32[]{:S(2)}) collective-permute-start(f32[64,128]{1,0:T(8,128)S(1)} %shard_map.71.refs_0_), channel_id=1, source_target_pairs={{0,2},{1,3},{2,0},{3,1},{4,6},{5,7},{6,4},{7,5},{8,10},{9,11},{10,... | collective-permute-start | bytes 98312 | tf_op jit(solution)/shard_map/ppermute | solution.py:21
  142.8 1.2 collective-permute-done.23.refs_7_
  144.0 0.7 collective-permute-done.10.refs_2_
  144.7 1.3 collective-permute-done.11.refs_3_
  145.9 1.5 %shard_map.87 = bf16[128,256]{1,0:T(8,128)(2,1)} custom-call(s32[3]{0:T(128)S(1)} %pad_add_fusion.at_ref, f32[64,128]{1,0:T(8,128)S(1)} %shard_map.71.refs_0_, f32[64,128]{1,0:T(8,128)S(1)} %collective-permute-done.9.refs_1_, f32[64,128]{1,0:T(8,128)S(1)} %collective-permute-done.10.refs_2_, f32[64,128]{1,0:T(8,128)S(1)} %collective-permute-done.11.refs_3_, ...), custom_call_target="tpu_custom_call" | custom-call | flops 67108864 | bytes 524288 | tf_op jit(solution)/shard_map/pallas_call | solution.py:197
  (65 shorter events, 1.8 us)
Async XLA Ops:
  0.0 1.6 %copy-start.1 = (bf16[1024,1024]{1,0:T(8,128)(2,1)S(1)}, bf16[1024,1024]{1,0:T(8,128)(2,1)}, u32[]{:S(2)}) copy-start(bf16[1024,1024]{1,0:T(8,128)(2,1)} %w_ref.4) | copy-start | bytes 6291460
  1.6 9.4 %copy-start.2 = (bf16[1024,1024]{1,0:T(8,128)(2,1)S(1)}, bf16[1024,1024]{1,0:T(8,128)(2,1)}, u32[]{:S(2)}) copy-start(bf16[1024,1024]{1,0:T(8,128)(2,1)} %w_ref.5) | copy-start | bytes 6291460
  20.7 1.6 %copy-start.3 = (bf16[1024,1024]{1,0:T(8,128)(2,1)S(1)}, bf16[1024,1024]{1,0:T(8,128)(2,1)}, u32[]{:S(2)}) copy-start(bf16[1024,1024]{1,0:T(8,128)(2,1)} %a_ref.3) | copy-start | bytes 6291460
  32.1 26.8 %collective-permute-start.36 = (f32[2,8,72,128]{3,2,1,0:T(8,128)}, f32[2,8,72,128]{3,2,1,0:T(8,128)}, u32[]{:S(2)}, u32[]{:S(2)}) collective-permute-start(f32[2,8,72,128]{3,2,1,0:T(8,128)} %shard_map.83), channel_id=1, source_target_pairs={{0,1},{1,0},{2,3},{3,2},{4,5},{5,4},{6,7},{7,6},{8,9},{9,8},{10,11... | collective-permute-start | bytes 1769480 | tf_op jit(solution)/shard_map/ppermute | solution.py:21
  37.5 25.6 %collective-permute-start.24 = (f32[2,8,72,128]{3,2,1,0:T(8,128)}, f32[2,8,72,128]{3,2,1,0:T(8,128)}, u32[]{:S(2)}, u32[]{:S(2)}) collective-permute-start(f32[2,8,72,128]{3,2,1,0:T(8,128)} %shard_map.78), channel_id=1, source_target_pairs={{0,1},{1,0},{2,3},{3,2},{4,5},{5,4},{6,7},{7,6},{8,9},{9,8},{10,11... | collective-permute-start | bytes 1769480 | tf_op jit(solution)/shard_map/ppermute | solution.py:21
  41.6 26.8 %collective-permute-start.12 = (f32[2,8,72,128]{3,2,1,0:T(8,128)S(1)}, f32[2,8,72,128]{3,2,1,0:T(8,128)}, u32[]{:S(2)}, u32[]{:S(2)}) collective-permute-start(f32[2,8,72,128]{3,2,1,0:T(8,128)S(1)} %shard_map.73), channel_id=1, source_target_pairs={{0,1},{1,0},{2,3},{3,2},{4,5},{5,4},{6,7},{7,6},{8,9},{9,8},{10,11... | collective-permute-start | bytes 1769480 | tf_op jit(solution)/shard_map/ppermute | solution.py:21
  46.2 25.5 %collective-permute-start = (f32[2,8,72,128]{3,2,1,0:T(8,128)S(1)}, f32[2,8,72,128]{3,2,1,0:T(8,128)}, u32[]{:S(2)}, u32[]{:S(2)}) collective-permute-start(f32[2,8,72,128]{3,2,1,0:T(8,128)S(1)} %shard_map.68), channel_id=1, source_target_pairs={{0,1},{1,0},{2,3},{3,2},{4,5},{5,4},{6,7},{7,6},{8,9},{9,8},{10,11... | collective-permute-start | bytes 1769480 | tf_op jit(solution)/shard_map/ppermute | solution.py:21
  60.1 12.9 %collective-permute-start.37 = (f32[8,72,128]{2,1,0:T(8,128)S(1)}, f32[8,72,128]{2,1,0:T(8,128)S(1)}, u32[]{:S(2)}, u32[]{:S(2)}) collective-permute-start(f32[8,72,128]{2,1,0:T(8,128)S(1)} %get-tuple-element.76), channel_id=1, source_target_pairs={{0,2},{1,3},{2,0},{3,1},{4,6},{5,7},{6,4},{7,5},{8,10},{9,11},{10,... | collective-permute-start | bytes 884744 | tf_op jit(solution)/shard_map/ppermute | solution.py:21
  64.3 13.0 %collective-permute-start.25 = (f32[8,72,128]{2,1,0:T(8,128)S(1)}, f32[8,72,128]{2,1,0:T(8,128)S(1)}, u32[]{:S(2)}, u32[]{:S(2)}) collective-permute-start(f32[8,72,128]{2,1,0:T(8,128)S(1)} %get-tuple-element.66), channel_id=1, source_target_pairs={{0,2},{1,3},{2,0},{3,1},{4,6},{5,7},{6,4},{7,5},{8,10},{9,11},{10,... | collective-permute-start | bytes 884744 | tf_op jit(solution)/shard_map/ppermute | solution.py:21
  69.7 13.9 %collective-permute-start.13 = (f32[8,72,128]{2,1,0:T(8,128)S(1)}, f32[8,72,128]{2,1,0:T(8,128)S(1)}, u32[]{:S(2)}, u32[]{:S(2)}) collective-permute-start(f32[8,72,128]{2,1,0:T(8,128)S(1)} %get-tuple-element.56), channel_id=1, source_target_pairs={{0,2},{1,3},{2,0},{3,1},{4,6},{5,7},{6,4},{7,5},{8,10},{9,11},{10,... | collective-permute-start | bytes 884744 | tf_op jit(solution)/shard_map/ppermute | solution.py:21
  72.9 73.0 %copy-start = (bf16[1024,256]{1,0:T(8,128)(2,1)S(1)}, bf16[1024,256]{1,0:T(8,128)(2,1)}, u32[]{:S(2)}) copy-start(bf16[1024,256]{1,0:T(8,128)(2,1)} %refs_16_.1) | copy-start | bytes 1572868
  72.9 16.3 %collective-permute-start.1 = (f32[8,72,128]{2,1,0:T(8,128)S(1)}, f32[8,72,128]{2,1,0:T(8,128)S(1)}, u32[]{:S(2)}, u32[]{:S(2)}) collective-permute-start(f32[8,72,128]{2,1,0:T(8,128)S(1)} %get-tuple-element.46), channel_id=1, source_target_pairs={{0,2},{1,3},{2,0},{3,1},{4,6},{5,7},{6,4},{7,5},{8,10},{9,11},{10,... | collective-permute-start | bytes 884744 | tf_op jit(solution)/shard_map/ppermute | solution.py:21
  73.6 20.0 %collective-permute-start.38 = (f32[72,128]{1,0:T(8,128)S(1)}, f32[72,128]{1,0:T(8,128)S(1)}, u32[]{:S(2)}, u32[]{:S(2)}) collective-permute-start(f32[72,128]{1,0:T(8,128)S(1)} %get-tuple-element.78), channel_id=1, source_target_pairs={{0,4},{1,5},{2,6},{3,7},{4,0},{5,1},{6,2},{7,3},{8,12},{9,13},{10,... | collective-permute-start | bytes 110600 | tf_op jit(solution)/shard_map/ppermute | solution.py:21
  75.7 19.4 %collective-permute-start.39 = (f32[72,128]{1,0:T(8,128)S(1)}, f32[72,128]{1,0:T(8,128)S(1)}, u32[]{:S(2)}, u32[]{:S(2)}) collective-permute-start(f32[72,128]{1,0:T(8,128)S(1)} %get-tuple-element.79), channel_id=1, source_target_pairs={{0,8},{1,9},{2,10},{3,11},{4,12},{5,13},{6,14},{7,15},{8,0},{9,1},... | collective-permute-start | bytes 110600 | tf_op jit(solution)/shard_map/ppermute | solution.py:21
  77.3 20.2 %collective-permute-start.40 = (f32[72,128]{1,0:T(8,128)S(1)}, f32[72,128]{1,0:T(8,128)S(1)}, u32[]{:S(2)}, u32[]{:S(2)}) collective-permute-start(f32[72,128]{1,0:T(8,128)S(1)} %get-tuple-element.80), channel_id=1, source_target_pairs={{0,12},{1,13},{2,14},{3,15},{4,8},{5,9},{6,10},{7,11},{8,4},{9,5},... | collective-permute-start | bytes 110600 | tf_op jit(solution)/shard_map/ppermute | solution.py:21
  83.5 15.5 %collective-permute-start.41 = (f32[72,128]{1,0:T(8,128)S(1)}, f32[72,128]{1,0:T(8,128)S(1)}, u32[]{:S(2)}, u32[]{:S(2)}) collective-permute-start(f32[72,128]{1,0:T(8,128)S(1)} %get-tuple-element.81), channel_id=1, source_target_pairs={{0,16},{1,17},{2,18},{3,19},{4,20},{5,21},{6,22},{7,23},{8,24},{9,... | collective-permute-start | bytes 110600 | tf_op jit(solution)/shard_map/ppermute | solution.py:21
  89.3 9.8 %collective-permute-start.42 = (f32[72,128]{1,0:T(8,128)S(1)}, f32[72,128]{1,0:T(8,128)S(1)}, u32[]{:S(2)}, u32[]{:S(2)}) collective-permute-start(f32[72,128]{1,0:T(8,128)S(1)} %get-tuple-element.82), channel_id=1, source_target_pairs={{0,20},{1,21},{2,22},{3,23},{4,16},{5,17},{6,18},{7,19},{8,28},{9,... | collective-permute-start | bytes 110600 | tf_op jit(solution)/shard_map/ppermute | solution.py:21
  93.7 7.3 %collective-permute-start.43 = (f32[72,128]{1,0:T(8,128)S(1)}, f32[72,128]{1,0:T(8,128)S(1)}, u32[]{:S(2)}, u32[]{:S(2)}) collective-permute-start(f32[72,128]{1,0:T(8,128)S(1)} %get-tuple-element.83), channel_id=1, source_target_pairs={{0,24},{1,25},{2,26},{3,27},{4,28},{5,29},{6,30},{7,31},{8,16},{9,... | collective-permute-start | bytes 110600 | tf_op jit(solution)/shard_map/ppermute | solution.py:21
  95.1 6.8 %collective-permute-start.44 = (f32[72,128]{1,0:T(8,128)S(1)}, f32[72,128]{1,0:T(8,128)S(1)}, u32[]{:S(2)}, u32[]{:S(2)}) collective-permute-start(f32[72,128]{1,0:T(8,128)S(1)} %get-tuple-element.84), channel_id=1, source_target_pairs={{0,28},{1,29},{2,30},{3,31},{4,24},{5,25},{6,26},{7,27},{8,20},{9,... | collective-permute-start | bytes 110600 | tf_op jit(solution)/shard_map/ppermute | solution.py:21
  97.5 7.4 %collective-permute-start.26 = (f32[72,128]{1,0:T(8,128)S(1)}, f32[72,128]{1,0:T(8,128)S(1)}, u32[]{:S(2)}, u32[]{:S(2)}) collective-permute-start(f32[72,128]{1,0:T(8,128)S(1)} %get-tuple-element.68), channel_id=1, source_target_pairs={{0,4},{1,5},{2,6},{3,7},{4,0},{5,1},{6,2},{7,3},{8,12},{9,13},{10,... | collective-permute-start | bytes 110600 | tf_op jit(solution)/shard_map/ppermute | solution.py:21
  99.0 7.8 %collective-permute-start.27 = (f32[72,128]{1,0:T(8,128)S(1)}, f32[72,128]{1,0:T(8,128)S(1)}, u32[]{:S(2)}, u32[]{:S(2)}) collective-permute-start(f32[72,128]{1,0:T(8,128)S(1)} %get-tuple-element.69), channel_id=1, source_target_pairs={{0,8},{1,9},{2,10},{3,11},{4,12},{5,13},{6,14},{7,15},{8,0},{9,1},... | collective-permute-start | bytes 110600 | tf_op jit(solution)/shard_map/ppermute | solution.py:21
  99.0 10.3 %collective-permute-start.28 = (f32[72,128]{1,0:T(8,128)S(1)}, f32[72,128]{1,0:T(8,128)S(1)}, u32[]{:S(2)}, u32[]{:S(2)}) collective-permute-start(f32[72,128]{1,0:T(8,128)S(1)} %get-tuple-element.70), channel_id=1, source_target_pairs={{0,12},{1,13},{2,14},{3,15},{4,8},{5,9},{6,10},{7,11},{8,4},{9,5},... | collective-permute-start | bytes 110600 | tf_op jit(solution)/shard_map/ppermute | solution.py:21
  101.0 9.9 %collective-permute-start.29 = (f32[72,128]{1,0:T(8,128)S(1)}, f32[72,128]{1,0:T(8,128)S(1)}, u32[]{:S(2)}, u32[]{:S(2)}) collective-permute-start(f32[72,128]{1,0:T(8,128)S(1)} %get-tuple-element.71), channel_id=1, source_target_pairs={{0,16},{1,17},{2,18},{3,19},{4,20},{5,21},{6,22},{7,23},{8,24},{9,... | collective-permute-start | bytes 110600 | tf_op jit(solution)/shard_map/ppermute | solution.py:21
  101.9 9.0 %collective-permute-start.30 = (f32[72,128]{1,0:T(8,128)S(1)}, f32[72,128]{1,0:T(8,128)S(1)}, u32[]{:S(2)}, u32[]{:S(2)}) collective-permute-start(f32[72,128]{1,0:T(8,128)S(1)} %get-tuple-element.72), channel_id=1, source_target_pairs={{0,20},{1,21},{2,22},{3,23},{4,16},{5,17},{6,18},{7,19},{8,28},{9,... | collective-permute-start | bytes 110600 | tf_op jit(solution)/shard_map/ppermute | solution.py:21
  104.9 8.0 %collective-permute-start.31 = (f32[72,128]{1,0:T(8,128)S(1)}, f32[72,128]{1,0:T(8,128)S(1)}, u32[]{:S(2)}, u32[]{:S(2)}) collective-permute-start(f32[72,128]{1,0:T(8,128)S(1)} %get-tuple-element.73), channel_id=1, source_target_pairs={{0,24},{1,25},{2,26},{3,27},{4,28},{5,29},{6,30},{7,31},{8,16},{9,... | collective-permute-start | bytes 110600 | tf_op jit(solution)/shard_map/ppermute | solution.py:21
  106.9 6.8 %collective-permute-start.32 = (f32[72,128]{1,0:T(8,128)S(1)}, f32[72,128]{1,0:T(8,128)S(1)}, u32[]{:S(2)}, u32[]{:S(2)}) collective-permute-start(f32[72,128]{1,0:T(8,128)S(1)} %get-tuple-element.74), channel_id=1, source_target_pairs={{0,28},{1,29},{2,30},{3,31},{4,24},{5,25},{6,26},{7,27},{8,20},{9,... | collective-permute-start | bytes 110600 | tf_op jit(solution)/shard_map/ppermute | solution.py:21
  109.4 7.4 %collective-permute-start.14 = (f32[72,128]{1,0:T(8,128)S(1)}, f32[72,128]{1,0:T(8,128)S(1)}, u32[]{:S(2)}, u32[]{:S(2)}) collective-permute-start(f32[72,128]{1,0:T(8,128)S(1)} %get-tuple-element.58), channel_id=1, source_target_pairs={{0,4},{1,5},{2,6},{3,7},{4,0},{5,1},{6,2},{7,3},{8,12},{9,13},{10,... | collective-permute-start | bytes 110600 | tf_op jit(solution)/shard_map/ppermute | solution.py:21
  110.9 7.8 %collective-permute-start.15 = (f32[72,128]{1,0:T(8,128)S(1)}, f32[72,128]{1,0:T(8,128)S(1)}, u32[]{:S(2)}, u32[]{:S(2)}) collective-permute-start(f32[72,128]{1,0:T(8,128)S(1)} %get-tuple-element.59), channel_id=1, source_target_pairs={{0,8},{1,9},{2,10},{3,11},{4,12},{5,13},{6,14},{7,15},{8,0},{9,1},... | collective-permute-start | bytes 110600 | tf_op jit(solution)/shard_map/ppermute | solution.py:21
  110.9 10.3 %collective-permute-start.16 = (f32[72,128]{1,0:T(8,128)S(1)}, f32[72,128]{1,0:T(8,128)S(1)}, u32[]{:S(2)}, u32[]{:S(2)}) collective-permute-start(f32[72,128]{1,0:T(8,128)S(1)} %get-tuple-element.60), channel_id=1, source_target_pairs={{0,12},{1,13},{2,14},{3,15},{4,8},{5,9},{6,10},{7,11},{8,4},{9,5},... | collective-permute-start | bytes 110600 | tf_op jit(solution)/shard_map/ppermute | solution.py:21
  112.9 9.9 %collective-permute-start.17 = (f32[72,128]{1,0:T(8,128)S(1)}, f32[72,128]{1,0:T(8,128)S(1)}, u32[]{:S(2)}, u32[]{:S(2)}) collective-permute-start(f32[72,128]{1,0:T(8,128)S(1)} %get-tuple-element.61), channel_id=1, source_target_pairs={{0,16},{1,17},{2,18},{3,19},{4,20},{5,21},{6,22},{7,23},{8,24},{9,... | collective-permute-start | bytes 110600 | tf_op jit(solution)/shard_map/ppermute | solution.py:21
  113.7 9.0 %collective-permute-start.18 = (f32[72,128]{1,0:T(8,128)S(1)}, f32[72,128]{1,0:T(8,128)S(1)}, u32[]{:S(2)}, u32[]{:S(2)}) collective-permute-start(f32[72,128]{1,0:T(8,128)S(1)} %get-tuple-element.62), channel_id=1, source_target_pairs={{0,20},{1,21},{2,22},{3,23},{4,16},{5,17},{6,18},{7,19},{8,28},{9,... | collective-permute-start | bytes 110600 | tf_op jit(solution)/shard_map/ppermute | solution.py:21
  116.7 8.0 %collective-permute-start.19 = (f32[72,128]{1,0:T(8,128)S(1)}, f32[72,128]{1,0:T(8,128)S(1)}, u32[]{:S(2)}, u32[]{:S(2)}) collective-permute-start(f32[72,128]{1,0:T(8,128)S(1)} %get-tuple-element.63), channel_id=1, source_target_pairs={{0,24},{1,25},{2,26},{3,27},{4,28},{5,29},{6,30},{7,31},{8,16},{9,... | collective-permute-start | bytes 110600 | tf_op jit(solution)/shard_map/ppermute | solution.py:21
  118.7 6.8 %collective-permute-start.20 = (f32[72,128]{1,0:T(8,128)S(1)}, f32[72,128]{1,0:T(8,128)S(1)}, u32[]{:S(2)}, u32[]{:S(2)}) collective-permute-start(f32[72,128]{1,0:T(8,128)S(1)} %get-tuple-element.64), channel_id=1, source_target_pairs={{0,28},{1,29},{2,30},{3,31},{4,24},{5,25},{6,26},{7,27},{8,20},{9,... | collective-permute-start | bytes 110600 | tf_op jit(solution)/shard_map/ppermute | solution.py:21
  121.2 7.4 %collective-permute-start.2 = (f32[72,128]{1,0:T(8,128)S(1)}, f32[72,128]{1,0:T(8,128)S(1)}, u32[]{:S(2)}, u32[]{:S(2)}) collective-permute-start(f32[72,128]{1,0:T(8,128)S(1)} %get-tuple-element.48), channel_id=1, source_target_pairs={{0,4},{1,5},{2,6},{3,7},{4,0},{5,1},{6,2},{7,3},{8,12},{9,13},{10,... | collective-permute-start | bytes 110600 | tf_op jit(solution)/shard_map/ppermute | solution.py:21
  122.7 7.2 %collective-permute-start.3 = (f32[72,128]{1,0:T(8,128)S(1)}, f32[72,128]{1,0:T(8,128)S(1)}, u32[]{:S(2)}, u32[]{:S(2)}) collective-permute-start(f32[72,128]{1,0:T(8,128)S(1)} %get-tuple-element.49), channel_id=1, source_target_pairs={{0,8},{1,9},{2,10},{3,11},{4,12},{5,13},{6,14},{7,15},{8,0},{9,1},... | collective-permute-start | bytes 110600 | tf_op jit(solution)/shard_map/ppermute | solution.py:21
  122.7 9.7 %collective-permute-start.4 = (f32[72,128]{1,0:T(8,128)S(1)}, f32[72,128]{1,0:T(8,128)S(1)}, u32[]{:S(2)}, u32[]{:S(2)}) collective-permute-start(f32[72,128]{1,0:T(8,128)S(1)} %get-tuple-element.50), channel_id=1, source_target_pairs={{0,12},{1,13},{2,14},{3,15},{4,8},{5,9},{6,10},{7,11},{8,4},{9,5},... | collective-permute-start | bytes 110600 | tf_op jit(solution)/shard_map/ppermute | solution.py:21
  124.7 7.8 %collective-permute-start.5 = (f32[72,128]{1,0:T(8,128)S(1)}, f32[72,128]{1,0:T(8,128)S(1)}, u32[]{:S(2)}, u32[]{:S(2)}) collective-permute-start(f32[72,128]{1,0:T(8,128)S(1)} %get-tuple-element.51), channel_id=1, source_target_pairs={{0,16},{1,17},{2,18},{3,19},{4,20},{5,21},{6,22},{7,23},{8,24},{9,... | collective-permute-start | bytes 110600 | tf_op jit(solution)/shard_map/ppermute | solution.py:21
  125.5 8.6 %collective-permute-start.6 = (f32[72,128]{1,0:T(8,128)S(1)}, f32[72,128]{1,0:T(8,128)S(1)}, u32[]{:S(2)}, u32[]{:S(2)}) collective-permute-start(f32[72,128]{1,0:T(8,128)S(1)} %get-tuple-element.52), channel_id=1, source_target_pairs={{0,20},{1,21},{2,22},{3,23},{4,16},{5,17},{6,18},{7,19},{8,28},{9,... | collective-permute-start | bytes 110600 | tf_op jit(solution)/shard_map/ppermute | solution.py:21
  128.6 6.0 %collective-permute-start.7 = (f32[72,128]{1,0:T(8,128)S(1)}, f32[72,128]{1,0:T(8,128)S(1)}, u32[]{:S(2)}, u32[]{:S(2)}) collective-permute-start(f32[72,128]{1,0:T(8,128)S(1)} %get-tuple-element.53), channel_id=1, source_target_pairs={{0,24},{1,25},{2,26},{3,27},{4,28},{5,29},{6,30},{7,31},{8,16},{9,... | collective-permute-start | bytes 110600 | tf_op jit(solution)/shard_map/ppermute | solution.py:21
  129.9 6.7 %collective-permute-start.8 = (f32[72,128]{1,0:T(8,128)S(1)}, f32[72,128]{1,0:T(8,128)S(1)}, u32[]{:S(2)}, u32[]{:S(2)}) collective-permute-start(f32[72,128]{1,0:T(8,128)S(1)} %get-tuple-element.54), channel_id=1, source_target_pairs={{0,28},{1,29},{2,30},{3,31},{4,24},{5,25},{6,26},{7,27},{8,20},{9,... | collective-permute-start | bytes 110600 | tf_op jit(solution)/shard_map/ppermute | solution.py:21
  132.4 5.7 %collective-permute-start.45 = (f32[64,128]{1,0:T(8,128)S(1)}, f32[64,128]{1,0:T(8,128)S(1)}, u32[]{:S(2)}, u32[]{:S(2)}) collective-permute-start(f32[64,128]{1,0:T(8,128)S(1)} %shard_map.86.refs_12_), channel_id=1, source_target_pairs={{0,1},{1,0},{2,3},{3,2},{4,5},{5,4},{6,7},{7,6},{8,9},{9,8},{10,11... | collective-permute-start | bytes 98312 | tf_op jit(solution)/shard_map/ppermute | solution.py:21
  132.5 5.6 %collective-permute-start.46 = (f32[64,128]{1,0:T(8,128)S(1)}, f32[64,128]{1,0:T(8,128)S(1)}, u32[]{:S(2)}, u32[]{:S(2)}) collective-permute-start(f32[64,128]{1,0:T(8,128)S(1)} %shard_map.86.refs_12_), channel_id=1, source_target_pairs={{0,2},{1,3},{2,0},{3,1},{4,6},{5,7},{6,4},{7,5},{8,10},{9,11},{10,... | collective-permute-start | bytes 98312 | tf_op jit(solution)/shard_map/ppermute | solution.py:21
  134.2 4.6 %collective-permute-start.47 = (f32[64,128]{1,0:T(8,128)S(1)}, f32[64,128]{1,0:T(8,128)S(1)}, u32[]{:S(2)}, u32[]{:S(2)}) collective-permute-start(f32[64,128]{1,0:T(8,128)S(1)} %shard_map.86.refs_12_), channel_id=1, source_target_pairs={{0,3},{1,2},{2,1},{3,0},{4,7},{5,6},{6,5},{7,4},{8,11},{9,10},{10,... | collective-permute-start | bytes 98312 | tf_op jit(solution)/shard_map/ppermute | solution.py:21
  134.5 5.8 %collective-permute-start.33 = (f32[64,128]{1,0:T(8,128)S(1)}, f32[64,128]{1,0:T(8,128)S(1)}, u32[]{:S(2)}, u32[]{:S(2)}) collective-permute-start(f32[64,128]{1,0:T(8,128)S(1)} %shard_map.81.refs_8_), channel_id=1, source_target_pairs={{0,1},{1,0},{2,3},{3,2},{4,5},{5,4},{6,7},{7,6},{8,9},{9,8},{10,11... | collective-permute-start | bytes 98312 | tf_op jit(solution)/shard_map/ppermute | solution.py:21
  136.6 3.9 %collective-permute-start.34 = (f32[64,128]{1,0:T(8,128)S(1)}, f32[64,128]{1,0:T(8,128)S(1)}, u32[]{:S(2)}, u32[]{:S(2)}) collective-permute-start(f32[64,128]{1,0:T(8,128)S(1)} %shard_map.81.refs_8_), channel_id=1, source_target_pairs={{0,2},{1,3},{2,0},{3,1},{4,6},{5,7},{6,4},{7,5},{8,10},{9,11},{10,... | collective-permute-start | bytes 98312 | tf_op jit(solution)/shard_map/ppermute | solution.py:21
  138.1 4.2 %collective-permute-start.35 = (f32[64,128]{1,0:T(8,128)S(1)}, f32[64,128]{1,0:T(8,128)S(1)}, u32[]{:S(2)}, u32[]{:S(2)}) collective-permute-start(f32[64,128]{1,0:T(8,128)S(1)} %shard_map.81.refs_8_), channel_id=1, source_target_pairs={{0,3},{1,2},{2,1},{3,0},{4,7},{5,6},{6,5},{7,4},{8,11},{9,10},{10,... | collective-permute-start | bytes 98312 | tf_op jit(solution)/shard_map/ppermute | solution.py:21
  138.1 4.3 %collective-permute-start.21 = (f32[64,128]{1,0:T(8,128)S(1)}, f32[64,128]{1,0:T(8,128)S(1)}, u32[]{:S(2)}, u32[]{:S(2)}) collective-permute-start(f32[64,128]{1,0:T(8,128)S(1)} %shard_map.76.refs_4_), channel_id=1, source_target_pairs={{0,1},{1,0},{2,3},{3,2},{4,5},{5,4},{6,7},{7,6},{8,9},{9,8},{10,11... | collective-permute-start | bytes 98312 | tf_op jit(solution)/shard_map/ppermute | solution.py:21
  138.8 4.0 %collective-permute-start.22 = (f32[64,128]{1,0:T(8,128)S(1)}, f32[64,128]{1,0:T(8,128)S(1)}, u32[]{:S(2)}, u32[]{:S(2)}) collective-permute-start(f32[64,128]{1,0:T(8,128)S(1)} %shard_map.76.refs_4_), channel_id=1, source_target_pairs={{0,2},{1,3},{2,0},{3,1},{4,6},{5,7},{6,4},{7,5},{8,10},{9,11},{10,... | collective-permute-start | bytes 98312 | tf_op jit(solution)/shard_map/ppermute | solution.py:21
  140.4 3.6 %collective-permute-start.23 = (f32[64,128]{1,0:T(8,128)S(1)}, f32[64,128]{1,0:T(8,128)S(1)}, u32[]{:S(2)}, u32[]{:S(2)}) collective-permute-start(f32[64,128]{1,0:T(8,128)S(1)} %shard_map.76.refs_4_), channel_id=1, source_target_pairs={{0,3},{1,2},{2,1},{3,0},{4,7},{5,6},{6,5},{7,4},{8,11},{9,10},{10,... | collective-permute-start | bytes 98312 | tf_op jit(solution)/shard_map/ppermute | solution.py:21
  140.5 4.1 %collective-permute-start.10 = (f32[64,128]{1,0:T(8,128)S(1)}, f32[64,128]{1,0:T(8,128)S(1)}, u32[]{:S(2)}, u32[]{:S(2)}) collective-permute-start(f32[64,128]{1,0:T(8,128)S(1)} %shard_map.71.refs_0_), channel_id=1, source_target_pairs={{0,2},{1,3},{2,0},{3,1},{4,6},{5,7},{6,4},{7,5},{8,10},{9,11},{10,... | collective-permute-start | bytes 98312 | tf_op jit(solution)/shard_map/ppermute | solution.py:21
  142.3 3.6 %collective-permute-start.11 = (f32[64,128]{1,0:T(8,128)S(1)}, f32[64,128]{1,0:T(8,128)S(1)}, u32[]{:S(2)}, u32[]{:S(2)}) collective-permute-start(f32[64,128]{1,0:T(8,128)S(1)} %shard_map.71.refs_0_), channel_id=1, source_target_pairs={{0,3},{1,2},{2,1},{3,0},{4,7},{5,6},{6,5},{7,4},{8,11},{9,10},{10,... | collective-permute-start | bytes 98312 | tf_op jit(solution)/shard_map/ppermute | solution.py:21
  142.4 3.5 %collective-permute-start.9 = (f32[64,128]{1,0:T(8,128)S(1)}, f32[64,128]{1,0:T(8,128)S(1)}, u32[]{:S(2)}, u32[]{:S(2)}) collective-permute-start(f32[64,128]{1,0:T(8,128)S(1)} %shard_map.71.refs_0_), channel_id=1, source_target_pairs={{0,1},{1,0},{2,3},{3,2},{4,5},{5,4},{6,7},{7,6},{8,9},{9,8},{10,11... | collective-permute-start | bytes 98312 | tf_op jit(solution)/shard_map/ppermute | solution.py:21

commit v2 on v0

v2 whole, which is shorter than its diff:
```python
import functools
import math

import jax
import jax.numpy as jnp
from jax import lax
from jax.experimental import pallas as pl
from jax.experimental.pallas import tpu as pltpu
from jax.sharding import PartitionSpec as P

H = 8
CORES = 2
AXES = ("tm", "patch")
VMEM = pl.BlockSpec(memory_space=pltpu.VMEM)
SMEM = pl.BlockSpec(memory_space=pltpu.SMEM)
PARAMS = pltpu.CompilerParams(vmem_limit_bytes=48 * 2**20)
EXTRA = 8
LEVELS = 30.0 * 2.0**10
UNITS = (2.0**20, 2.0**10, 1.0, 2.0**-10, 2.0**-20)


def xor_permute(value, n, step):
    return lax.ppermute(value, AXES, [(i, i ^ step) for i in range(n)])


def project_kernel(with_query, at_ref, t_ref, wk_ref, wv_ref, *refs):
    def dot(a, w):
        return jnp.dot(a[...], w[...], preferred_element_type=jnp.float32).astype(jnp.bfloat16)

    if with_query:
        l_ref, wq_ref, k_ref, v_ref, q_ref = refs
        q_ref[...] = dot(l_ref, wq_ref).T
    else:
        k_ref, v_ref = refs
    k_ref[...] = dot(t_ref, wk_ref)
    v_ref[...] = dot(t_ref, wv_ref).T


def project(at, tokens, w_key, w_value, latents=None, w_query=None, steps=4):
    (n, d), cols = tokens.shape, w_key.shape[1] // CORES
    weight = pl.BlockSpec((d, cols), lambda i, at: (0, at[3]))
    args = [tokens, w_key, w_value]
    in_specs = [pl.BlockSpec((n // steps, d), lambda i, at: (i, 0)), weight, weight]
    outs = [(n, cols), (cols, n)]
    out_specs = [
        pl.BlockSpec((n // steps, cols), lambda i, at: (i, 0)),
        pl.BlockSpec((cols, n // steps), lambda i, at: (0, i)),
    ]
    flops = 4 * n * d * cols
    if latents is not None:
        m = latents.shape[0]
        args += [latents, w_query]
        in_specs += [pl.BlockSpec((m // steps, d), lambda i, at: (i, 0)), weight]
        outs.append((cols, m))
        out_specs.append(pl.BlockSpec((cols, m // steps), lambda i, at: (0, i)))
        flops += 2 * m * d * cols
    return pl.pallas_call(
        functools.partial(project_kernel, latents is not None),
        grid_spec=pltpu.PrefetchScalarGridSpec(
            num_scalar_prefetch=1, grid=(steps,), in_specs=in_specs, out_specs=out_specs
        ),
        out_shape=[jax.ShapeDtypeStruct(s, jnp.bfloat16) for s in outs],
        compiler_params=PARAMS,
        cost_estimate=pl.CostEstimate(flops=flops, bytes_accessed=2 * (n * d + 2 * d * cols + 2 * n * cols), transcendentals=0),
    )(at, *args)


def merge(parts):
    peak = functools.reduce(jnp.maximum, [p for _, _, p in parts])
    factors = [jnp.exp2(p - peak) for _, _, p in parts]
    num, den = (
        functools.reduce(lambda a, b: a + b, [part[i] * f for part, f in zip(parts, factors)]) for i in range(2)
    )
    return num, den, peak


def nearest(value):
    return jnp.floor(value + 0.5)


def spread(value):
    place = nearest(jnp.abs(value) * LEVELS) * 2.0**-10
    power = jnp.floor(place)
    return jnp.where(value < 0, -1.0, 1.0) * (1.0 + place - power) * jnp.exp2(power - 14.0)


def gather_up(value):
    size = jnp.abs(value)
    power = jnp.clip(jnp.floor(jnp.log2(size)), -14.0, 15.0)
    return jnp.where(value < 0, -1.0, 1.0) * (power + 13.0 + size * jnp.exp2(-power)) * (2.0**10 / LEVELS)


def encode(part):
    num, den, peak = part
    mean = num / den
    most = jnp.max(jnp.abs(mean), axis=0, keepdims=True)
    exponent = jnp.ceil(jnp.log2(jnp.clip(most, 2.0**-100, 2.0**100)) + 2.0**-10)
    rest, digits = peak + jnp.log2(den), [exponent]
    for unit in UNITS[:-1]:
        digits.append(nearest(rest * (1.0 / unit)))
        rest = rest - digits[-1] * unit
    digits.append(rest * (1.0 / UNITS[-1]))
    row = lax.broadcasted_iota(jnp.int32, (EXTRA, mean.shape[1]), 0)
    tail = jnp.zeros((EXTRA, mean.shape[1]), jnp.float32)
    for i, digit in enumerate(digits):
        tail = jnp.where(row == i, digit, tail)
    return jnp.concatenate([spread(mean * jnp.exp2(-exponent)), tail], axis=0)


def decode(rows):
    feats = rows.shape[0] - EXTRA
    exponent, *digits = (rows[feats + i : feats + i + 1] for i in range(len(UNITS) + 1))
    peak = functools.reduce(lambda a, b: a + b, [d * u for d, u in zip(reversed(digits), reversed(UNITS))])
    return gather_up(rows[:feats]) * jnp.exp2(exponent), jnp.ones_like(peak), peak


def attend_kernel(tile, chunk, blocks, head_ref, q_ref, *refs):
    kv, got, (o_ref, s0, s1) = refs[: 2 * blocks], refs[2 * blocks : -3], refs[-3:]
    size, latents = q_ref.shape
    tokens = kv[0].shape[0]
    n_tm, rows, block = o_ref.shape
    coef = math.log2(math.e) / math.sqrt(size)
    slots = (s0, s1)
    ones = jnp.ones((16, chunk), jnp.bfloat16)
    items = [(j, b) for j in range(latents // tile) for b in range(blocks)]
    peak, done = None, []
    for i in range(len(items) + 1):
        now, before = slots[i % 2], slots[(i - 1) % 2]
        acc, top = jnp.zeros((size + 16, tile), jnp.float32), None
        for c in range(tokens // chunk):
            part = slice(c * chunk, (c + 1) * chunk)
            if i < len(items):
                j, b = items[i]
                s = jnp.dot(kv[2 * b][part, :], q_ref[:, j * tile : (j + 1) * tile], preferred_element_type=jnp.float32)
                now[part, :] = s
                high = jnp.max(s.reshape(chunk // 8, 8, tile), axis=0)
                top = high if top is None else jnp.maximum(top, high)
            if i > 0:
                w = jnp.exp2((before[part, :] - peak) * coef).astype(jnp.bfloat16)
                v = jnp.concatenate([kv[2 * items[i - 1][1] + 1][:, part], ones], axis=0)
                acc = acc + jnp.dot(v, w, preferred_element_type=jnp.float32)
        if i > 0:
            done.append((acc[:size], acc[size : size + 1], peak * coef))
            if len(done) == blocks:
                for b in range(tile // block):
                    tm = items[i - 1][0] * (tile // block) + b
                    lanes = slice(b * block, (b + 1) * block)
                    o_ref[tm] = encode(merge([tuple(v[:, lanes] for v in d) for d in done] + [decode(g[tm]) for g in got]))
                done = []
        if i < len(items):
            peak = jnp.max(top, axis=0, keepdims=True)


def attend(head, query_t, blocks, got, n_tm, heads, tile=512, chunk=1024):
    size, latents, tokens = query_t.shape[0] // heads, query_t.shape[1], blocks[0][0].shape[0]
    shape = (n_tm, size + EXTRA, latents // n_tm)
    whole = pl.BlockSpec(shape, lambda i, h: (0, 0, 0))
    return pl.pallas_call(
        functools.partial(attend_kernel, tile, chunk, len(blocks)),
        grid_spec=pltpu.PrefetchScalarGridSpec(
            num_scalar_prefetch=1,
            grid=(1,),
            in_specs=[pl.BlockSpec((size, latents), lambda i, h: (h[0], 0))]
            + [
                pl.BlockSpec((tokens, size), lambda i, h: (0, h[0])),
                pl.BlockSpec((size, tokens), lambda i, h: (h[0], 0)),
            ]
            * len(blocks)
            + [whole] * len(got),
            out_specs=whole,
            scratch_shapes=[pltpu.VMEM((tokens, tile), jnp.float32)] * 2,
        ),
        out_shape=jax.ShapeDtypeStruct(shape, jnp.float32),
        compiler_params=PARAMS,
        cost_estimate=pl.CostEstimate(
            flops=4 * tokens * latents * size * len(blocks),
            bytes_accessed=4 * math.prod(shape),
            transcendentals=tokens * latents * len(blocks),
        ),
    )(head.astype(jnp.int32).reshape(1), query_t, *[a for pair in blocks for a in pair], *got)


def attended_kernel(part_ref, out):
    n_tm, heads, rows, _ = part_ref.shape
    feats = rows - EXTRA
    for i in range(heads):
        num, den, _ = merge([decode(part_ref[t, i]) for t in range(n_tm)])
        out[i * feats : (i + 1) * feats, :] = num / den


def attended(parts):
    n_tm, heads, rows, block = parts.shape
    return pl.pallas_call(
        attended_kernel,
        out_shape=jax.ShapeDtypeStruct(((rows - EXTRA) * heads, block), jnp.float32),
        in_specs=[VMEM],
        out_specs=VMEM,
        compiler_params=PARAMS,
        cost_estimate=pl.CostEstimate(flops=parts.size * 4, bytes_accessed=parts.size * 4, transcendentals=0),
    )(parts)


def finish_kernel(at_ref, *refs):
    pieces, (w_ref, o_ref, normed) = refs[:-3], refs[-3:]
    feats, me = pieces[0].shape[0], at_ref[2]
    width = feats * len(pieces)
    squares = functools.reduce(lambda a, b: a + b, [jnp.square(p[...]) for p in pieces])
    scale = lax.rsqrt(jnp.sum(squares, axis=0, keepdims=True) * (1.0 / width) + 1e-06)
    for s, piece in enumerate(pieces):
        owner = me ^ s
        at = owner % CORES * (width // CORES) + owner // CORES * feats
        normed[pl.ds(pl.multiple_of(at, feats), feats), :] = (piece[...] * scale).astype(jnp.bfloat16)
    o_ref[...] = lax.dot_general(
        normed[...], w_ref[...], (((0,), (0,)), ((), ())), preferred_element_type=jnp.float32
    ).astype(jnp.bfloat16)


def finish(at, pieces, w_out):
    block = pieces[0].shape[1]
    return pl.pallas_call(
        finish_kernel,
        out_shape=jax.ShapeDtypeStruct((block, w_out.shape[1]), jnp.bfloat16),
        in_specs=[SMEM] + [VMEM] * (len(pieces) + 1),
        out_specs=VMEM,
        scratch_shapes=[pltpu.VMEM((w_out.shape[0], block), jnp.bfloat16)],
        compiler_params=PARAMS,
        cost_estimate=pl.CostEstimate(flops=2 * block * w_out.size, bytes_accessed=2 * w_out.size, transcendentals=0),
    )(at, *pieces, w_out)


def per_device(n_tm, n_patch, latents, tokens, w_query, w_key, w_value, w_out):
    n, n_x = n_tm * n_patch, n_patch // CORES
    tm, patch = lax.axis_index("tm"), lax.axis_index("patch")
    x, core = patch // CORES, patch % CORES
    at = jnp.stack([x, tm, patch, core]).astype(jnp.int32)
    heads = H // CORES
    own_heads = heads // n_x

    sibling = xor_permute(tokens, n, 1)
    keys, vals_t, query_t = project(at, tokens, w_key, w_value, latents, w_query)
    near = [(keys, vals_t)]
    both = None
    got = [[] for _ in range(own_heads)]
    mine = []
    for s in range(n_x - 1, -1, -1):
        for j in range(own_heads):
            head = (x ^ s) * own_heads + j
            if both is None:
                first = attend(head, query_t, near, [], n_tm, heads)
                sibling, first = lax.optimization_barrier((sibling, first))
                far = [tuple(project(at, sibling, w_key, w_value))]
                both = near + far
                part = attend(head, query_t, far, [first], n_tm, heads)
            else:
                part = attend(head, query_t, both, [] if s else got[j], n_tm, heads)
            query_t, part = lax.optimization_barrier((query_t, part))
            if s:
                got[j].append(xor_permute(part.astype(jnp.float16), n, CORES * s).astype(jnp.float32))
            else:
                mine.append(part.astype(jnp.float16))
    mine = lax.all_to_all(jnp.stack(mine, axis=1), "tm", 0, 0, tiled=True).astype(jnp.float32)
    pieces = [attended(mine)]
    pieces += [xor_permute(pieces[0], n, CORES * s) for s in range(1, n_x)]
    pieces = [p for piece in pieces for p in (piece, xor_permute(piece, n, 1))]
    return finish(at, pieces, w_out)


def solution(mesh):
    return jax.shard_map(
        functools.partial(per_device, mesh.shape["tm"], mesh.shape["patch"]),
        mesh=mesh,
        in_specs=(P(), P(("tm", "patch"), None), P(), P(), P(), P(None, "patch")),
        out_specs=P("tm", "patch"),
        check_vma=False,
    )
```

time: 413 us -> 86.6 us (0.21)
  waiting for transfers between devices: 217 us -> 5.3 us
  matrix products: 91.2 us -> 0 us
  Pallas kernels: 0 us -> 49.8 us
  blocking collectives: 47.9 us -> 22 us
  other arithmetic: 28.7 us -> 3.15 us
  between operations: 14 us -> 0.16 us
  local copies, waits for them, and re-layouts: 11.6 us -> 1.32 us
  starting transfers between devices: 0.26 us -> 4.56 us
    unnamed x4 -> x0, waiting for transfers between devices: 217 us -> none
    dot_general x20 -> x0, matrix products: 91.2 us -> none  [the longest x8 37.2 us: block_part(): jnp.dot(weight, vals[:, cols], preferred_element_type=jnp.float32)]
    pallas_call x0 -> x9, Pallas kernels: none -> 49.8 us  [the longest x5 29.9 us: attend(): pl.pallas_call(functools.partial(attend_kernel, tile, chunk, len(blocks))...]
    pmax x1 -> x0, blocking collectives: 42.2 us -> none  [per_device(): lax.pmax(peaks.astype(jnp.bfloat16), ('tm', 'patch')).astype(peaks.dtype)]
    reduce_sum x9 -> x0, other arithmetic: 23.4 us -> none  [the longest x8 23.3 us: block_part(): totals.append(jnp.sum(weight.astype(jnp.float32), axis=1))]
    all_to_all x0 -> x1, blocking collectives: none -> 22 us  [per_device(): lax.all_to_all(jnp.stack(mine, axis=1), 'tm', 0, 0, tiled=True)]
    unnamed x56 -> x8, local copies, waits for them, and re-layouts: 11.4 us -> 1.32 us
    all_gather x1 -> x0, blocking collectives: 5.79 us -> none  [per_device(): lax.all_gather(finish(own_rows, own_total), 'patch', axis=0, tiled=True)]
  transfers between devices with their start and end apart: 2 -> 6, of which waited for: 2 -> 3; matrix products, arithmetic and copies ran while one was open for 14% -> 1% of each run, Pallas kernels for 0% -> 32%
where the time goes in v2:
time: 86.6 us; the launch traced here: 86.2 us
  Pallas kernels  49.8 us (58%)
  blocking collectives  22 us (25%)
  waiting for transfers between devices  5.3 us (6%)
  starting transfers between devices  4.56 us (5%)
  other arithmetic  3.15 us (4%)
  local copies, waits for them, and re-layouts  1.32 us (2%)
    pallas_call x5, Pallas kernels, attend(): pl.pallas_call(functools.partial(attend_kernel, tile, chunk, len(blocks))...  29.9 us
    all_to_all x1, blocking collectives, per_device(): lax.all_to_all(jnp.stack(mine, axis=1), 'tm', 0, 0, tiled=True)  22 us
    pallas_call x2, Pallas kernels, project(): pl.pallas_call(functools.partial(project_kernel, latents is not None), gr...  17.7 us
    ppermute x6, waiting for transfers between devices, xor_permute(): return lax.ppermute(value, AXES, [(i, i ^ step) for i in range(n)])  5.3 us
    ppermute x6, starting transfers between devices, xor_permute(): return lax.ppermute(value, AXES, [(i, i ^ step) for i in range(n)])  4.56 us
    convert_element_type x2, other arithmetic, per_device(): xor_permute(part.astype(jnp.float16), n, CORES * s).astype(jnp.float32)  1.99 us
  transfers between devices with their start and end apart: 6, of which 3 were waited for; matrix products, arithmetic and copies ran while one was open for 1% of the time, Pallas kernels for 32%

profile of v2, /device:TPU:0, one launch (start us, length us, event | category | flops | bytes accessed | tf_op | source)
XLA Modules:
  0.0 86.2 jit_solution(6305508324387688741)
XLA Ops:
  0.0 0.5 collective-permute-start
  0.5 0.1 pad_add_fusion.at_ref
  0.5 9.6 %shard_map.64 = (bf16[2048,512]{1,0:T(8,128)(2,1)S(1)}, bf16[512,2048]{1,0:T(8,128)(2,1)S(1)}, bf16[512,1024]{1,0:T(8,128)(2,1)S(1)}) custom-call(s32[4]{0:T(128)S(1)} %pad_add_fusion.at_ref, bf16[2048,1024]{1,0:T(8,128)(2,1)} %t_ref.1, bf16[1024,1024]{1,0:T(8,128)(2,1)} %wk_ref.3, bf16[1024,1024]{1,0:T(8,128)(2,1)} %wv_ref.3, bf16[1024,1024]{1,0:T(8,128)(2,1)} %refs_0_.1, ...), custom_call_target="tpu_custom_call" | custom-call | flops 5368709120 | bytes 10485760 | tf_op jit(solution)/shard_map/pallas_call | solution.py:57
  10.2 0.0 copy-start
  10.2 3.3 %shard_map.65.refs_2_ = f32[8,136,128]{2,1,0:T(8,128)S(1)} custom-call(s32[1]{0:T(128)} %bitcast.4.head_ref, bf16[512,1024]{1,0:T(8,128)(2,1)S(1)} %get-tuple-element.30.q_ref, bf16[2048,512]{1,0:T(8,128)(2,1)S(1)} %get-tuple-element.20.refs_0_, bf16[512,2048]{1,0:T(8,128)(2,1)S(1)} %get-tuple-element.21.refs_1_), custom_call_target="tpu_custom_call" | custom-call | flops 1073741824 | bytes 557056 | tf_op jit(solution)/shard_map/pallas_call | solution.py:158
  13.5 0.0 collective-permute-done.t_ref
  13.5 8.1 %shard_map.66 = (bf16[2048,512]{1,0:T(8,128)(2,1)S(1)}, bf16[512,2048]{1,0:T(8,128)(2,1)S(1)}) custom-call(s32[4]{0:T(128)S(1)} %pad_add_fusion.at_ref, bf16[2048,1024]{1,0:T(8,128)(2,1)} %collective-permute-done.t_ref, bf16[1024,1024]{1,0:T(8,128)(2,1)} %wk_ref.3, bf16[1024,1024]{1,0:T(8,128)(2,1)} %wv_ref.3), custom_call_target="tpu_custom_call" | custom-call | flops 4294967296 | bytes 10485760 | tf_op jit(solution)/shard_map/pallas_call | solution.py:57
  21.6 0.0 copy-start.2
  21.6 1.3 %copy-done.2 = bf16[512,2048]{1,0:T(8,128)(2,1)} copy-done((bf16[512,2048]{1,0:T(8,128)(2,1)}, bf16[512,2048]{1,0:T(8,128)(2,1)S(1)}, u32[]{:S(2)}) %copy-start.2) | copy-done | bytes 2097176
  22.9 0.0 copy-start.1
  22.9 4.9 %shard_map.67 = f32[8,136,128]{2,1,0:T(8,128)S(1)} custom-call(s32[1]{0:T(128)} %bitcast.4.head_ref, bf16[512,1024]{1,0:T(8,128)(2,1)S(1)} %get-tuple-element.30.q_ref, bf16[2048,512]{1,0:T(8,128)(2,1)S(1)} %get-tuple-element.23.refs_0_.refs_2_, bf16[512,2048]{1,0:T(8,128)(2,1)} %copy-done.2, f32[8,136,128]{2,1,0:T(8,128)S(1)} %shard_map.65.refs_2_), custom_call_target="tpu_custom_call" | custom-call | flops 1073741824 | bytes 557056 | tf_op jit(solution)/shard_map/pallas_call | solution.py:158
  27.8 0.0 copy-done.1
  27.9 0.7 convert_element_type.21
  28.6 2.5 %collective-permute-start.1 = (f16[8,136,128]{2,1,0:T(8,128)(2,1)}, f16[8,136,128]{2,1,0:T(8,128)(2,1)}, u32[]{:S(2)}, u32[]{:S(2)}) collective-permute-start(f16[8,136,128]{2,1,0:T(8,128)(2,1)} %convert_element_type.21), channel_id=1, source_target_pairs={{0,2},{1,3},{2,0},{3,1},{4,6},{5,7},{6,4},{7,5},{8,10},{9,11},{10,... | collective-permute-start | bytes 835592 | tf_op jit(solution)/shard_map/ppermute | solution.py:23
  31.1 0.0 copy-done
  31.1 7.1 %shard_map.68 = f32[8,136,128]{2,1,0:T(8,128)S(1)} custom-call(s32[1]{0:T(128)} %bitcast.5.head_ref, bf16[512,1024]{1,0:T(8,128)(2,1)S(1)} %get-tuple-element.30.q_ref, bf16[2048,512]{1,0:T(8,128)(2,1)S(1)} %get-tuple-element.20.refs_0_, bf16[512,2048]{1,0:T(8,128)(2,1)S(1)} %get-tuple-element.21.refs_1_, bf16[2048,512]{1,0:T(8,128)(2,1)} %copy-done.1, ...), custom_call_target="tpu_custom_call" | custom-call | flops 2147483648 | bytes 557056 | tf_op jit(solution)/shard_map/pallas_call | solution.py:158
  38.2 0.1 collective-permute-start.2
  38.3 0.4 collective-permute-done.1
  38.7 1.0 %convert_element_type.22.refs_4_ = f32[8,136,128]{2,1,0:T(8,128)S(1)} convert(f16[8,136,128]{2,1,0:T(8,128)(2,1)} %collective-permute-done.1) | non-fusion elementwise | flops 139264 | bytes 835584 | tf_op jit(solution)/shard_map/convert_element_type | solution.py:258
  39.7 7.4 %shard_map.69 = f32[8,136,128]{2,1,0:T(8,128)S(1)} custom-call(s32[1]{0:T(128)} %bitcast.6.head_ref, bf16[512,1024]{1,0:T(8,128)(2,1)S(1)} %get-tuple-element.30.q_ref, bf16[2048,512]{1,0:T(8,128)(2,1)S(1)} %get-tuple-element.20.refs_0_, bf16[512,2048]{1,0:T(8,128)(2,1)} %copy-done, bf16[2048,512]{1,0:T(8,128)(2,1)} %copy-done.1, ...), custom_call_target="tpu_custom_call" | custom-call | flops 2147483648 | bytes 557056 | tf_op jit(solution)/shard_map/pallas_call | solution.py:158
  47.2 0.0 collective-permute-done.2
  47.2 1.0 %convert_element_type.25.refs_4_ = f32[8,136,128]{2,1,0:T(8,128)S(1)} convert(f16[8,136,128]{2,1,0:T(8,128)(2,1)} %collective-permute-done.2) | non-fusion elementwise | flops 139264 | bytes 835584 | tf_op jit(solution)/shard_map/convert_element_type | solution.py:258
  48.2 7.2 %shard_map.70 = f32[8,136,128]{2,1,0:T(8,128)S(1)} custom-call(s32[1]{0:T(128)} %bitcast.8.head_ref, bf16[512,1024]{1,0:T(8,128)(2,1)S(1)} %get-tuple-element.30.q_ref, bf16[2048,512]{1,0:T(8,128)(2,1)S(1)} %get-tuple-element.20.refs_0_, bf16[512,2048]{1,0:T(8,128)(2,1)} %copy-done, bf16[2048,512]{1,0:T(8,128)(2,1)} %copy-done.1, ...), custom_call_target="tpu_custom_call" | custom-call | flops 2147483648 | bytes 557056 | tf_op jit(solution)/shard_map/pallas_call | solution.py:158
  55.4 0.1 convert_bitcast_fusion
  55.5 0.1 pad_maximum_fusion
  55.6 0.0 copy-start.3
  55.6 22.0 %all_to_all.5 = f16[8,2,136,128]{3,2,1,0:T(8,128)(2,1)S(1)} all-to-all(f16[8,2,136,128]{3,2,1,0:T(8,128)(2,1)S(1)} %pad_maximum_fusion), channel_id=1, replica_groups=mesh['tm'=8,'patch'=4] {'tm'}, dimensions={0} | all-to-all | bytes 1114112 | tf_op jit(solution)/shard_map/all_to_all | solution.py:261
  77.6 0.1 convert_element_type.27.part_ref
  77.7 0.6 shard_map.71.refs_0_
  78.3 1.5 %collective-permute-start.4 = (f32[256,128]{1,0:T(8,128)S(1)}, f32[256,128]{1,0:T(8,128)S(1)}, u32[]{:S(2)}, u32[]{:S(2)}) collective-permute-start(f32[256,128]{1,0:T(8,128)S(1)} %shard_map.71.refs_0_), channel_id=1, source_target_pairs={{0,2},{1,3},{2,0},{3,1},{4,6},{5,7},{6,4},{7,5},{8,10},{9,11},{10,... | collective-permute-start | bytes 393224 | tf_op jit(solution)/shard_map/ppermute | solution.py:23
  79.8 0.0 collective-permute-start.3
  79.8 3.5 %collective-permute-done.4.refs_2_ = f32[256,128]{1,0:T(8,128)S(1)} collective-permute-done((f32[256,128]{1,0:T(8,128)S(1)}, f32[256,128]{1,0:T(8,128)S(1)}, u32[]{:S(2)}, u32[]{:S(2)}) %collective-permute-start.4) | collective-permute-done | bytes 131104 | tf_op jit(solution)/shard_map/ppermute | solution.py:23
  83.3 0.0 collective-permute-start.5
  83.3 0.0 collective-permute-done.3.refs_1_
  83.3 1.3 %collective-permute-done.5.refs_3_ = f32[256,128]{1,0:T(8,128)S(1)} collective-permute-done((f32[256,128]{1,0:T(8,128)S(1)}, f32[256,128]{1,0:T(8,128)S(1)}, u32[]{:S(2)}, u32[]{:S(2)}) %collective-permute-start.5) | collective-permute-done | bytes 131104 | tf_op jit(solution)/shard_map/ppermute | solution.py:23
  84.7 0.0 copy-done.3
  84.7 1.6 %shard_map.72 = bf16[128,256]{1,0:T(8,128)(2,1)} custom-call(s32[4]{0:T(128)S(1)} %pad_add_fusion.at_ref, f32[256,128]{1,0:T(8,128)S(1)} %shard_map.71.refs_0_, f32[256,128]{1,0:T(8,128)S(1)} %collective-permute-done.3.refs_1_, f32[256,128]{1,0:T(8,128)S(1)} %collective-permute-done.4.refs_2_, f32[256,128]{1,0:T(8,128)S(1)} %collective-permute-done.5.refs_3_, ...), custom_call_target="tpu_custom_call" | custom-call | flops 67108864 | bytes 524288 | tf_op jit(solution)/shard_map/pallas_call | solution.py:220
  (1 shorter events, 0.0 us)
Async XLA Ops:
  0.0 13.5 %collective-permute-start = (bf16[2048,1024]{1,0:T(8,128)(2,1)}, bf16[2048,1024]{1,0:T(8,128)(2,1)}, u32[]{:S(2)}, u32[]{:S(2)}) collective-permute-start(bf16[2048,1024]{1,0:T(8,128)(2,1)} %t_ref.1), channel_id=1, source_target_pairs={{0,1},{1,0},{2,3},{3,2},{4,5},{5,4},{6,7},{7,6},{8,9},{9,8},{10,11... | collective-permute-start | bytes 12582920 | tf_op jit(solution)/shard_map/ppermute | solution.py:23
  10.2 20.9 %copy-start = (bf16[512,2048]{1,0:T(8,128)(2,1)}, bf16[512,2048]{1,0:T(8,128)(2,1)S(1)}, u32[]{:S(2)}) copy-start(bf16[512,2048]{1,0:T(8,128)(2,1)S(1)} %get-tuple-element.21.refs_1_) | copy-start | bytes 6291460
  21.6 1.3 %copy-start.2 = (bf16[512,2048]{1,0:T(8,128)(2,1)}, bf16[512,2048]{1,0:T(8,128)(2,1)S(1)}, u32[]{:S(2)}) copy-start(bf16[512,2048]{1,0:T(8,128)(2,1)S(1)} %get-tuple-element.24.refs_1_.refs_3_) | copy-start | bytes 6291460
  22.9 5.0 %copy-start.1 = (bf16[2048,512]{1,0:T(8,128)(2,1)}, bf16[2048,512]{1,0:T(8,128)(2,1)S(1)}, u32[]{:S(2)}) copy-start(bf16[2048,512]{1,0:T(8,128)(2,1)S(1)} %get-tuple-element.23.refs_0_.refs_2_) | copy-start | bytes 6291460
  28.6 10.1 %collective-permute-start.1 = (f16[8,136,128]{2,1,0:T(8,128)(2,1)}, f16[8,136,128]{2,1,0:T(8,128)(2,1)}, u32[]{:S(2)}, u32[]{:S(2)}) collective-permute-start(f16[8,136,128]{2,1,0:T(8,128)(2,1)} %convert_element_type.21), channel_id=1, source_target_pairs={{0,2},{1,3},{2,0},{3,1},{4,6},{5,7},{6,4},{7,5},{8,10},{9,11},{10,... | collective-permute-start | bytes 835592 | tf_op jit(solution)/shard_map/ppermute | solution.py:23
  38.2 9.0 %collective-permute-start.2 = (f16[8,136,128]{2,1,0:T(8,128)(2,1)S(1)}, f16[8,136,128]{2,1,0:T(8,128)(2,1)}, u32[]{:S(2)}, u32[]{:S(2)}) collective-permute-start(f16[8,136,128]{2,1,0:T(8,128)(2,1)S(1)} %convert_element_type.24), channel_id=1, source_target_pairs={{0,2},{1,3},{2,0},{3,1},{4,6},{5,7},{6,4},{7,5},{8,10},{9,11},{10,... | collective-permute-start | bytes 835592 | tf_op jit(solution)/shard_map/ppermute | solution.py:23
  55.6 29.1 %copy-start.3 = (bf16[1024,256]{1,0:T(8,128)(2,1)S(1)}, bf16[1024,256]{1,0:T(8,128)(2,1)}, u32[]{:S(2)}) copy-start(bf16[1024,256]{1,0:T(8,128)(2,1)} %refs_4_.1) | copy-start | bytes 1572868
  78.3 5.0 %collective-permute-start.4 = (f32[256,128]{1,0:T(8,128)S(1)}, f32[256,128]{1,0:T(8,128)S(1)}, u32[]{:S(2)}, u32[]{:S(2)}) collective-permute-start(f32[256,128]{1,0:T(8,128)S(1)} %shard_map.71.refs_0_), channel_id=1, source_target_pairs={{0,2},{1,3},{2,0},{3,1},{4,6},{5,7},{6,4},{7,5},{8,10},{9,11},{10,... | collective-permute-start | bytes 393224 | tf_op jit(solution)/shard_map/ppermute | solution.py:23
  79.8 3.5 %collective-permute-start.3 = (f32[256,128]{1,0:T(8,128)S(1)}, f32[256,128]{1,0:T(8,128)S(1)}, u32[]{:S(2)}, u32[]{:S(2)}) collective-permute-start(f32[256,128]{1,0:T(8,128)S(1)} %shard_map.71.refs_0_), channel_id=1, source_target_pairs={{0,1},{1,0},{2,3},{3,2},{4,5},{5,4},{6,7},{7,6},{8,9},{9,8},{10,11... | collective-permute-start | bytes 393224 | tf_op jit(solution)/shard_map/ppermute | solution.py:23
  83.3 1.3 %collective-permute-start.5 = (f32[256,128]{1,0:T(8,128)S(1)}, f32[256,128]{1,0:T(8,128)S(1)}, u32[]{:S(2)}, u32[]{:S(2)}) collective-permute-start(f32[256,128]{1,0:T(8,128)S(1)} %collective-permute-done.4.refs_2_), channel_id=1, source_target_pairs={{0,1},{1,0},{2,3},{3,2},{4,5},{5,4},{6,7},{7,6},{8,9},{9,8},{10,11... | collective-permute-start | bytes 393224 | tf_op jit(solution)/shard_map/ppermute | solution.py:23

commit v3 on v2

v3 whole, which is shorter than its diff:
```python
import functools
import math

import jax
import jax.numpy as jnp
from jax import lax
from jax.experimental import pallas as pl
from jax.experimental.pallas import tpu as pltpu
from jax.sharding import PartitionSpec as P

H = 8
CORES = 2
NEAR = 2
AXES = ("tm", "patch")
VMEM = pl.BlockSpec(memory_space=pltpu.VMEM)
HBM = pl.BlockSpec(memory_space=pltpu.HBM)
SMEM = pl.BlockSpec(memory_space=pltpu.SMEM)
PARAMS = pltpu.CompilerParams(vmem_limit_bytes=24 * 2**20)
EXTRA = 8
LEVELS = 30.0 * 2.0**10
UNITS = (2.0**20, 2.0**10, 1.0, 2.0**-10, 2.0**-20)


def xor_permute(value, n, step):
    return lax.ppermute(value, AXES, [(i, i ^ step) for i in range(n)])


def dot(a, w):
    return jnp.dot(a, w, preferred_element_type=jnp.float32).astype(jnp.bfloat16)


def project_own_kernel(at_ref, t_hbm, l_hbm, wq_hbm, wk_hbm, wv_hbm, k_ref, v_ref, q_ref, wk_ref, wv_ref, wq_ref, t_ref, l_ref, sems):
    near, core = at_ref[1], at_ref[3]
    chunks, rows, _ = t_ref.shape
    cols = k_ref.shape[1]
    half = l_ref.shape[1] * l_ref.shape[2]
    columns = pl.ds(pl.multiple_of(core * cols, cols), cols)
    moves = [(wk_hbm.at[:, columns], wk_ref), (t_hbm.at[0], t_ref.at[0]), (wv_hbm.at[:, columns], wv_ref)]
    moves += [(t_hbm.at[c], t_ref.at[c]) for c in range(1, chunks)]
    moves += [(wq_hbm.at[:, columns], wq_ref), (l_hbm.at[:, near ^ 1], l_ref.at[0]), (l_hbm.at[:, near], l_ref.at[1])]
    copies = [pltpu.make_async_copy(src, dst, sems.at[i]) for i, (src, dst) in enumerate(moves)]
    for copy in copies:
        copy.start()
    for c in range(chunks):
        part = slice(c * rows, (c + 1) * rows)
        for copy in copies[:2] if c == 0 else [copies[c + 2]]:
            copy.wait()
        k_ref[part, :] = dot(t_ref[c], wk_ref[...])
        if c == 0:
            copies[2].wait()
        v_ref[:, part] = dot(t_ref[c], wv_ref[...]).T
    copies[chunks + 2].wait()
    for h in range(NEAR):
        copies[chunks + 3 + h].wait()
        q_ref[:, h * half : (h + 1) * half] = dot(l_ref[h].reshape(half, -1), wq_ref[...]).T


def project_own(at, tokens, latents, w_query, w_key, w_value, chunks=4):
    (n, d), cols = tokens.shape, w_key.shape[1] // CORES
    n_far, _, block, _ = latents.shape
    m = n_far * NEAR * block
    return pl.pallas_call(
        project_own_kernel,
        out_shape=[jax.ShapeDtypeStruct(s, jnp.bfloat16) for s in ((n, cols), (cols, n), (cols, m), (d, cols), (d, cols))],
        in_specs=[SMEM] + [HBM] * 5,
        out_specs=[VMEM] * 5,
        scratch_shapes=[
            pltpu.VMEM((d, cols), jnp.bfloat16),
            pltpu.VMEM((chunks, n // chunks, d), jnp.bfloat16),
            pltpu.VMEM((NEAR, n_far, block, d), jnp.bfloat16),
            pltpu.SemaphoreType.DMA((chunks + 5,)),
        ],
        compiler_params=pltpu.CompilerParams(vmem_limit_bytes=46 * 2**20),
        cost_estimate=pl.CostEstimate(
            flops=(4 * n + 2 * m) * d * cols, bytes_accessed=2 * (n * d + m * d + 3 * d * cols), transcendentals=0
        ),
    )(at, tokens.reshape(chunks, n // chunks, d), latents, w_query, w_key, w_value)


def project_kernel(chunks, t_ref, wk_ref, wv_ref, k_ref, v_ref):
    rows = t_ref.shape[0] // chunks
    for c in range(chunks):
        part = slice(c * rows, (c + 1) * rows)
        k_ref[part, :] = dot(t_ref[part, :], wk_ref[...])
        v_ref[:, part] = dot(t_ref[part, :], wv_ref[...]).T


def project(tokens, w_key, w_value, chunks=4):
    (n, d), cols = tokens.shape, w_key.shape[1]
    return pl.pallas_call(
        functools.partial(project_kernel, chunks),
        out_shape=[jax.ShapeDtypeStruct(s, jnp.bfloat16) for s in ((n, cols), (cols, n))],
        in_specs=[VMEM] * 3,
        out_specs=[VMEM] * 2,
        compiler_params=PARAMS,
        cost_estimate=pl.CostEstimate(flops=4 * n * d * cols, bytes_accessed=2 * (n * d + 2 * d * cols), transcendentals=0),
    )(tokens, w_key, w_value)


def merge(parts):
    peak = functools.reduce(jnp.maximum, [p for _, _, p in parts])
    factors = [jnp.exp2(p - peak) for _, _, p in parts]
    num, den = (
        functools.reduce(lambda a, b: a + b, [part[i] * f for part, f in zip(parts, factors)]) for i in range(2)
    )
    return num, den, peak


def nearest(value):
    return jnp.floor(value + 0.5)


def spread(value):
    place = nearest(jnp.abs(value) * LEVELS) * 2.0**-10
    power = jnp.floor(place)
    return jnp.where(value < 0, -1.0, 1.0) * (1.0 + place - power) * jnp.exp2(power - 14.0)


def gather_up(value):
    size = jnp.abs(value)
    power = jnp.clip(jnp.floor(jnp.log2(size)), -14.0, 15.0)
    return jnp.where(value < 0, -1.0, 1.0) * (power + 13.0 + size * jnp.exp2(-power)) * (2.0**10 / LEVELS)


def encode(part):
    num, den, peak = part
    mean = num / den
    most = jnp.max(jnp.abs(mean), axis=0, keepdims=True)
    exponent = jnp.ceil(jnp.log2(jnp.clip(most, 2.0**-100, 2.0**100)) + 2.0**-10)
    rest, digits = peak + jnp.log2(den), [exponent]
    for unit in UNITS[:-1]:
        digits.append(nearest(rest * (1.0 / unit)))
        rest = rest - digits[-1] * unit
    digits.append(rest * (1.0 / UNITS[-1]))
    row = lax.broadcasted_iota(jnp.int32, (EXTRA, mean.shape[1]), 0)
    tail = jnp.zeros((EXTRA, mean.shape[1]), jnp.float32)
    for i, digit in enumerate(digits):
        tail = jnp.where(row == i, digit, tail)
    return jnp.concatenate([spread(mean * jnp.exp2(-exponent)), tail], axis=0)


def decode(rows):
    feats = rows.shape[0] - EXTRA
    exponent, *digits = (rows[feats + i : feats + i + 1] for i in range(len(UNITS) + 1))
    peak = functools.reduce(lambda a, b: a + b, [d * u for d, u in zip(reversed(digits), reversed(UNITS))])
    return gather_up(rows[:feats]) * jnp.exp2(exponent), jnp.ones_like(peak), peak


def unpack(rows):
    feats = rows.shape[0] - EXTRA
    return rows[:feats], rows[feats : feats + 1], rows[feats + 1 : feats + 2]


def attend_kernel(chunk, half, blocks, encoded, at_ref, q_ref, *refs):
    kv, got, (o_ref, s0, s1) = refs[: 2 * blocks], refs[2 * blocks : -3], refs[-3:]
    tokens, lanes = s0.shape
    heads, n_far, rows, block = o_ref.shape
    size = rows - EXTRA
    coef = math.log2(math.e) / math.sqrt(size)
    slots = (s0, s1)
    ones = jnp.ones((16, chunk), jnp.bfloat16)
    row = lax.broadcasted_iota(jnp.int32, (EXTRA, lanes), 0)
    items = [(j, b) for j in range(heads) for b in range(blocks)]

    def columns(j):
        return pl.ds(pl.multiple_of((at_ref[0] * heads + j) * size, size), size)

    peak, done = None, []
    for i in range(len(items) + 1):
        now, before = slots[i % 2], slots[(i - 1) % 2]
        acc, top = jnp.zeros((size + 16, lanes), jnp.float32), None
        for c in range(tokens // chunk):
            part = slice(c * chunk, (c + 1) * chunk)
            if i < len(items):
                j, b = items[i]
                q = q_ref[columns(j), half * lanes : (half + 1) * lanes]
                s = jnp.dot(kv[2 * b][part, columns(j)], q, preferred_element_type=jnp.float32)
                now[part, :] = s
                high = jnp.max(s.reshape(chunk // 8, 8, lanes), axis=0)
                top = high if top is None else jnp.maximum(top, high)
            if i > 0:
                j, b = items[i - 1]
                w = jnp.exp2((before[part, :] - peak) * coef).astype(jnp.bfloat16)
                v = jnp.concatenate([kv[2 * b + 1][columns(j), part], ones], axis=0)
                acc = acc + jnp.dot(v, w, preferred_element_type=jnp.float32)
        if i > 0:
            j = items[i - 1][0]
            done.append((acc[:size], acc[size : size + 1], peak * coef))
            if len(done) == blocks:
                for f in range(n_far):
                    at = slice(f * block, (f + 1) * block)
                    part = merge([tuple(v[:, at] for v in d) for d in done] + [unpack(g[j, f]) for g in got])
                    if encoded:
                        o_ref[j, f] = encode(part)
                    else:
                        num, den, high = part
                        o_ref[j, f, :size] = num
                        o_ref[j, f, size:] = jnp.where(row[:, at] == 0, den, high)
                done = []
        if i < len(items):
            peak = jnp.max(top, axis=0, keepdims=True)


def attend(group, half, query_t, blocks, got, shape, encoded, chunk=1024):
    heads, n_far, rows, block = shape
    lanes, tokens = n_far * block, blocks[0][0].shape[0]
    return pl.pallas_call(
        functools.partial(attend_kernel, chunk, half, len(blocks), encoded),
        out_shape=jax.ShapeDtypeStruct(shape, jnp.float32),
        in_specs=[SMEM] + [VMEM] * (1 + 2 * len(blocks) + len(got)),
        out_specs=VMEM,
        scratch_shapes=[pltpu.VMEM((tokens, lanes), jnp.float32)] * 2,
        compiler_params=PARAMS,
        cost_estimate=pl.CostEstimate(
            flops=4 * tokens * lanes * (rows - EXTRA) * heads * len(blocks),
            bytes_accessed=4 * math.prod(shape),
            transcendentals=tokens * lanes * heads * len(blocks),
        ),
    )(group.astype(jnp.int32).reshape(1), query_t, *[a for pair in blocks for a in pair], *got)


def combine_kernel(far_first, own_ref, *refs):
    got, out = refs[:-1], refs[-1]
    heads, n_far = own_ref.shape[:2]
    for j in range(heads):
        for f in range(n_far):
            part = encode(merge([unpack(own_ref[j, f])] + [decode(g[j, f]) for g in got]))
            if far_first:
                out[f, j] = part
            else:
                out[j, f] = part


def combine(own, got, far_first):
    heads, n_far, rows, block = own.shape
    shape = (n_far, heads, rows, block) if far_first else own.shape
    return pl.pallas_call(
        functools.partial(combine_kernel, far_first),
        out_shape=jax.ShapeDtypeStruct(shape, jnp.float32),
        in_specs=[VMEM] * (1 + len(got)),
        out_specs=VMEM,
        compiler_params=PARAMS,
        cost_estimate=pl.CostEstimate(flops=own.size * 20, bytes_accessed=own.size * 12, transcendentals=0),
    )(own, *got)


def attended_kernel(part_ref, out):
    n_tm, heads, rows, _ = part_ref.shape
    feats = rows - EXTRA
    for i in range(heads):
        num, den, _ = merge([decode(part_ref[t, i]) for t in range(n_tm)])
        out[i * feats : (i + 1) * feats, :] = num / den


def attended(parts):
    n_tm, heads, rows, block = parts.shape
    return pl.pallas_call(
        attended_kernel,
        out_shape=jax.ShapeDtypeStruct(((rows - EXTRA) * heads, block), jnp.float32),
        in_specs=[VMEM],
        out_specs=VMEM,
        compiler_params=PARAMS,
        cost_estimate=pl.CostEstimate(flops=parts.size * 4, bytes_accessed=parts.size * 4, transcendentals=0),
    )(parts)


def finish_kernel(at_ref, *refs):
    pieces, (w_ref, o_ref, normed) = refs[:-3], refs[-3:]
    feats, me = pieces[0].shape[0], at_ref[2]
    width = feats * len(pieces)
    squares = functools.reduce(lambda a, b: a + b, [jnp.square(p[...]) for p in pieces])
    scale = lax.rsqrt(jnp.sum(squares, axis=0, keepdims=True) * (1.0 / width) + 1e-06)
    for s, piece in enumerate(pieces):
        owner = me ^ s
        at = owner % CORES * (width // CORES) + owner // CORES * feats
        normed[pl.ds(pl.multiple_of(at, feats), feats), :] = (piece[...] * scale).astype(jnp.bfloat16)
    o_ref[...] = lax.dot_general(
        normed[...], w_ref[...], (((0,), (0,)), ((), ())), preferred_element_type=jnp.float32
    ).astype(jnp.bfloat16)


def finish(at, pieces, w_out):
    block = pieces[0].shape[1]
    return pl.pallas_call(
        finish_kernel,
        out_shape=jax.ShapeDtypeStruct((block, w_out.shape[1]), jnp.bfloat16),
        in_specs=[SMEM] + [VMEM] * (len(pieces) + 1),
        out_specs=VMEM,
        scratch_shapes=[pltpu.VMEM((w_out.shape[0], block), jnp.bfloat16)],
        compiler_params=PARAMS,
        cost_estimate=pl.CostEstimate(flops=2 * block * w_out.size, bytes_accessed=2 * w_out.size, transcendentals=0),
    )(at, *pieces, w_out)


def narrow(part):
    return part.astype(jnp.float16)


def wide(part):
    return part.astype(jnp.float32)


def per_device(n_tm, n_patch, latents, tokens, w_query, w_key, w_value, w_out):
    n, n_x, n_far = n_tm * n_patch, n_patch // CORES, n_tm // NEAR
    tm, patch = lax.axis_index("tm"), lax.axis_index("patch")
    x, core = patch // CORES, patch % CORES
    at = jnp.stack([x, tm % NEAR, patch, core]).astype(jnp.int32)
    heads = H // n_patch
    block, d = latents.shape[0] // n_tm, latents.shape[1]
    shape = (heads, n_far, d // H + EXTRA, block)

    sibling = xor_permute(tokens, n, 1)
    latents = latents.reshape(n_far, NEAR, block, d)
    keys, vals_t, query_t, own_key, own_value = project_own(at, tokens, latents, w_query, w_key, w_value)
    near = [(keys, vals_t)]
    both = None
    got = [[], []]
    for s in range(n_x - 1, -1, -1):
        group = x ^ s
        for half in range(2):
            if both is None:
                part = attend(group, half, query_t, near, [], shape, False)
                sibling, part = lax.optimization_barrier((sibling, part))
                far = [tuple(project(sibling, own_key, own_value))]
                both = near + far
                part = attend(group, half, query_t, far, [part], shape, True)
            else:
                part = attend(group, half, query_t, both, [], shape, s > 0)
            query_t, part = lax.optimization_barrier((query_t, part))
            if s:
                got[half].append(wide(xor_permute(narrow(part), n, CORES * s)))
            elif half == 0:
                part = combine(part, got[0], False)
                got[1].append(wide(xor_permute(narrow(part), n, n_patch)))
            else:
                part = combine(part, got[1], True)
    groups = [[f * NEAR + k for f in range(n_far)] for k in range(NEAR)]
    part = wide(lax.all_to_all(narrow(part), "tm", 0, 0, axis_index_groups=groups, tiled=True))
    pieces = [attended(part)]
    pieces += [xor_permute(pieces[0], n, CORES * s) for s in range(1, n_x)]
    pieces = [p for piece in pieces for p in (piece, xor_permute(piece, n, 1))]
    return finish(at, pieces, w_out)


def solution(mesh):
    return jax.shard_map(
        functools.partial(per_device, mesh.shape["tm"], mesh.shape["patch"]),
        mesh=mesh,
        in_specs=(P(), P(("tm", "patch"), None), P(), P(), P(), P(None, "patch")),
        out_specs=P("tm", "patch"),
        check_vma=False,
    )
```

time: 86.6 us -> 69.6 us (0.80)
  blocking collectives: 22 us -> 13.4 us
  Pallas kernels: 49.8 us -> 42.9 us
  other arithmetic: 3.15 us -> 0.39 us
  starting transfers between devices: 4.56 us -> 6.78 us
  local copies, waits for them, and re-layouts: 1.32 us -> 0.01 us
    all_to_all x1, blocking collectives: 22 us -> 13.4 us  [per_device(): lax.all_to_all(narrow(part), 'tm', 0, 0, axis_index_groups=groups, tiled=...]
    pallas_call x7 -> x9, Pallas kernels: 47.6 us -> 41.1 us  [the longest x5 23.2 us: attend(): pl.pallas_call(functools.partial(attend_kernel, chunk, half, len(blocks),...]
    convert_element_type x5 -> x8, other arithmetic: 2.85 us -> 0.31 us  [the longest x4 0.16 us: narrow(): return part.astype(jnp.float16)]
    ppermute x6 -> x7, starting transfers between devices: 4.56 us -> 6.78 us  [xor_permute(): return lax.ppermute(value, AXES, [(i, i ^ step) for i in range(n)])]
    unnamed x8 -> x2, local copies, waits for them, and re-layouts: 1.32 us -> 0.01 us
    ppermute x6 -> x7, waiting for transfers between devices: 5.3 us -> 5.77 us  [xor_permute(): return lax.ppermute(value, AXES, [(i, i ^ step) for i in range(n)])]
  transfers between devices with their start and end apart: 6 -> 7, of which waited for: 3 -> 3; matrix products, arithmetic and copies ran while one was open for 1% -> 0% of each run, Pallas kernels for 32% -> 43%
where the time goes in v3:
time: 69.6 us; the launch traced here: 69.4 us
  Pallas kernels  42.9 us (62%)
  blocking collectives  13.4 us (19%)
  starting transfers between devices  6.78 us (10%)
  waiting for transfers between devices  5.77 us (8%)
    pallas_call x5, Pallas kernels, attend(): pl.pallas_call(functools.partial(attend_kernel, chunk, half, len(blocks),...  23.2 us
    all_to_all x1, blocking collectives, per_device(): lax.all_to_all(narrow(part), 'tm', 0, 0, axis_index_groups=groups, tiled=...  13.4 us
    pallas_call x1, Pallas kernels, project_own(): pl.pallas_call(project_own_kernel, out_shape=[jax.ShapeDtypeStruct(s, jnp...  9.32 us
    pallas_call x1, Pallas kernels, project(): pl.pallas_call(functools.partial(project_kernel, chunks), out_shape=[jax....  6.85 us
    ppermute x7, starting transfers between devices, xor_permute(): return lax.ppermute(value, AXES, [(i, i ^ step) for i in range(n)])  6.78 us
    ppermute x7, waiting for transfers between devices, xor_permute(): return lax.ppermute(value, AXES, [(i, i ^ step) for i in range(n)])  5.77 us
    pallas_call x2, Pallas kernels, combine(): pl.pallas_call(functools.partial(combine_kernel, far_first), out_shape=ja...  1.73 us
    pallas_call x1, Pallas kernels, finish(): pl.pallas_call(finish_kernel, out_shape=jax.ShapeDtypeStruct((block, w_ou...  1.55 us
  transfers between devices with their start and end apart: 7, of which 3 were waited for; matrix products, arithmetic and copies ran while one was open for 0% of the time, Pallas kernels for 43%

profile of v3, /device:TPU:0, one launch (start us, length us, event | category | flops | bytes accessed | tf_op | source)
XLA Modules:
  0.0 69.4 jit_solution(9396506206642271966)
XLA Ops:
  0.0 0.5 collective-permute-start
  0.5 0.1 pad_add_fusion.at_ref
  0.5 9.3 %shard_map.64 = (bf16[2048,512]{1,0:T(8,128)(2,1)S(1)}, bf16[512,2048]{1,0:T(8,128)(2,1)S(1)}, bf16[512,1024]{1,0:T(8,128)(2,1)S(1)}, bf16[1024,512]{1,0:T(8,128)(2,1)S(1)}, bf16[1024,512]{1,0:T(8,128)(2,1)S(1)}) custom-call(s32[4]{0:T(128)S(1)} %pad_add_fusion.at_ref, bf16[4,512,1024]{2,1,0:T(8,128)(2,1)} %bitcast.7, bf16[4,2,128,1024]{3,2,1,0:T(8,128)(2,1)} %bitcast.8, ...), custom_call_target="tpu_custom_call" | custom-call | flops 5368709120 | bytes 9437184 | tf_op jit(solution)/shard_map/pallas_call | solution.py:62
  9.9 2.8 %shard_map.65.refs_2_ = f32[2,4,136,128]{3,2,1,0:T(8,128)S(1)} custom-call(s32[1]{0:T(128)} %bitcast.6.at_ref, bf16[512,1024]{1,0:T(8,128)(2,1)S(1)} %get-tuple-element.32.q_ref, bf16[2048,512]{1,0:T(8,128)(2,1)S(1)} %get-tuple-element.22.refs_0_, bf16[512,2048]{1,0:T(8,128)(2,1)S(1)} %get-tuple-element.23.refs_1_), custom_call_target="tpu_custom_call" | custom-call | flops 1073741824 | bytes 557056 | tf_op jit(solution)/shard_map/pallas_call | solution.py:207
  12.7 0.0 collective-permute-done.t_ref
  12.7 6.8 %shard_map.66 = (bf16[2048,512]{1,0:T(8,128)(2,1)S(1)}, bf16[512,2048]{1,0:T(8,128)(2,1)S(1)}) custom-call(bf16[2048,1024]{1,0:T(8,128)(2,1)} %collective-permute-done.t_ref, bf16[1024,512]{1,0:T(8,128)(2,1)S(1)} %get-tuple-element.25.wk_ref, bf16[1024,512]{1,0:T(8,128)(2,1)S(1)} %get-tuple-element.26.wv_ref), custom_call_target="tpu_custom_call" | custom-call | flops 4294967296 | bytes 6291456 | tf_op jit(solution)/shard_map/pallas_call | solution.py:90
  19.5 3.4 %shard_map.67 = f32[2,4,136,128]{3,2,1,0:T(8,128)S(1)} custom-call(s32[1]{0:T(128)} %bitcast.6.at_ref, bf16[512,1024]{1,0:T(8,128)(2,1)S(1)} %get-tuple-element.32.q_ref, bf16[2048,512]{1,0:T(8,128)(2,1)S(1)} %get-tuple-element.27.refs_0_.refs_2_, bf16[512,2048]{1,0:T(8,128)(2,1)S(1)} %get-tuple-element.28.refs_1_.refs_3_, ...), custom_call_target="tpu_custom_call" | custom-call | flops 1073741824 | bytes 557056 | tf_op jit(solution)/shard_map/pallas_call | solution.py:207
  23.0 2.6 %collective-permute-start.2 = (f16[2,4,136,128]{3,2,1,0:T(8,128)(2,1)S(1)}, f16[2,4,136,128]{3,2,1,0:T(8,128)(2,1)S(1)}, u32[]{:S(2)}, u32[]{:S(2)}) collective-permute-start(f16[2,4,136,128]{3,2,1,0:T(8,128)(2,1)S(1)} %convert_element_type.26), channel_id=1, source_target_pairs={{0,2},{1,3},{2,0},{3,1},{4,6},{5,7},{6,4},{7,5},{8,10},{9,11},{10,... | collective-permute-start | bytes 835592 | tf_op jit(solution)/shard_map/ppermute | solution.py:25
  25.6 5.8 %shard_map.68 = f32[2,4,136,128]{3,2,1,0:T(8,128)S(1)} custom-call(s32[1]{0:T(128)} %bitcast.6.at_ref, bf16[512,1024]{1,0:T(8,128)(2,1)S(1)} %get-tuple-element.32.q_ref, bf16[2048,512]{1,0:T(8,128)(2,1)S(1)} %get-tuple-element.22.refs_0_, bf16[512,2048]{1,0:T(8,128)(2,1)S(1)} %get-tuple-element.23.refs_1_, ...), custom_call_target="tpu_custom_call" | custom-call | flops 2147483648 | bytes 557056 | tf_op jit(solution)/shard_map/pallas_call | solution.py:207
  31.4 0.1 collective-permute-start.1
  31.5 5.5 %shard_map.69.own_ref = f32[2,4,136,128]{3,2,1,0:T(8,128)S(1)} custom-call(s32[1]{0:T(128)} %bitcast.at_ref, bf16[512,1024]{1,0:T(8,128)(2,1)S(1)} %get-tuple-element.32.q_ref, bf16[2048,512]{1,0:T(8,128)(2,1)S(1)} %get-tuple-element.22.refs_0_, bf16[512,2048]{1,0:T(8,128)(2,1)S(1)} %get-tuple-element.23.refs_1_, ...), custom_call_target="tpu_custom_call" | custom-call | flops 2147483648 | bytes 557056 | tf_op jit(solution)/shard_map/pallas_call | solution.py:207
  37.0 0.0 collective-permute-done.2
  37.0 0.7 %shard_map.71 = f32[2,4,136,128]{3,2,1,0:T(8,128)S(1)} custom-call(f32[2,4,136,128]{3,2,1,0:T(8,128)S(1)} %shard_map.69.own_ref, f32[2,4,136,128]{3,2,1,0:T(8,128)S(1)} %convert_element_type.27.refs_0_), custom_call_target="tpu_custom_call" | custom-call | flops 2785280 | bytes 1671168 | tf_op jit(solution)/shard_map/pallas_call | solution.py:237
  37.8 2.1 %collective-permute-start.3 = (f16[2,4,136,128]{3,2,1,0:T(8,128)(2,1)S(1)}, f16[2,4,136,128]{3,2,1,0:T(8,128)(2,1)S(1)}, u32[]{:S(2)}, u32[]{:S(2)}) collective-permute-start(f16[2,4,136,128]{3,2,1,0:T(8,128)(2,1)S(1)} %convert_element_type.28), channel_id=1, source_target_pairs={{0,4},{1,5},{2,6},{3,7},{4,0},{5,1},{6,2},{7,3},{8,12},{9,13},{10,... | collective-permute-start | bytes 835592 | tf_op jit(solution)/shard_map/ppermute | solution.py:25
  39.9 5.7 %shard_map.70.own_ref = f32[2,4,136,128]{3,2,1,0:T(8,128)S(1)} custom-call(s32[1]{0:T(128)} %bitcast.at_ref, bf16[512,1024]{1,0:T(8,128)(2,1)S(1)} %get-tuple-element.32.q_ref, bf16[2048,512]{1,0:T(8,128)(2,1)S(1)} %get-tuple-element.22.refs_0_, bf16[512,2048]{1,0:T(8,128)(2,1)S(1)} %get-tuple-element.23.refs_1_, ...), custom_call_target="tpu_custom_call" | custom-call | flops 2147483648 | bytes 557056 | tf_op jit(solution)/shard_map/pallas_call | solution.py:207
  45.6 0.0 collective-permute-done.1
  45.6 1.0 %collective-permute-done.3 = f16[2,4,136,128]{3,2,1,0:T(8,128)(2,1)S(1)} collective-permute-done((f16[2,4,136,128]{3,2,1,0:T(8,128)(2,1)S(1)}, f16[2,4,136,128]{3,2,1,0:T(8,128)(2,1)S(1)}, u32[]{:S(2)}, u32[]{:S(2)}) %collective-permute-start.3) | collective-permute-done | bytes 278560 | tf_op jit(solution)/shard_map/ppermute | solution.py:25
  46.7 0.0 copy-start
  46.7 1.0 %shard_map.72 = f32[4,2,136,128]{3,2,1,0:T(8,128)S(1)} custom-call(f32[2,4,136,128]{3,2,1,0:T(8,128)S(1)} %shard_map.70.own_ref, f32[2,4,136,128]{3,2,1,0:T(8,128)S(1)} %convert_element_type.25.refs_0_, f32[2,4,136,128]{3,2,1,0:T(8,128)S(1)} %convert_element_type.29.refs_1_), custom_call_target="tpu_custom_call" | custom-call | flops 2785280 | bytes 1671168 | tf_op jit(solution)/shard_map/pallas_call | solution.py:237
  47.8 13.4 %all_to_all.5 = f16[4,2,136,128]{3,2,1,0:T(8,128)(2,1)S(1)} all-to-all(f16[4,2,136,128]{3,2,1,0:T(8,128)(2,1)S(1)} %convert_element_type.30), channel_id=1, replica_groups={{0,8,16,24},{4,12,20,28},{1,9,17,25},{5,13,21,29},{2,10,18,26},{6,14,22..., dimensions={0} | all-to-all | bytes 557056 | tf_op jit(solution)/shard_map/all_to_all | solution.py:338
  61.2 0.3 shard_map.73.refs_0_
  61.5 1.6 %collective-permute-start.5 = (f32[256,128]{1,0:T(8,128)S(1)}, f32[256,128]{1,0:T(8,128)S(1)}, u32[]{:S(2)}, u32[]{:S(2)}) collective-permute-start(f32[256,128]{1,0:T(8,128)S(1)} %shard_map.73.refs_0_), channel_id=1, source_target_pairs={{0,2},{1,3},{2,0},{3,1},{4,6},{5,7},{6,4},{7,5},{8,10},{9,11},{10,... | collective-permute-start | bytes 393224 | tf_op jit(solution)/shard_map/ppermute | solution.py:25
  63.1 0.0 collective-permute-start.4
  63.1 3.4 %collective-permute-done.5.refs_2_ = f32[256,128]{1,0:T(8,128)S(1)} collective-permute-done((f32[256,128]{1,0:T(8,128)S(1)}, f32[256,128]{1,0:T(8,128)S(1)}, u32[]{:S(2)}, u32[]{:S(2)}) %collective-permute-start.5) | collective-permute-done | bytes 131104 | tf_op jit(solution)/shard_map/ppermute | solution.py:25
  66.5 0.0 collective-permute-start.6
  66.5 0.0 collective-permute-done.4.refs_1_
  66.5 1.3 %collective-permute-done.6.refs_3_ = f32[256,128]{1,0:T(8,128)S(1)} collective-permute-done((f32[256,128]{1,0:T(8,128)S(1)}, f32[256,128]{1,0:T(8,128)S(1)}, u32[]{:S(2)}, u32[]{:S(2)}) %collective-permute-start.6) | collective-permute-done | bytes 131104 | tf_op jit(solution)/shard_map/ppermute | solution.py:25
  67.9 0.0 copy-done
  67.9 1.6 %shard_map.74 = bf16[128,256]{1,0:T(8,128)(2,1)} custom-call(s32[4]{0:T(128)S(1)} %pad_add_fusion.at_ref, f32[256,128]{1,0:T(8,128)S(1)} %shard_map.73.refs_0_, f32[256,128]{1,0:T(8,128)S(1)} %collective-permute-done.4.refs_1_, f32[256,128]{1,0:T(8,128)S(1)} %collective-permute-done.5.refs_2_, f32[256,128]{1,0:T(8,128)S(1)} %collective-permute-done.6.refs_3_, ...), custom_call_target="tpu_custom_call" | custom-call | flops 67108864 | bytes 524288 | tf_op jit(solution)/shard_map/pallas_call | solution.py:284
  (8 shorter events, 0.3 us)
Async XLA Ops:
  0.0 12.7 %collective-permute-start = (bf16[2048,1024]{1,0:T(8,128)(2,1)}, bf16[2048,1024]{1,0:T(8,128)(2,1)}, u32[]{:S(2)}, u32[]{:S(2)}) collective-permute-start(bf16[2048,1024]{1,0:T(8,128)(2,1)} %param.7), channel_id=1, source_target_pairs={{0,1},{1,0},{2,3},{3,2},{4,5},{5,4},{6,7},{7,6},{8,9},{9,8},{10,11... | collective-permute-start | bytes 12582920 | tf_op jit(solution)/shard_map/ppermute | solution.py:25
  23.0 14.0 %collective-permute-start.2 = (f16[2,4,136,128]{3,2,1,0:T(8,128)(2,1)S(1)}, f16[2,4,136,128]{3,2,1,0:T(8,128)(2,1)S(1)}, u32[]{:S(2)}, u32[]{:S(2)}) collective-permute-start(f16[2,4,136,128]{3,2,1,0:T(8,128)(2,1)S(1)} %convert_element_type.26), channel_id=1, source_target_pairs={{0,2},{1,3},{2,0},{3,1},{4,6},{5,7},{6,4},{7,5},{8,10},{9,11},{10,... | collective-permute-start | bytes 835592 | tf_op jit(solution)/shard_map/ppermute | solution.py:25
  31.4 14.2 %collective-permute-start.1 = (f16[2,4,136,128]{3,2,1,0:T(8,128)(2,1)S(1)}, f16[2,4,136,128]{3,2,1,0:T(8,128)(2,1)S(1)}, u32[]{:S(2)}, u32[]{:S(2)}) collective-permute-start(f16[2,4,136,128]{3,2,1,0:T(8,128)(2,1)S(1)} %convert_element_type.24), channel_id=1, source_target_pairs={{0,2},{1,3},{2,0},{3,1},{4,6},{5,7},{6,4},{7,5},{8,10},{9,11},{10,... | collective-permute-start | bytes 835592 | tf_op jit(solution)/shard_map/ppermute | solution.py:25
  37.8 8.9 %collective-permute-start.3 = (f16[2,4,136,128]{3,2,1,0:T(8,128)(2,1)S(1)}, f16[2,4,136,128]{3,2,1,0:T(8,128)(2,1)S(1)}, u32[]{:S(2)}, u32[]{:S(2)}) collective-permute-start(f16[2,4,136,128]{3,2,1,0:T(8,128)(2,1)S(1)} %convert_element_type.28), channel_id=1, source_target_pairs={{0,4},{1,5},{2,6},{3,7},{4,0},{5,1},{6,2},{7,3},{8,12},{9,13},{10,... | collective-permute-start | bytes 835592 | tf_op jit(solution)/shard_map/ppermute | solution.py:25
  46.7 21.2 %copy-start = (bf16[1024,256]{1,0:T(8,128)(2,1)S(1)}, bf16[1024,256]{1,0:T(8,128)(2,1)}, u32[]{:S(2)}) copy-start(bf16[1024,256]{1,0:T(8,128)(2,1)} %refs_4_.1) | copy-start | bytes 1572868
  61.5 5.0 %collective-permute-start.5 = (f32[256,128]{1,0:T(8,128)S(1)}, f32[256,128]{1,0:T(8,128)S(1)}, u32[]{:S(2)}, u32[]{:S(2)}) collective-permute-start(f32[256,128]{1,0:T(8,128)S(1)} %shard_map.73.refs_0_), channel_id=1, source_target_pairs={{0,2},{1,3},{2,0},{3,1},{4,6},{5,7},{6,4},{7,5},{8,10},{9,11},{10,... | collective-permute-start | bytes 393224 | tf_op jit(solution)/shard_map/ppermute | solution.py:25
  63.1 3.4 %collective-permute-start.4 = (f32[256,128]{1,0:T(8,128)S(1)}, f32[256,128]{1,0:T(8,128)S(1)}, u32[]{:S(2)}, u32[]{:S(2)}) collective-permute-start(f32[256,128]{1,0:T(8,128)S(1)} %shard_map.73.refs_0_), channel_id=1, source_target_pairs={{0,1},{1,0},{2,3},{3,2},{4,5},{5,4},{6,7},{7,6},{8,9},{9,8},{10,11... | collective-permute-start | bytes 393224 | tf_op jit(solution)/shard_map/ppermute | solution.py:25
  66.5 1.3 %collective-permute-start.6 = (f32[256,128]{1,0:T(8,128)S(1)}, f32[256,128]{1,0:T(8,128)S(1)}, u32[]{:S(2)}, u32[]{:S(2)}) collective-permute-start(f32[256,128]{1,0:T(8,128)S(1)} %collective-permute-done.5.refs_2_), channel_id=1, source_target_pairs={{0,1},{1,0},{2,3},{3,2},{4,5},{5,4},{6,7},{7,6},{8,9},{9,8},{10,11... | collective-permute-start | bytes 393224 | tf_op jit(solution)/shard_map/ppermute | solution.py:25

commit v4 on v3

--- a/solution.py
+++ b/solution.py
@@ -39,12 +39,15 @@
     moves += [(t_hbm.at[c], t_ref.at[c]) for c in range(1, chunks)]
     moves += [(wq_hbm.at[:, columns], wq_ref), (l_hbm.at[:, near ^ 1], l_ref.at[0]), (l_hbm.at[:, near], l_ref.at[1])]
     copies = [pltpu.make_async_copy(src, dst, sems.at[i]) for i, (src, dst) in enumerate(moves)]
-    for copy in copies:
+    for copy in copies[:3]:
         copy.start()
     for c in range(chunks):
         part = slice(c * rows, (c + 1) * rows)
         for copy in copies[:2] if c == 0 else [copies[c + 2]]:
             copy.wait()
+        if c == 0:
+            for copy in copies[3:]:
+                copy.start()
         k_ref[part, :] = dot(t_ref[c], wk_ref[...])
         if c == 0:
             copies[2].wait()
@@ -55,7 +58,7 @@
         q_ref[:, h * half : (h + 1) * half] = dot(l_ref[h].reshape(half, -1), wq_ref[...]).T
 
 
-def project_own(at, tokens, latents, w_query, w_key, w_value, chunks=4):
+def project_own(at, tokens, latents, w_query, w_key, w_value, chunks=2):
     (n, d), cols = tokens.shape, w_key.shape[1] // CORES
     n_far, _, block, _ = latents.shape
     m = n_far * NEAR * block
@@ -85,7 +88,7 @@
         v_ref[:, part] = dot(t_ref[part, :], wv_ref[...]).T
 
 
-def project(tokens, w_key, w_value, chunks=4):
+def project(tokens, w_key, w_value, chunks=2):
     (n, d), cols = tokens.shape, w_key.shape[1]
     return pl.pallas_call(
         functools.partial(project_kernel, chunks),
@@ -151,6 +154,12 @@
     return rows[:feats], rows[feats : feats + 1], rows[feats + 1 : feats + 2]
 
 
+def pack(part):
+    num, den, peak = part
+    row = lax.broadcasted_iota(jnp.int32, (EXTRA, num.shape[1]), 0)
+    return jnp.concatenate([num, jnp.where(row == 0, den, peak)], axis=0)
+
+
 def attend_kernel(chunk, half, blocks, encoded, at_ref, q_ref, *refs):
     kv, got, (o_ref, s0, s1) = refs[: 2 * blocks], refs[2 * blocks : -3], refs[-3:]
     tokens, lanes = s0.shape
@@ -159,7 +168,6 @@
     coef = math.log2(math.e) / math.sqrt(size)
     slots = (s0, s1)
     ones = jnp.ones((16, chunk), jnp.bfloat16)
-    row = lax.broadcasted_iota(jnp.int32, (EXTRA, lanes), 0)
     items = [(j, b) for j in range(heads) for b in range(blocks)]
 
     def columns(j):
@@ -190,12 +198,7 @@
                 for f in range(n_far):
                     at = slice(f * block, (f + 1) * block)
                     part = merge([tuple(v[:, at] for v in d) for d in done] + [unpack(g[j, f]) for g in got])
-                    if encoded:
-                        o_ref[j, f] = encode(part)
-                    else:
-                        num, den, high = part
-                        o_ref[j, f, :size] = num
-                        o_ref[j, f, size:] = jnp.where(row[:, at] == 0, den, high)
+                    o_ref[j, f] = encode(part) if encoded else pack(part)
                 done = []
         if i < len(items):
             peak = jnp.max(top, axis=0, keepdims=True)
@@ -219,24 +222,18 @@
     )(group.astype(jnp.int32).reshape(1), query_t, *[a for pair in blocks for a in pair], *got)
 
 
-def combine_kernel(far_first, own_ref, *refs):
+def combine_kernel(own_ref, *refs):
     got, out = refs[:-1], refs[-1]
     heads, n_far = own_ref.shape[:2]
     for j in range(heads):
         for f in range(n_far):
-            part = encode(merge([unpack(own_ref[j, f])] + [decode(g[j, f]) for g in got]))
-            if far_first:
-                out[f, j] = part
-            else:
-                out[j, f] = part
-
-
-def combine(own, got, far_first):
-    heads, n_far, rows, block = own.shape
-    shape = (n_far, heads, rows, block) if far_first else own.shape
-    return pl.pallas_call(
-        functools.partial(combine_kernel, far_first),
-        out_shape=jax.ShapeDtypeStruct(shape, jnp.float32),
+            out[j, f] = encode(merge([unpack(own_ref[j, f])] + [decode(g[j, f]) for g in got]))
+
+
+def combine(own, got):
+    return pl.pallas_call(
+        combine_kernel,
+        out_shape=jax.ShapeDtypeStruct(own.shape, jnp.float32),
         in_specs=[VMEM] * (1 + len(got)),
         out_specs=VMEM,
         compiler_params=PARAMS,
@@ -244,24 +241,46 @@
     )(own, *got)
 
 
-def attended_kernel(part_ref, out):
-    n_tm, heads, rows, _ = part_ref.shape
+def scatter_kernel(n_far, at_ref, own_ref, *refs):
+    got, outs = refs[:-n_far], refs[-n_far:]
+    far = at_ref[4]
+    for s, out in enumerate(outs):
+        for j in range(own_ref.shape[0]):
+            part = merge([unpack(own_ref[j, far ^ s])] + [decode(g[j, far ^ s]) for g in got])
+            out[j] = encode(part) if s else pack(part)
+
+
+def scatter(at, own, got):
+    heads, n_far, rows, block = own.shape
+    return pl.pallas_call(
+        functools.partial(scatter_kernel, n_far),
+        out_shape=[jax.ShapeDtypeStruct((heads, rows, block), jnp.float32)] * n_far,
+        in_specs=[SMEM] + [VMEM] * (1 + len(got)),
+        out_specs=[VMEM] * n_far,
+        compiler_params=PARAMS,
+        cost_estimate=pl.CostEstimate(flops=own.size * 20, bytes_accessed=own.size * 12, transcendentals=0),
+    )(at, own, *got)
+
+
+def attended_kernel(own_ref, *refs):
+    got, out = refs[:-1], refs[-1]
+    heads, rows, _ = own_ref.shape
     feats = rows - EXTRA
     for i in range(heads):
-        num, den, _ = merge([decode(part_ref[t, i]) for t in range(n_tm)])
+        num, den, _ = merge([unpack(own_ref[i])] + [decode(g[i]) for g in got])
         out[i * feats : (i + 1) * feats, :] = num / den
 
 
-def attended(parts):
-    n_tm, heads, rows, block = parts.shape
+def attended(own, got):
+    heads, rows, block = own.shape
     return pl.pallas_call(
         attended_kernel,
         out_shape=jax.ShapeDtypeStruct(((rows - EXTRA) * heads, block), jnp.float32),
-        in_specs=[VMEM],
+        in_specs=[VMEM] * (1 + len(got)),
         out_specs=VMEM,
         compiler_params=PARAMS,
-        cost_estimate=pl.CostEstimate(flops=parts.size * 4, bytes_accessed=parts.size * 4, transcendentals=0),
-    )(parts)
+        cost_estimate=pl.CostEstimate(flops=own.size * 20, bytes_accessed=own.size * 16, transcendentals=0),
+    )(own, *got)
 
 
 def finish_kernel(at_ref, *refs):
@@ -304,7 +323,7 @@
     n, n_x, n_far = n_tm * n_patch, n_patch // CORES, n_tm // NEAR
     tm, patch = lax.axis_index("tm"), lax.axis_index("patch")
     x, core = patch // CORES, patch % CORES
-    at = jnp.stack([x, tm % NEAR, patch, core]).astype(jnp.int32)
+    at = jnp.stack([x, tm % NEAR, patch, core, tm // NEAR]).astype(jnp.int32)
     heads = H // n_patch
     block, d = latents.shape[0] // n_tm, latents.shape[1]
     shape = (heads, n_far, d // H + EXTRA, block)
@@ -330,13 +349,14 @@
             if s:
                 got[half].append(wide(xor_permute(narrow(part), n, CORES * s)))
             elif half == 0:
-                part = combine(part, got[0], False)
+                part = combine(part, got[0])
                 got[1].append(wide(xor_permute(narrow(part), n, n_patch)))
             else:
-                part = combine(part, got[1], True)
-    groups = [[f * NEAR + k for f in range(n_far)] for k in range(NEAR)]
-    part = wide(lax.all_to_all(narrow(part), "tm", 0, 0, axis_index_groups=groups, tiled=True))
-    pieces = [attended(part)]
+                mine, *sent = scatter(at, part, got[1])
+    far_got = {}
+    for s in sorted(range(1, n_far), key=lambda s: (-s.bit_length(), s)):
+        far_got[s] = wide(xor_permute(narrow(sent[s - 1]), n, n_patch * NEAR * s))
+    pieces = [attended(mine, [far_got[s] for s in range(1, n_far)])]
     pieces += [xor_permute(pieces[0], n, CORES * s) for s in range(1, n_x)]
     pieces = [p for piece in pieces for p in (piece, xor_permute(piece, n, 1))]
     return finish(at, pieces, w_out)

time: 69.6 us -> 65.8 us (0.945)
  blocking collectives: 13.4 us -> 0 us
  waiting for transfers between devices: 5.77 us -> 10.6 us
  starting transfers between devices: 6.78 us -> 11.3 us
    all_to_all x1 -> x0, blocking collectives: 13.4 us -> none  [per_device(): lax.all_to_all(narrow(part), 'tm', 0, 0, axis_index_groups=groups, tiled=...]
    ppermute x7 -> x10, waiting for transfers between devices: 5.77 us -> 10.6 us  [xor_permute(): return lax.ppermute(value, AXES, [(i, i ^ step) for i in range(n)])]
    ppermute x7 -> x10, starting transfers between devices: 6.78 us -> 11.3 us  [xor_permute(): return lax.ppermute(value, AXES, [(i, i ^ step) for i in range(n)])]
  transfers between devices with their start and end apart: 7 -> 10, of which waited for: 3 -> 5; matrix products, arithmetic and copies ran while one was open for 0% -> 0% of each run, Pallas kernels for 43% -> 45%
where the time goes in v4:
time: 65.8 us; the launch traced here: 65.7 us
  Pallas kernels  43.1 us (66%)
  starting transfers between devices  11.3 us (17%)
  waiting for transfers between devices  10.6 us (16%)
    pallas_call x5, Pallas kernels, attend(): pl.pallas_call(functools.partial(attend_kernel, chunk, half, len(blocks),...  23.2 us
    ppermute x10, starting transfers between devices, xor_permute(): return lax.ppermute(value, AXES, [(i, i ^ step) for i in range(n)])  11.3 us
    ppermute x10, waiting for transfers between devices, xor_permute(): return lax.ppermute(value, AXES, [(i, i ^ step) for i in range(n)])  10.6 us
    pallas_call x1, Pallas kernels, project_own(): pl.pallas_call(project_own_kernel, out_shape=[jax.ShapeDtypeStruct(s, jnp...  9.14 us
    pallas_call x1, Pallas kernels, project(): pl.pallas_call(functools.partial(project_kernel, chunks), out_shape=[jax....  6.81 us
    pallas_call x1, Pallas kernels, finish(): pl.pallas_call(finish_kernel, out_shape=jax.ShapeDtypeStruct((block, w_ou...  1.55 us
    pallas_call x1, Pallas kernels, scatter(): pl.pallas_call(functools.partial(scatter_kernel, n_far), out_shape=[jax.S...  1.49 us
  transfers between devices with their start and end apart: 10, of which 5 were waited for; matrix products, arithmetic and copies ran while one was open for 0% of the time, Pallas kernels for 45%

profile of v4, /device:TPU:0, one launch (start us, length us, event | category | flops | bytes accessed | tf_op | source)
XLA Modules:
  0.0 65.7 jit_solution(7600454996084699974)
XLA Ops:
  0.0 0.5 collective-permute-start
  0.5 0.1 stack.23.at_ref
  0.5 9.1 %shard_map.64 = (bf16[2048,512]{1,0:T(8,128)(2,1)S(1)}, bf16[512,2048]{1,0:T(8,128)(2,1)S(1)}, bf16[512,1024]{1,0:T(8,128)(2,1)S(1)}, bf16[1024,512]{1,0:T(8,128)(2,1)S(1)}, bf16[1024,512]{1,0:T(8,128)(2,1)S(1)}) custom-call(s32[5]{0:T(128)S(1)} %stack.23.at_ref, bf16[2,1024,1024]{2,1,0:T(8,128)(2,1)} %bitcast.8, bf16[4,2,128,1024]{3,2,1,0:T(8,128)(2,1)} %bitcast.9, ...), custom_call_target="tpu_custom_call" | custom-call | flops 5368709120 | bytes 9437184 | tf_op jit(solution)/shard_map/pallas_call | solution.py:65
  9.7 2.8 %shard_map.65.refs_2_ = f32[2,4,136,128]{3,2,1,0:T(8,128)S(1)} custom-call(s32[1]{0:T(128)} %bitcast.7.at_ref, bf16[512,1024]{1,0:T(8,128)(2,1)S(1)} %get-tuple-element.36.q_ref, bf16[2048,512]{1,0:T(8,128)(2,1)S(1)} %get-tuple-element.26.refs_0_, bf16[512,2048]{1,0:T(8,128)(2,1)S(1)} %get-tuple-element.27.refs_1_), custom_call_target="tpu_custom_call" | custom-call | flops 1073741824 | bytes 557056 | tf_op jit(solution)/shard_map/pallas_call | solution.py:210
  12.5 0.0 collective-permute-done.t_ref
  12.5 6.8 %shard_map.66 = (bf16[2048,512]{1,0:T(8,128)(2,1)S(1)}, bf16[512,2048]{1,0:T(8,128)(2,1)S(1)}) custom-call(bf16[2048,1024]{1,0:T(8,128)(2,1)} %collective-permute-done.t_ref, bf16[1024,512]{1,0:T(8,128)(2,1)S(1)} %get-tuple-element.29.wk_ref, bf16[1024,512]{1,0:T(8,128)(2,1)S(1)} %get-tuple-element.30.wv_ref), custom_call_target="tpu_custom_call" | custom-call | flops 4294967296 | bytes 6291456 | tf_op jit(solution)/shard_map/pallas_call | solution.py:93
  19.3 3.4 %shard_map.67 = f32[2,4,136,128]{3,2,1,0:T(8,128)S(1)} custom-call(s32[1]{0:T(128)} %bitcast.7.at_ref, bf16[512,1024]{1,0:T(8,128)(2,1)S(1)} %get-tuple-element.36.q_ref, bf16[2048,512]{1,0:T(8,128)(2,1)S(1)} %get-tuple-element.31.refs_0_.refs_2_, bf16[512,2048]{1,0:T(8,128)(2,1)S(1)} %get-tuple-element.32.refs_1_.refs_3_, ...), custom_call_target="tpu_custom_call" | custom-call | flops 1073741824 | bytes 557056 | tf_op jit(solution)/shard_map/pallas_call | solution.py:210
  22.8 2.5 %collective-permute-start.2 = (f16[2,4,136,128]{3,2,1,0:T(8,128)(2,1)S(1)}, f16[2,4,136,128]{3,2,1,0:T(8,128)(2,1)S(1)}, u32[]{:S(2)}, u32[]{:S(2)}) collective-permute-start(f16[2,4,136,128]{3,2,1,0:T(8,128)(2,1)S(1)} %convert_element_type.38), channel_id=1, source_target_pairs={{0,2},{1,3},{2,0},{3,1},{4,6},{5,7},{6,4},{7,5},{8,10},{9,11},{10,... | collective-permute-start | bytes 835592 | tf_op jit(solution)/shard_map/ppermute | solution.py:25
  25.3 5.8 %shard_map.68 = f32[2,4,136,128]{3,2,1,0:T(8,128)S(1)} custom-call(s32[1]{0:T(128)} %bitcast.7.at_ref, bf16[512,1024]{1,0:T(8,128)(2,1)S(1)} %get-tuple-element.36.q_ref, bf16[2048,512]{1,0:T(8,128)(2,1)S(1)} %get-tuple-element.26.refs_0_, bf16[512,2048]{1,0:T(8,128)(2,1)S(1)} %get-tuple-element.27.refs_1_, ...), custom_call_target="tpu_custom_call" | custom-call | flops 2147483648 | bytes 557056 | tf_op jit(solution)/shard_map/pallas_call | solution.py:210
  31.2 0.1 collective-permute-start.1
  31.3 5.5 %shard_map.69.own_ref = f32[2,4,136,128]{3,2,1,0:T(8,128)S(1)} custom-call(s32[1]{0:T(128)} %bitcast.at_ref, bf16[512,1024]{1,0:T(8,128)(2,1)S(1)} %get-tuple-element.36.q_ref, bf16[2048,512]{1,0:T(8,128)(2,1)S(1)} %get-tuple-element.26.refs_0_, bf16[512,2048]{1,0:T(8,128)(2,1)S(1)} %get-tuple-element.27.refs_1_, ...), custom_call_target="tpu_custom_call" | custom-call | flops 2147483648 | bytes 557056 | tf_op jit(solution)/shard_map/pallas_call | solution.py:210
  36.8 0.0 collective-permute-done.2
  36.8 0.7 %shard_map.71 = f32[2,4,136,128]{3,2,1,0:T(8,128)S(1)} custom-call(f32[2,4,136,128]{3,2,1,0:T(8,128)S(1)} %shard_map.69.own_ref, f32[2,4,136,128]{3,2,1,0:T(8,128)S(1)} %convert_element_type.39.refs_0_), custom_call_target="tpu_custom_call" | custom-call | flops 2785280 | bytes 1671168 | tf_op jit(solution)/shard_map/pallas_call | solution.py:234
  37.6 2.1 %collective-permute-start.3 = (f16[2,4,136,128]{3,2,1,0:T(8,128)(2,1)S(1)}, f16[2,4,136,128]{3,2,1,0:T(8,128)(2,1)S(1)}, u32[]{:S(2)}, u32[]{:S(2)}) collective-permute-start(f16[2,4,136,128]{3,2,1,0:T(8,128)(2,1)S(1)} %convert_element_type.40), channel_id=1, source_target_pairs={{0,4},{1,5},{2,6},{3,7},{4,0},{5,1},{6,2},{7,3},{8,12},{9,13},{10,... | collective-permute-start | bytes 835592 | tf_op jit(solution)/shard_map/ppermute | solution.py:25
  39.7 5.7 %shard_map.70.own_ref = f32[2,4,136,128]{3,2,1,0:T(8,128)S(1)} custom-call(s32[1]{0:T(128)} %bitcast.at_ref, bf16[512,1024]{1,0:T(8,128)(2,1)S(1)} %get-tuple-element.36.q_ref, bf16[2048,512]{1,0:T(8,128)(2,1)S(1)} %get-tuple-element.26.refs_0_, bf16[512,2048]{1,0:T(8,128)(2,1)S(1)} %get-tuple-element.27.refs_1_, ...), custom_call_target="tpu_custom_call" | custom-call | flops 2147483648 | bytes 557056 | tf_op jit(solution)/shard_map/pallas_call | solution.py:210
  45.4 0.0 collective-permute-done.1
  45.4 0.0 copy-start
  45.4 1.0 %collective-permute-done.3 = f16[2,4,136,128]{3,2,1,0:T(8,128)(2,1)S(1)} collective-permute-done((f16[2,4,136,128]{3,2,1,0:T(8,128)(2,1)S(1)}, f16[2,4,136,128]{3,2,1,0:T(8,128)(2,1)S(1)}, u32[]{:S(2)}, u32[]{:S(2)}) %collective-permute-start.3) | collective-permute-done | bytes 278560 | tf_op jit(solution)/shard_map/ppermute | solution.py:25
  46.5 1.5 %shard_map.72 = (f32[2,136,128]{2,1,0:T(8,128)S(1)}, f32[2,136,128]{2,1,0:T(8,128)S(1)}, f32[2,136,128]{2,1,0:T(8,128)S(1)}, f32[2,136,128]{2,1,0:T(8,128)S(1)}) custom-call(s32[5]{0:T(128)S(1)} %stack.23.at_ref, f32[2,4,136,128]{3,2,1,0:T(8,128)S(1)} %shard_map.70.own_ref, f32[2,4,136,128]{3,2,1,0:T(8,128)S(1)} %convert_element_type.37.refs_0_, ...), custom_call_target="tpu_custom_call" | custom-call | flops 2785280 | bytes 1671168 | tf_op jit(solution)/shard_map/pallas_call | solution.py:255
  48.0 3.9 %collective-permute-start.6 = (f16[2,136,128]{2,1,0:T(8,128)(2,1)S(1)}, f16[2,136,128]{2,1,0:T(8,128)(2,1)S(1)}, u32[]{:S(2)}, u32[]{:S(2)}) collective-permute-start(f16[2,136,128]{2,1,0:T(8,128)(2,1)S(1)} %convert_element_type.46), channel_id=1, source_target_pairs={{0,24},{1,25},{2,26},{3,27},{4,28},{5,29},{6,30},{7,31},{8,16},{9,... | collective-permute-start | bytes 208904 | tf_op jit(solution)/shard_map/ppermute | solution.py:25
  51.9 0.0 collective-permute-start.5
  51.9 0.7 %collective-permute-start.4 = (f16[2,136,128]{2,1,0:T(8,128)(2,1)S(1)}, f16[2,136,128]{2,1,0:T(8,128)(2,1)S(1)}, u32[]{:S(2)}, u32[]{:S(2)}) collective-permute-start(f16[2,136,128]{2,1,0:T(8,128)(2,1)S(1)} %convert_element_type.42), channel_id=1, source_target_pairs={{0,8},{1,9},{2,10},{3,11},{4,12},{5,13},{6,14},{7,15},{8,0},{9,1},... | collective-permute-start | bytes 208904 | tf_op jit(solution)/shard_map/ppermute | solution.py:25
  52.6 2.3 %collective-permute-done.6 = f16[2,136,128]{2,1,0:T(8,128)(2,1)S(1)} collective-permute-done((f16[2,136,128]{2,1,0:T(8,128)(2,1)S(1)}, f16[2,136,128]{2,1,0:T(8,128)(2,1)S(1)}, u32[]{:S(2)}, u32[]{:S(2)}) %collective-permute-start.6) | collective-permute-done | bytes 69664 | tf_op jit(solution)/shard_map/ppermute | solution.py:25
  54.9 2.5 %collective-permute-done.5 = f16[2,136,128]{2,1,0:T(8,128)(2,1)S(1)} collective-permute-done((f16[2,136,128]{2,1,0:T(8,128)(2,1)S(1)}, f16[2,136,128]{2,1,0:T(8,128)(2,1)S(1)}, u32[]{:S(2)}, u32[]{:S(2)}) %collective-permute-start.5) | collective-permute-done | bytes 69664 | tf_op jit(solution)/shard_map/ppermute | solution.py:25
  57.4 0.0 collective-permute-done.4
  57.5 0.2 shard_map.73.refs_0_
  57.7 1.6 %collective-permute-start.8 = (f32[256,128]{1,0:T(8,128)S(1)}, f32[256,128]{1,0:T(8,128)S(1)}, u32[]{:S(2)}, u32[]{:S(2)}) collective-permute-start(f32[256,128]{1,0:T(8,128)S(1)} %shard_map.73.refs_0_), channel_id=1, source_target_pairs={{0,2},{1,3},{2,0},{3,1},{4,6},{5,7},{6,4},{7,5},{8,10},{9,11},{10,... | collective-permute-start | bytes 393224 | tf_op jit(solution)/shard_map/ppermute | solution.py:25
  59.3 0.0 collective-permute-start.7
  59.3 3.4 %collective-permute-done.8.refs_2_ = f32[256,128]{1,0:T(8,128)S(1)} collective-permute-done((f32[256,128]{1,0:T(8,128)S(1)}, f32[256,128]{1,0:T(8,128)S(1)}, u32[]{:S(2)}, u32[]{:S(2)}) %collective-permute-start.8) | collective-permute-done | bytes 131104 | tf_op jit(solution)/shard_map/ppermute | solution.py:25
  62.8 0.0 collective-permute-start.9
  62.8 0.0 collective-permute-done.7.refs_1_
  62.8 1.3 %collective-permute-done.9.refs_3_ = f32[256,128]{1,0:T(8,128)S(1)} collective-permute-done((f32[256,128]{1,0:T(8,128)S(1)}, f32[256,128]{1,0:T(8,128)S(1)}, u32[]{:S(2)}, u32[]{:S(2)}) %collective-permute-start.9) | collective-permute-done | bytes 131104 | tf_op jit(solution)/shard_map/ppermute | solution.py:25
  64.1 0.0 copy-done
  64.1 1.5 %shard_map.74 = bf16[128,256]{1,0:T(8,128)(2,1)} custom-call(s32[5]{0:T(128)S(1)} %stack.23.at_ref, f32[256,128]{1,0:T(8,128)S(1)} %shard_map.73.refs_0_, f32[256,128]{1,0:T(8,128)S(1)} %collective-permute-done.7.refs_1_, f32[256,128]{1,0:T(8,128)S(1)} %collective-permute-done.8.refs_2_, f32[256,128]{1,0:T(8,128)S(1)} %collective-permute-done.9.refs_3_, ...), custom_call_target="tpu_custom_call" | custom-call | flops 67108864 | bytes 524288 | tf_op jit(solution)/shard_map/pallas_call | solution.py:303
  (12 shorter events, 0.3 us)
Async XLA Ops:
  0.0 12.5 %collective-permute-start = (bf16[2048,1024]{1,0:T(8,128)(2,1)}, bf16[2048,1024]{1,0:T(8,128)(2,1)}, u32[]{:S(2)}, u32[]{:S(2)}) collective-permute-start(bf16[2048,1024]{1,0:T(8,128)(2,1)} %param.7), channel_id=1, source_target_pairs={{0,1},{1,0},{2,3},{3,2},{4,5},{5,4},{6,7},{7,6},{8,9},{9,8},{10,11... | collective-permute-start | bytes 12582920 | tf_op jit(solution)/shard_map/ppermute | solution.py:25
  22.8 14.0 %collective-permute-start.2 = (f16[2,4,136,128]{3,2,1,0:T(8,128)(2,1)S(1)}, f16[2,4,136,128]{3,2,1,0:T(8,128)(2,1)S(1)}, u32[]{:S(2)}, u32[]{:S(2)}) collective-permute-start(f16[2,4,136,128]{3,2,1,0:T(8,128)(2,1)S(1)} %convert_element_type.38), channel_id=1, source_target_pairs={{0,2},{1,3},{2,0},{3,1},{4,6},{5,7},{6,4},{7,5},{8,10},{9,11},{10,... | collective-permute-start | bytes 835592 | tf_op jit(solution)/shard_map/ppermute | solution.py:25
  31.2 14.2 %collective-permute-start.1 = (f16[2,4,136,128]{3,2,1,0:T(8,128)(2,1)S(1)}, f16[2,4,136,128]{3,2,1,0:T(8,128)(2,1)S(1)}, u32[]{:S(2)}, u32[]{:S(2)}) collective-permute-start(f16[2,4,136,128]{3,2,1,0:T(8,128)(2,1)S(1)} %convert_element_type.36), channel_id=1, source_target_pairs={{0,2},{1,3},{2,0},{3,1},{4,6},{5,7},{6,4},{7,5},{8,10},{9,11},{10,... | collective-permute-start | bytes 835592 | tf_op jit(solution)/shard_map/ppermute | solution.py:25
  37.6 8.9 %collective-permute-start.3 = (f16[2,4,136,128]{3,2,1,0:T(8,128)(2,1)S(1)}, f16[2,4,136,128]{3,2,1,0:T(8,128)(2,1)S(1)}, u32[]{:S(2)}, u32[]{:S(2)}) collective-permute-start(f16[2,4,136,128]{3,2,1,0:T(8,128)(2,1)S(1)} %convert_element_type.40), channel_id=1, source_target_pairs={{0,4},{1,5},{2,6},{3,7},{4,0},{5,1},{6,2},{7,3},{8,12},{9,13},{10,... | collective-permute-start | bytes 835592 | tf_op jit(solution)/shard_map/ppermute | solution.py:25
  45.4 18.7 %copy-start = (bf16[1024,256]{1,0:T(8,128)(2,1)S(1)}, bf16[1024,256]{1,0:T(8,128)(2,1)}, u32[]{:S(2)}) copy-start(bf16[1024,256]{1,0:T(8,128)(2,1)} %refs_4_.1) | copy-start | bytes 1572868
  48.0 6.9 %collective-permute-start.6 = (f16[2,136,128]{2,1,0:T(8,128)(2,1)S(1)}, f16[2,136,128]{2,1,0:T(8,128)(2,1)S(1)}, u32[]{:S(2)}, u32[]{:S(2)}) collective-permute-start(f16[2,136,128]{2,1,0:T(8,128)(2,1)S(1)} %convert_element_type.46), channel_id=1, source_target_pairs={{0,24},{1,25},{2,26},{3,27},{4,28},{5,29},{6,30},{7,31},{8,16},{9,... | collective-permute-start | bytes 208904 | tf_op jit(solution)/shard_map/ppermute | solution.py:25
  51.9 5.5 %collective-permute-start.5 = (f16[2,136,128]{2,1,0:T(8,128)(2,1)S(1)}, f16[2,136,128]{2,1,0:T(8,128)(2,1)S(1)}, u32[]{:S(2)}, u32[]{:S(2)}) collective-permute-start(f16[2,136,128]{2,1,0:T(8,128)(2,1)S(1)} %convert_element_type.44), channel_id=1, source_target_pairs={{0,16},{1,17},{2,18},{3,19},{4,20},{5,21},{6,22},{7,23},{8,24},{9,... | collective-permute-start | bytes 208904 | tf_op jit(solution)/shard_map/ppermute | solution.py:25
  51.9 5.5 %collective-permute-start.4 = (f16[2,136,128]{2,1,0:T(8,128)(2,1)S(1)}, f16[2,136,128]{2,1,0:T(8,128)(2,1)S(1)}, u32[]{:S(2)}, u32[]{:S(2)}) collective-permute-start(f16[2,136,128]{2,1,0:T(8,128)(2,1)S(1)} %convert_element_type.42), channel_id=1, source_target_pairs={{0,8},{1,9},{2,10},{3,11},{4,12},{5,13},{6,14},{7,15},{8,0},{9,1},... | collective-permute-start | bytes 208904 | tf_op jit(solution)/shard_map/ppermute | solution.py:25
  57.7 5.0 %collective-permute-start.8 = (f32[256,128]{1,0:T(8,128)S(1)}, f32[256,128]{1,0:T(8,128)S(1)}, u32[]{:S(2)}, u32[]{:S(2)}) collective-permute-start(f32[256,128]{1,0:T(8,128)S(1)} %shard_map.73.refs_0_), channel_id=1, source_target_pairs={{0,2},{1,3},{2,0},{3,1},{4,6},{5,7},{6,4},{7,5},{8,10},{9,11},{10,... | collective-permute-start | bytes 393224 | tf_op jit(solution)/shard_map/ppermute | solution.py:25
  59.3 3.5 %collective-permute-start.7 = (f32[256,128]{1,0:T(8,128)S(1)}, f32[256,128]{1,0:T(8,128)S(1)}, u32[]{:S(2)}, u32[]{:S(2)}) collective-permute-start(f32[256,128]{1,0:T(8,128)S(1)} %shard_map.73.refs_0_), channel_id=1, source_target_pairs={{0,1},{1,0},{2,3},{3,2},{4,5},{5,4},{6,7},{7,6},{8,9},{9,8},{10,11... | collective-permute-start | bytes 393224 | tf_op jit(solution)/shard_map/ppermute | solution.py:25
  62.8 1.3 %collective-permute-start.9 = (f32[256,128]{1,0:T(8,128)S(1)}, f32[256,128]{1,0:T(8,128)S(1)}, u32[]{:S(2)}, u32[]{:S(2)}) collective-permute-start(f32[256,128]{1,0:T(8,128)S(1)} %collective-permute-done.8.refs_2_), channel_id=1, source_target_pairs={{0,1},{1,0},{2,3},{3,2},{4,5},{5,4},{6,7},{7,6},{8,9},{9,8},{10,11... | collective-permute-start | bytes 393224 | tf_op jit(solution)/shard_map/ppermute | solution.py:25

commit v5 on v4

--- a/solution.py
+++ b/solution.py
@@ -31,34 +31,43 @@
 
 def project_own_kernel(at_ref, t_hbm, l_hbm, wq_hbm, wk_hbm, wv_hbm, k_ref, v_ref, q_ref, wk_ref, wv_ref, wq_ref, t_ref, l_ref, sems):
     near, core = at_ref[1], at_ref[3]
-    chunks, rows, _ = t_ref.shape
+    n = t_ref.shape[0]
     cols = k_ref.shape[1]
     half = l_ref.shape[1] * l_ref.shape[2]
     columns = pl.ds(pl.multiple_of(core * cols, cols), cols)
-    moves = [(wk_hbm.at[:, columns], wk_ref), (t_hbm.at[0], t_ref.at[0]), (wv_hbm.at[:, columns], wv_ref)]
-    moves += [(t_hbm.at[c], t_ref.at[c]) for c in range(1, chunks)]
+    parts = [slice(0, n // 4), slice(n // 4, n // 2), slice(n // 2, n)]
+    moves = [(wk_hbm.at[:, columns], wk_ref), (t_hbm.at[parts[0]], t_ref.at[parts[0]])]
+    moves += [(wv_hbm.at[:, columns], wv_ref)] + [(t_hbm.at[p], t_ref.at[p]) for p in parts[1:]]
     moves += [(wq_hbm.at[:, columns], wq_ref), (l_hbm.at[:, near ^ 1], l_ref.at[0]), (l_hbm.at[:, near], l_ref.at[1])]
     copies = [pltpu.make_async_copy(src, dst, sems.at[i]) for i, (src, dst) in enumerate(moves)]
-    for copy in copies[:3]:
+
+    def wait(*which):
+        for i in which:
+            copies[i].wait()
+
+    def project_keys(part):
+        k_ref[part, :] = dot(t_ref[part, :], wk_ref[...])
+
+    def project_vals(part):
+        v_ref[:, part] = dot(t_ref[part, :], wv_ref[...]).T
+
+    for copy in copies:
         copy.start()
-    for c in range(chunks):
-        part = slice(c * rows, (c + 1) * rows)
-        for copy in copies[:2] if c == 0 else [copies[c + 2]]:
-            copy.wait()
-        if c == 0:
-            for copy in copies[3:]:
-                copy.start()
-        k_ref[part, :] = dot(t_ref[c], wk_ref[...])
-        if c == 0:
-            copies[2].wait()
-        v_ref[:, part] = dot(t_ref[c], wv_ref[...]).T
-    copies[chunks + 2].wait()
+    wait(0, 1)
+    project_keys(parts[0])
+    wait(2, 3)
+    project_vals(parts[0])
+    project_keys(parts[1])
+    project_vals(parts[1])
+    wait(4)
+    project_keys(parts[2])
+    project_vals(parts[2])
+    wait(5, 6, 7)
     for h in range(NEAR):
-        copies[chunks + 3 + h].wait()
         q_ref[:, h * half : (h + 1) * half] = dot(l_ref[h].reshape(half, -1), wq_ref[...]).T
 
 
-def project_own(at, tokens, latents, w_query, w_key, w_value, chunks=2):
+def project_own(at, tokens, latents, w_query, w_key, w_value):
     (n, d), cols = tokens.shape, w_key.shape[1] // CORES
     n_far, _, block, _ = latents.shape
     m = n_far * NEAR * block
@@ -69,32 +78,37 @@
         out_specs=[VMEM] * 5,
         scratch_shapes=[
             pltpu.VMEM((d, cols), jnp.bfloat16),
-            pltpu.VMEM((chunks, n // chunks, d), jnp.bfloat16),
+            pltpu.VMEM((n, d), jnp.bfloat16),
             pltpu.VMEM((NEAR, n_far, block, d), jnp.bfloat16),
-            pltpu.SemaphoreType.DMA((chunks + 5,)),
+            pltpu.SemaphoreType.DMA((8,)),
         ],
         compiler_params=pltpu.CompilerParams(vmem_limit_bytes=46 * 2**20),
         cost_estimate=pl.CostEstimate(
             flops=(4 * n + 2 * m) * d * cols, bytes_accessed=2 * (n * d + m * d + 3 * d * cols), transcendentals=0
         ),
-    )(at, tokens.reshape(chunks, n // chunks, d), latents, w_query, w_key, w_value)
-
-
-def project_kernel(chunks, t_ref, wk_ref, wv_ref, k_ref, v_ref):
-    rows = t_ref.shape[0] // chunks
-    for c in range(chunks):
-        part = slice(c * rows, (c + 1) * rows)
+    )(at, tokens, latents, w_query, w_key, w_value)
+
+
+def project_kernel(t_hbm, wk_ref, wv_ref, k_ref, v_ref, t_ref, sems):
+    n = t_ref.shape[0]
+    parts = [slice(0, n // 4), slice(n // 4, n // 2), slice(n // 2, n)]
+    copies = [pltpu.make_async_copy(t_hbm.at[p], t_ref.at[p], sems.at[i]) for i, p in enumerate(parts)]
+    for copy in copies:
+        copy.start()
+    for copy, part in zip(copies, parts):
+        copy.wait()
         k_ref[part, :] = dot(t_ref[part, :], wk_ref[...])
         v_ref[:, part] = dot(t_ref[part, :], wv_ref[...]).T
 
 
-def project(tokens, w_key, w_value, chunks=2):
+def project(tokens, w_key, w_value):
     (n, d), cols = tokens.shape, w_key.shape[1]
     return pl.pallas_call(
-        functools.partial(project_kernel, chunks),
+        project_kernel,
         out_shape=[jax.ShapeDtypeStruct(s, jnp.bfloat16) for s in ((n, cols), (cols, n))],
-        in_specs=[VMEM] * 3,
+        in_specs=[HBM, VMEM, VMEM],
         out_specs=[VMEM] * 2,
+        scratch_shapes=[pltpu.VMEM((n, d), jnp.bfloat16), pltpu.SemaphoreType.DMA((3,))],
         compiler_params=PARAMS,
         cost_estimate=pl.CostEstimate(flops=4 * n * d * cols, bytes_accessed=2 * (n * d + 2 * d * cols), transcendentals=0),
     )(tokens, w_key, w_value)
@@ -222,17 +236,18 @@
     )(group.astype(jnp.int32).reshape(1), query_t, *[a for pair in blocks for a in pair], *got)
 
 
-def combine_kernel(own_ref, *refs):
+def combine_kernel(encoded, own_ref, *refs):
     got, out = refs[:-1], refs[-1]
     heads, n_far = own_ref.shape[:2]
     for j in range(heads):
         for f in range(n_far):
-            out[j, f] = encode(merge([unpack(own_ref[j, f])] + [decode(g[j, f]) for g in got]))
-
-
-def combine(own, got):
-    return pl.pallas_call(
-        combine_kernel,
+            part = merge([unpack(own_ref[j, f])] + [decode(g[j, f]) for g in got])
+            out[j, f] = encode(part) if encoded else pack(part)
+
+
+def combine(own, got, encoded):
+    return pl.pallas_call(
+        functools.partial(combine_kernel, encoded),
         out_shape=jax.ShapeDtypeStruct(own.shape, jnp.float32),
         in_specs=[VMEM] * (1 + len(got)),
         out_specs=VMEM,
@@ -333,7 +348,7 @@
     keys, vals_t, query_t, own_key, own_value = project_own(at, tokens, latents, w_query, w_key, w_value)
     near = [(keys, vals_t)]
     both = None
-    got = [[], []]
+    got, across = [[], []], []
     for s in range(n_x - 1, -1, -1):
         group = x ^ s
         for half in range(2):
@@ -349,10 +364,11 @@
             if s:
                 got[half].append(wide(xor_permute(narrow(part), n, CORES * s)))
             elif half == 0:
-                part = combine(part, got[0])
-                got[1].append(wide(xor_permute(narrow(part), n, n_patch)))
+                part = combine(part, got[0], True)
+                across.append(wide(xor_permute(narrow(part), n, n_patch)))
             else:
-                mine, *sent = scatter(at, part, got[1])
+                part = combine(part, got[1], False)
+                mine, *sent = scatter(at, part, across)
     far_got = {}
     for s in sorted(range(1, n_far), key=lambda s: (-s.bit_length(), s)):
         far_got[s] = wide(xor_permute(narrow(sent[s - 1]), n, n_patch * NEAR * s))

time: 65.8 us -> 64.5 us (0.980)
  Pallas kernels: 43.1 us -> 42.1 us
    pallas_call x2 -> x3, Pallas kernels: 7.52 us -> 7.43 us  [the longest x1 6.39 us: project(): pl.pallas_call(project_kernel, out_shape=[jax.ShapeDtypeStruct(s, jnp.bfl...]
  transfers between devices with their start and end apart: 10 -> 10, of which waited for: 5 -> 5; matrix products, arithmetic and copies ran while one was open for 0% -> 0% of each run, Pallas kernels for 45% -> 46%
where the time goes in v5:
time: 64.5 us; the launch traced here: 64.3 us
  Pallas kernels  42.1 us (65%)
  starting transfers between devices  11.4 us (18%)
  waiting for transfers between devices  10.2 us (16%)
    pallas_call x5, Pallas kernels, attend(): pl.pallas_call(functools.partial(attend_kernel, chunk, half, len(blocks),...  23.2 us
    ppermute x10, starting transfers between devices, xor_permute(): return lax.ppermute(value, AXES, [(i, i ^ step) for i in range(n)])  11.4 us
    ppermute x10, waiting for transfers between devices, xor_permute(): return lax.ppermute(value, AXES, [(i, i ^ step) for i in range(n)])  10.2 us
    pallas_call x1, Pallas kernels, project_own(): pl.pallas_call(project_own_kernel, out_shape=[jax.ShapeDtypeStruct(s, jnp...  8.54 us
    pallas_call x1, Pallas kernels, project(): pl.pallas_call(project_kernel, out_shape=[jax.ShapeDtypeStruct(s, jnp.bfl...  6.39 us
    pallas_call x1, Pallas kernels, finish(): pl.pallas_call(finish_kernel, out_shape=jax.ShapeDtypeStruct((block, w_ou...  1.55 us
  transfers between devices with their start and end apart: 10, of which 5 were waited for; matrix products, arithmetic and copies ran while one was open for 0% of the time, Pallas kernels for 46%

profile of v5, /device:TPU:0, one launch (start us, length us, event | category | flops | bytes accessed | tf_op | source)
XLA Modules:
  0.0 64.3 jit_solution(5797190862462185097)
XLA Ops:
  0.0 0.5 collective-permute-start
  0.5 0.1 stack.23.at_ref
  0.5 8.5 %shard_map.64 = (bf16[2048,512]{1,0:T(8,128)(2,1)S(1)}, bf16[512,2048]{1,0:T(8,128)(2,1)S(1)}, bf16[512,1024]{1,0:T(8,128)(2,1)S(1)}, bf16[1024,512]{1,0:T(8,128)(2,1)S(1)}, bf16[1024,512]{1,0:T(8,128)(2,1)S(1)}) custom-call(s32[5]{0:T(128)S(1)} %stack.23.at_ref, bf16[2048,1024]{1,0:T(8,128)(2,1)} %t_hbm.1, bf16[4,2,128,1024]{3,2,1,0:T(8,128)(2,1)} %bitcast.7, ...), custom_call_target="tpu_custom_call" | custom-call | flops 5368709120 | bytes 9437184 | tf_op jit(solution)/shard_map/pallas_call | solution.py:74
  9.1 2.8 %shard_map.65.refs_2_ = f32[2,4,136,128]{3,2,1,0:T(8,128)S(1)} custom-call(s32[1]{0:T(128)} %bitcast.6.at_ref, bf16[512,1024]{1,0:T(8,128)(2,1)S(1)} %get-tuple-element.36.q_ref, bf16[2048,512]{1,0:T(8,128)(2,1)S(1)} %get-tuple-element.26.refs_0_, bf16[512,2048]{1,0:T(8,128)(2,1)S(1)} %get-tuple-element.27.refs_1_), custom_call_target="tpu_custom_call" | custom-call | flops 1073741824 | bytes 557056 | tf_op jit(solution)/shard_map/pallas_call | solution.py:224
  11.9 0.0 collective-permute-done.t_hbm
  11.9 6.4 %shard_map.66 = (bf16[2048,512]{1,0:T(8,128)(2,1)S(1)}, bf16[512,2048]{1,0:T(8,128)(2,1)S(1)}) custom-call(bf16[2048,1024]{1,0:T(8,128)(2,1)} %collective-permute-done.t_hbm, bf16[1024,512]{1,0:T(8,128)(2,1)S(1)} %get-tuple-element.29.wk_ref, bf16[1024,512]{1,0:T(8,128)(2,1)S(1)} %get-tuple-element.30.wv_ref), custom_call_target="tpu_custom_call" | custom-call | flops 4294967296 | bytes 6291456 | tf_op jit(solution)/shard_map/pallas_call | solution.py:106
  18.3 3.4 %shard_map.67 = f32[2,4,136,128]{3,2,1,0:T(8,128)S(1)} custom-call(s32[1]{0:T(128)} %bitcast.6.at_ref, bf16[512,1024]{1,0:T(8,128)(2,1)S(1)} %get-tuple-element.36.q_ref, bf16[2048,512]{1,0:T(8,128)(2,1)S(1)} %get-tuple-element.31.refs_0_.refs_2_, bf16[512,2048]{1,0:T(8,128)(2,1)S(1)} %get-tuple-element.32.refs_1_.refs_3_, ...), custom_call_target="tpu_custom_call" | custom-call | flops 1073741824 | bytes 557056 | tf_op jit(solution)/shard_map/pallas_call | solution.py:224
  21.8 2.6 %collective-permute-start.2 = (f16[2,4,136,128]{3,2,1,0:T(8,128)(2,1)S(1)}, f16[2,4,136,128]{3,2,1,0:T(8,128)(2,1)S(1)}, u32[]{:S(2)}, u32[]{:S(2)}) collective-permute-start(f16[2,4,136,128]{3,2,1,0:T(8,128)(2,1)S(1)} %convert_element_type.38), channel_id=1, source_target_pairs={{0,2},{1,3},{2,0},{3,1},{4,6},{5,7},{6,4},{7,5},{8,10},{9,11},{10,... | collective-permute-start | bytes 835592 | tf_op jit(solution)/shard_map/ppermute | solution.py:25
  24.3 5.8 %shard_map.68 = f32[2,4,136,128]{3,2,1,0:T(8,128)S(1)} custom-call(s32[1]{0:T(128)} %bitcast.6.at_ref, bf16[512,1024]{1,0:T(8,128)(2,1)S(1)} %get-tuple-element.36.q_ref, bf16[2048,512]{1,0:T(8,128)(2,1)S(1)} %get-tuple-element.26.refs_0_, bf16[512,2048]{1,0:T(8,128)(2,1)S(1)} %get-tuple-element.27.refs_1_, ...), custom_call_target="tpu_custom_call" | custom-call | flops 2147483648 | bytes 557056 | tf_op jit(solution)/shard_map/pallas_call | solution.py:224
  30.2 0.1 collective-permute-start.1
  30.3 5.5 %shard_map.69.own_ref = f32[2,4,136,128]{3,2,1,0:T(8,128)S(1)} custom-call(s32[1]{0:T(128)} %bitcast.at_ref, bf16[512,1024]{1,0:T(8,128)(2,1)S(1)} %get-tuple-element.36.q_ref, bf16[2048,512]{1,0:T(8,128)(2,1)S(1)} %get-tuple-element.26.refs_0_, bf16[512,2048]{1,0:T(8,128)(2,1)S(1)} %get-tuple-element.27.refs_1_, ...), custom_call_target="tpu_custom_call" | custom-call | flops 2147483648 | bytes 557056 | tf_op jit(solution)/shard_map/pallas_call | solution.py:224
  35.8 0.0 collective-permute-done.2
  35.8 0.7 %shard_map.72 = f32[2,4,136,128]{3,2,1,0:T(8,128)S(1)} custom-call(f32[2,4,136,128]{3,2,1,0:T(8,128)S(1)} %shard_map.69.own_ref, f32[2,4,136,128]{3,2,1,0:T(8,128)S(1)} %convert_element_type.39.refs_0_), custom_call_target="tpu_custom_call" | custom-call | flops 2785280 | bytes 1671168 | tf_op jit(solution)/shard_map/pallas_call | solution.py:249
  36.6 2.1 %collective-permute-start.3 = (f16[2,4,136,128]{3,2,1,0:T(8,128)(2,1)S(1)}, f16[2,4,136,128]{3,2,1,0:T(8,128)(2,1)S(1)}, u32[]{:S(2)}, u32[]{:S(2)}) collective-permute-start(f16[2,4,136,128]{3,2,1,0:T(8,128)(2,1)S(1)} %convert_element_type.40), channel_id=1, source_target_pairs={{0,4},{1,5},{2,6},{3,7},{4,0},{5,1},{6,2},{7,3},{8,12},{9,13},{10,... | collective-permute-start | bytes 835592 | tf_op jit(solution)/shard_map/ppermute | solution.py:25
  38.7 5.7 %shard_map.70.own_ref = f32[2,4,136,128]{3,2,1,0:T(8,128)S(1)} custom-call(s32[1]{0:T(128)} %bitcast.at_ref, bf16[512,1024]{1,0:T(8,128)(2,1)S(1)} %get-tuple-element.36.q_ref, bf16[2048,512]{1,0:T(8,128)(2,1)S(1)} %get-tuple-element.26.refs_0_, bf16[512,2048]{1,0:T(8,128)(2,1)S(1)} %get-tuple-element.27.refs_1_, ...), custom_call_target="tpu_custom_call" | custom-call | flops 2147483648 | bytes 557056 | tf_op jit(solution)/shard_map/pallas_call | solution.py:224
  44.4 0.0 collective-permute-done.1
  44.4 0.3 shard_map.71.own_ref
  44.8 0.0 copy-start
  44.8 0.7 %collective-permute-done.3 = f16[2,4,136,128]{3,2,1,0:T(8,128)(2,1)S(1)} collective-permute-done((f16[2,4,136,128]{3,2,1,0:T(8,128)(2,1)S(1)}, f16[2,4,136,128]{3,2,1,0:T(8,128)(2,1)S(1)}, u32[]{:S(2)}, u32[]{:S(2)}) %collective-permute-start.3) | collective-permute-done | bytes 278560 | tf_op jit(solution)/shard_map/ppermute | solution.py:25
  45.5 1.2 %shard_map.73 = (f32[2,136,128]{2,1,0:T(8,128)S(1)}, f32[2,136,128]{2,1,0:T(8,128)S(1)}, f32[2,136,128]{2,1,0:T(8,128)S(1)}, f32[2,136,128]{2,1,0:T(8,128)S(1)}) custom-call(s32[5]{0:T(128)S(1)} %stack.23.at_ref, f32[2,4,136,128]{3,2,1,0:T(8,128)S(1)} %shard_map.71.own_ref, f32[2,4,136,128]{3,2,1,0:T(8,128)S(1)} %convert_element_type.41.refs_0_), custom_call_target="tpu_custom_call" | custom-call | flops 2785280 | bytes 1671168 | tf_op jit(solution)/shard_map/pallas_call | solution.py:270
  46.7 3.9 %collective-permute-start.6 = (f16[2,136,128]{2,1,0:T(8,128)(2,1)S(1)}, f16[2,136,128]{2,1,0:T(8,128)(2,1)S(1)}, u32[]{:S(2)}, u32[]{:S(2)}) collective-permute-start(f16[2,136,128]{2,1,0:T(8,128)(2,1)S(1)} %convert_element_type.46), channel_id=1, source_target_pairs={{0,24},{1,25},{2,26},{3,27},{4,28},{5,29},{6,30},{7,31},{8,16},{9,... | collective-permute-start | bytes 208904 | tf_op jit(solution)/shard_map/ppermute | solution.py:25
  50.6 0.0 collective-permute-start.5
  50.6 0.7 %collective-permute-start.4 = (f16[2,136,128]{2,1,0:T(8,128)(2,1)S(1)}, f16[2,136,128]{2,1,0:T(8,128)(2,1)S(1)}, u32[]{:S(2)}, u32[]{:S(2)}) collective-permute-start(f16[2,136,128]{2,1,0:T(8,128)(2,1)S(1)} %convert_element_type.42), channel_id=1, source_target_pairs={{0,8},{1,9},{2,10},{3,11},{4,12},{5,13},{6,14},{7,15},{8,0},{9,1},... | collective-permute-start | bytes 208904 | tf_op jit(solution)/shard_map/ppermute | solution.py:25
  51.3 2.3 %collective-permute-done.6 = f16[2,136,128]{2,1,0:T(8,128)(2,1)S(1)} collective-permute-done((f16[2,136,128]{2,1,0:T(8,128)(2,1)S(1)}, f16[2,136,128]{2,1,0:T(8,128)(2,1)S(1)}, u32[]{:S(2)}, u32[]{:S(2)}) %collective-permute-start.6) | collective-permute-done | bytes 69664 | tf_op jit(solution)/shard_map/ppermute | solution.py:25
  53.6 2.5 %collective-permute-done.5 = f16[2,136,128]{2,1,0:T(8,128)(2,1)S(1)} collective-permute-done((f16[2,136,128]{2,1,0:T(8,128)(2,1)S(1)}, f16[2,136,128]{2,1,0:T(8,128)(2,1)S(1)}, u32[]{:S(2)}, u32[]{:S(2)}) %collective-permute-start.5) | collective-permute-done | bytes 69664 | tf_op jit(solution)/shard_map/ppermute | solution.py:25
  56.1 0.0 collective-permute-done.4
  56.1 0.2 shard_map.74.refs_0_
  56.4 1.6 %collective-permute-start.8 = (f32[256,128]{1,0:T(8,128)S(1)}, f32[256,128]{1,0:T(8,128)S(1)}, u32[]{:S(2)}, u32[]{:S(2)}) collective-permute-start(f32[256,128]{1,0:T(8,128)S(1)} %shard_map.74.refs_0_), channel_id=1, source_target_pairs={{0,2},{1,3},{2,0},{3,1},{4,6},{5,7},{6,4},{7,5},{8,10},{9,11},{10,... | collective-permute-start | bytes 393224 | tf_op jit(solution)/shard_map/ppermute | solution.py:25
  58.0 0.0 collective-permute-start.7
  58.0 3.4 %collective-permute-done.8.refs_2_ = f32[256,128]{1,0:T(8,128)S(1)} collective-permute-done((f32[256,128]{1,0:T(8,128)S(1)}, f32[256,128]{1,0:T(8,128)S(1)}, u32[]{:S(2)}, u32[]{:S(2)}) %collective-permute-start.8) | collective-permute-done | bytes 131104 | tf_op jit(solution)/shard_map/ppermute | solution.py:25
  61.4 0.0 collective-permute-start.9
  61.4 0.0 collective-permute-done.7.refs_1_
  61.4 1.3 %collective-permute-done.9.refs_3_ = f32[256,128]{1,0:T(8,128)S(1)} collective-permute-done((f32[256,128]{1,0:T(8,128)S(1)}, f32[256,128]{1,0:T(8,128)S(1)}, u32[]{:S(2)}, u32[]{:S(2)}) %collective-permute-start.9) | collective-permute-done | bytes 131104 | tf_op jit(solution)/shard_map/ppermute | solution.py:25
  62.8 0.0 copy-done
  62.8 1.5 %shard_map.75 = bf16[128,256]{1,0:T(8,128)(2,1)} custom-call(s32[5]{0:T(128)S(1)} %stack.23.at_ref, f32[256,128]{1,0:T(8,128)S(1)} %shard_map.74.refs_0_, f32[256,128]{1,0:T(8,128)S(1)} %collective-permute-done.7.refs_1_, f32[256,128]{1,0:T(8,128)S(1)} %collective-permute-done.8.refs_2_, f32[256,128]{1,0:T(8,128)S(1)} %collective-permute-done.9.refs_3_, ...), custom_call_target="tpu_custom_call" | custom-call | flops 67108864 | bytes 524288 | tf_op jit(solution)/shard_map/pallas_call | solution.py:318
  (12 shorter events, 0.3 us)
Async XLA Ops:
  0.0 11.9 %collective-permute-start = (bf16[2048,1024]{1,0:T(8,128)(2,1)}, bf16[2048,1024]{1,0:T(8,128)(2,1)}, u32[]{:S(2)}, u32[]{:S(2)}) collective-permute-start(bf16[2048,1024]{1,0:T(8,128)(2,1)} %t_hbm.1), channel_id=1, source_target_pairs={{0,1},{1,0},{2,3},{3,2},{4,5},{5,4},{6,7},{7,6},{8,9},{9,8},{10,11... | collective-permute-start | bytes 12582920 | tf_op jit(solution)/shard_map/ppermute | solution.py:25
  21.8 14.0 %collective-permute-start.2 = (f16[2,4,136,128]{3,2,1,0:T(8,128)(2,1)S(1)}, f16[2,4,136,128]{3,2,1,0:T(8,128)(2,1)S(1)}, u32[]{:S(2)}, u32[]{:S(2)}) collective-permute-start(f16[2,4,136,128]{3,2,1,0:T(8,128)(2,1)S(1)} %convert_element_type.38), channel_id=1, source_target_pairs={{0,2},{1,3},{2,0},{3,1},{4,6},{5,7},{6,4},{7,5},{8,10},{9,11},{10,... | collective-permute-start | bytes 835592 | tf_op jit(solution)/shard_map/ppermute | solution.py:25
  30.2 14.2 %collective-permute-start.1 = (f16[2,4,136,128]{3,2,1,0:T(8,128)(2,1)S(1)}, f16[2,4,136,128]{3,2,1,0:T(8,128)(2,1)S(1)}, u32[]{:S(2)}, u32[]{:S(2)}) collective-permute-start(f16[2,4,136,128]{3,2,1,0:T(8,128)(2,1)S(1)} %convert_element_type.36), channel_id=1, source_target_pairs={{0,2},{1,3},{2,0},{3,1},{4,6},{5,7},{6,4},{7,5},{8,10},{9,11},{10,... | collective-permute-start | bytes 835592 | tf_op jit(solution)/shard_map/ppermute | solution.py:25
  36.6 8.9 %collective-permute-start.3 = (f16[2,4,136,128]{3,2,1,0:T(8,128)(2,1)S(1)}, f16[2,4,136,128]{3,2,1,0:T(8,128)(2,1)S(1)}, u32[]{:S(2)}, u32[]{:S(2)}) collective-permute-start(f16[2,4,136,128]{3,2,1,0:T(8,128)(2,1)S(1)} %convert_element_type.40), channel_id=1, source_target_pairs={{0,4},{1,5},{2,6},{3,7},{4,0},{5,1},{6,2},{7,3},{8,12},{9,13},{10,... | collective-permute-start | bytes 835592 | tf_op jit(solution)/shard_map/ppermute | solution.py:25
  44.8 18.0 %copy-start = (bf16[1024,256]{1,0:T(8,128)(2,1)S(1)}, bf16[1024,256]{1,0:T(8,128)(2,1)}, u32[]{:S(2)}) copy-start(bf16[1024,256]{1,0:T(8,128)(2,1)} %refs_4_.1) | copy-start | bytes 1572868
  46.7 6.9 %collective-permute-start.6 = (f16[2,136,128]{2,1,0:T(8,128)(2,1)S(1)}, f16[2,136,128]{2,1,0:T(8,128)(2,1)S(1)}, u32[]{:S(2)}, u32[]{:S(2)}) collective-permute-start(f16[2,136,128]{2,1,0:T(8,128)(2,1)S(1)} %convert_element_type.46), channel_id=1, source_target_pairs={{0,24},{1,25},{2,26},{3,27},{4,28},{5,29},{6,30},{7,31},{8,16},{9,... | collective-permute-start | bytes 208904 | tf_op jit(solution)/shard_map/ppermute | solution.py:25
  50.6 5.5 %collective-permute-start.5 = (f16[2,136,128]{2,1,0:T(8,128)(2,1)S(1)}, f16[2,136,128]{2,1,0:T(8,128)(2,1)S(1)}, u32[]{:S(2)}, u32[]{:S(2)}) collective-permute-start(f16[2,136,128]{2,1,0:T(8,128)(2,1)S(1)} %convert_element_type.44), channel_id=1, source_target_pairs={{0,16},{1,17},{2,18},{3,19},{4,20},{5,21},{6,22},{7,23},{8,24},{9,... | collective-permute-start | bytes 208904 | tf_op jit(solution)/shard_map/ppermute | solution.py:25
  50.6 5.5 %collective-permute-start.4 = (f16[2,136,128]{2,1,0:T(8,128)(2,1)S(1)}, f16[2,136,128]{2,1,0:T(8,128)(2,1)S(1)}, u32[]{:S(2)}, u32[]{:S(2)}) collective-permute-start(f16[2,136,128]{2,1,0:T(8,128)(2,1)S(1)} %convert_element_type.42), channel_id=1, source_target_pairs={{0,8},{1,9},{2,10},{3,11},{4,12},{5,13},{6,14},{7,15},{8,0},{9,1},... | collective-permute-start | bytes 208904 | tf_op jit(solution)/shard_map/ppermute | solution.py:25
  56.4 5.0 %collective-permute-start.8 = (f32[256,128]{1,0:T(8,128)S(1)}, f32[256,128]{1,0:T(8,128)S(1)}, u32[]{:S(2)}, u32[]{:S(2)}) collective-permute-start(f32[256,128]{1,0:T(8,128)S(1)} %shard_map.74.refs_0_), channel_id=1, source_target_pairs={{0,2},{1,3},{2,0},{3,1},{4,6},{5,7},{6,4},{7,5},{8,10},{9,11},{10,... | collective-permute-start | bytes 393224 | tf_op jit(solution)/shard_map/ppermute | solution.py:25
  58.0 3.4 %collective-permute-start.7 = (f32[256,128]{1,0:T(8,128)S(1)}, f32[256,128]{1,0:T(8,128)S(1)}, u32[]{:S(2)}, u32[]{:S(2)}) collective-permute-start(f32[256,128]{1,0:T(8,128)S(1)} %shard_map.74.refs_0_), channel_id=1, source_target_pairs={{0,1},{1,0},{2,3},{3,2},{4,5},{5,4},{6,7},{7,6},{8,9},{9,8},{10,11... | collective-permute-start | bytes 393224 | tf_op jit(solution)/shard_map/ppermute | solution.py:25
  61.4 1.3 %collective-permute-start.9 = (f32[256,128]{1,0:T(8,128)S(1)}, f32[256,128]{1,0:T(8,128)S(1)}, u32[]{:S(2)}, u32[]{:S(2)}) collective-permute-start(f32[256,128]{1,0:T(8,128)S(1)} %collective-permute-done.8.refs_2_), channel_id=1, source_target_pairs={{0,1},{1,0},{2,3},{3,2},{4,5},{5,4},{6,7},{7,6},{8,9},{9,8},{10,11... | collective-permute-start | bytes 393224 | tf_op jit(solution)/shard_map/ppermute | solution.py:25

commit v6 on v5

--- a/solution.py
+++ b/solution.py
@@ -33,6 +33,8 @@
     near, core = at_ref[1], at_ref[3]
     n = t_ref.shape[0]
     cols = k_ref.shape[1]
+    size = cols // (H // CORES)
+    coef = math.log2(math.e) / math.sqrt(size)
     half = l_ref.shape[1] * l_ref.shape[2]
     columns = pl.ds(pl.multiple_of(core * cols, cols), cols)
     parts = [slice(0, n // 4), slice(n // 4, n // 2), slice(n // 2, n)]
@@ -64,7 +66,13 @@
     project_vals(parts[2])
     wait(5, 6, 7)
     for h in range(NEAR):
-        q_ref[:, h * half : (h + 1) * half] = dot(l_ref[h].reshape(half, -1), wq_ref[...]).T
+        query = dot(l_ref[h].reshape(half, -1), wq_ref[...]).T.astype(jnp.float32) * coef
+        high = query.astype(jnp.bfloat16)
+        low = (query - high.astype(jnp.float32)).astype(jnp.bfloat16)
+        for j in range(cols // size):
+            rows = slice(j * size, (j + 1) * size)
+            q_ref[2 * j * size : (2 * j + 1) * size, h * half : (h + 1) * half] = high[rows]
+            q_ref[(2 * j + 1) * size : (2 * j + 2) * size, h * half : (h + 1) * half] = low[rows]
 
 
 def project_own(at, tokens, latents, w_query, w_key, w_value):
@@ -73,7 +81,7 @@
     m = n_far * NEAR * block
     return pl.pallas_call(
         project_own_kernel,
-        out_shape=[jax.ShapeDtypeStruct(s, jnp.bfloat16) for s in ((n, cols), (cols, n), (cols, m), (d, cols), (d, cols))],
+        out_shape=[jax.ShapeDtypeStruct(s, jnp.bfloat16) for s in ((n, cols), (cols, n), (2 * cols, m), (d, cols), (d, cols))],
         in_specs=[SMEM] + [HBM] * 5,
         out_specs=[VMEM] * 5,
         scratch_shapes=[
@@ -82,7 +90,7 @@
             pltpu.VMEM((NEAR, n_far, block, d), jnp.bfloat16),
             pltpu.SemaphoreType.DMA((8,)),
         ],
-        compiler_params=pltpu.CompilerParams(vmem_limit_bytes=46 * 2**20),
+        compiler_params=pltpu.CompilerParams(vmem_limit_bytes=45 * 2**20),
         cost_estimate=pl.CostEstimate(
             flops=(4 * n + 2 * m) * d * cols, bytes_accessed=2 * (n * d + m * d + 3 * d * cols), transcendentals=0
         ),
@@ -179,7 +187,6 @@
     tokens, lanes = s0.shape
     heads, n_far, rows, block = o_ref.shape
     size = rows - EXTRA
-    coef = math.log2(math.e) / math.sqrt(size)
     slots = (s0, s1)
     ones = jnp.ones((16, chunk), jnp.bfloat16)
     items = [(j, b) for j in range(heads) for b in range(blocks)]
@@ -195,19 +202,20 @@
             part = slice(c * chunk, (c + 1) * chunk)
             if i < len(items):
                 j, b = items[i]
-                q = q_ref[columns(j), half * lanes : (half + 1) * lanes]
-                s = jnp.dot(kv[2 * b][part, columns(j)], q, preferred_element_type=jnp.float32)
+                q = q_ref[pl.ds(pl.multiple_of((at_ref[0] * heads + j) * 2 * size, 2 * size), 2 * size), half * lanes : (half + 1) * lanes]
+                k = kv[2 * b][part, columns(j)]
+                s = jnp.dot(jnp.concatenate([k, k], axis=1), q, preferred_element_type=jnp.float32)
                 now[part, :] = s
                 high = jnp.max(s.reshape(chunk // 8, 8, lanes), axis=0)
                 top = high if top is None else jnp.maximum(top, high)
             if i > 0:
                 j, b = items[i - 1]
-                w = jnp.exp2((before[part, :] - peak) * coef).astype(jnp.bfloat16)
+                w = jnp.exp2(before[part, :] - peak).astype(jnp.bfloat16)
                 v = jnp.concatenate([kv[2 * b + 1][columns(j), part], ones], axis=0)
                 acc = acc + jnp.dot(v, w, preferred_element_type=jnp.float32)
         if i > 0:
             j = items[i - 1][0]
-            done.append((acc[:size], acc[size : size + 1], peak * coef))
+            done.append((acc[:size], acc[size : size + 1], peak))
             if len(done) == blocks:
                 for f in range(n_far):
                     at = slice(f * block, (f + 1) * block)

time: 64.5 us -> 64 us (level)
  Pallas kernels: 42.1 us -> 41.3 us
    pallas_call x5, Pallas kernels: 23.2 us -> 22.3 us  [attend(): pl.pallas_call(functools.partial(attend_kernel, chunk, half, len(blocks),...]
  transfers between devices with their start and end apart: 10 -> 10, of which waited for: 5 -> 5; matrix products, arithmetic and copies ran while one was open for 0% -> 0% of each run, Pallas kernels for 46% -> 45%
where the time goes in v6:
time: 64 us; the launch traced here: 63.9 us
  Pallas kernels  41.3 us (65%)
  starting transfers between devices  11.3 us (18%)
  waiting for transfers between devices  10.6 us (17%)
    pallas_call x5, Pallas kernels, attend(): pl.pallas_call(functools.partial(attend_kernel, chunk, half, len(blocks),...  22.3 us
    ppermute x10, starting transfers between devices, xor_permute(): return lax.ppermute(value, AXES, [(i, i ^ step) for i in range(n)])  11.3 us
    ppermute x10, waiting for transfers between devices, xor_permute(): return lax.ppermute(value, AXES, [(i, i ^ step) for i in range(n)])  10.6 us
    pallas_call x1, Pallas kernels, project_own(): pl.pallas_call(project_own_kernel, out_shape=[jax.ShapeDtypeStruct(s, jnp...  8.68 us
    pallas_call x1, Pallas kernels, project(): pl.pallas_call(project_kernel, out_shape=[jax.ShapeDtypeStruct(s, jnp.bfl...  6.38 us
    pallas_call x1, Pallas kernels, finish(): pl.pallas_call(finish_kernel, out_shape=jax.ShapeDtypeStruct((block, w_ou...  1.55 us
  transfers between devices with their start and end apart: 10, of which 5 were waited for; matrix products, arithmetic and copies ran while one was open for 0% of the time, Pallas kernels for 45%

profile of v6, /device:TPU:0, one launch (start us, length us, event | category | flops | bytes accessed | tf_op | source)
XLA Modules:
  0.0 63.9 jit_solution(3820432128882593706)
XLA Ops:
  0.0 0.5 collective-permute-start
  0.5 0.1 stack.23.at_ref
  0.5 8.7 %shard_map.64 = (bf16[2048,512]{1,0:T(8,128)(2,1)S(1)}, bf16[512,2048]{1,0:T(8,128)(2,1)S(1)}, bf16[1024,1024]{1,0:T(8,128)(2,1)S(1)}, bf16[1024,512]{1,0:T(8,128)(2,1)S(1)}, bf16[1024,512]{1,0:T(8,128)(2,1)S(1)}) custom-call(s32[5]{0:T(128)S(1)} %stack.23.at_ref, bf16[2048,1024]{1,0:T(8,128)(2,1)} %t_hbm.1, bf16[4,2,128,1024]{3,2,1,0:T(8,128)(2,1)} %bitcast.7, ...), custom_call_target="tpu_custom_call" | custom-call | flops 5368709120 | bytes 9437184 | tf_op jit(solution)/shard_map/pallas_call | solution.py:82
  9.2 2.8 %shard_map.65.refs_2_ = f32[2,4,136,128]{3,2,1,0:T(8,128)S(1)} custom-call(s32[1]{0:T(128)} %bitcast.6.at_ref, bf16[1024,1024]{1,0:T(8,128)(2,1)S(1)} %get-tuple-element.36.q_ref, bf16[2048,512]{1,0:T(8,128)(2,1)S(1)} %get-tuple-element.26.refs_0_, bf16[512,2048]{1,0:T(8,128)(2,1)S(1)} %get-tuple-element.27.refs_1_), custom_call_target="tpu_custom_call" | custom-call | flops 1073741824 | bytes 557056 | tf_op jit(solution)/shard_map/pallas_call | solution.py:232
  12.1 0.0 collective-permute-done.t_hbm
  12.1 6.4 %shard_map.66 = (bf16[2048,512]{1,0:T(8,128)(2,1)S(1)}, bf16[512,2048]{1,0:T(8,128)(2,1)S(1)}) custom-call(bf16[2048,1024]{1,0:T(8,128)(2,1)} %collective-permute-done.t_hbm, bf16[1024,512]{1,0:T(8,128)(2,1)S(1)} %get-tuple-element.29.wk_ref, bf16[1024,512]{1,0:T(8,128)(2,1)S(1)} %get-tuple-element.30.wv_ref), custom_call_target="tpu_custom_call" | custom-call | flops 4294967296 | bytes 6291456 | tf_op jit(solution)/shard_map/pallas_call | solution.py:114
  18.5 3.4 %shard_map.67 = f32[2,4,136,128]{3,2,1,0:T(8,128)S(1)} custom-call(s32[1]{0:T(128)} %bitcast.6.at_ref, bf16[1024,1024]{1,0:T(8,128)(2,1)S(1)} %get-tuple-element.36.q_ref, bf16[2048,512]{1,0:T(8,128)(2,1)S(1)} %get-tuple-element.31.refs_0_.refs_2_, bf16[512,2048]{1,0:T(8,128)(2,1)S(1)} %get-tuple-element.32.refs_1_.refs_3_, ...), custom_call_target="tpu_custom_call" | custom-call | flops 1073741824 | bytes 557056 | tf_op jit(solution)/shard_map/pallas_call | solution.py:232
  22.0 2.6 %collective-permute-start.2 = (f16[2,4,136,128]{3,2,1,0:T(8,128)(2,1)S(1)}, f16[2,4,136,128]{3,2,1,0:T(8,128)(2,1)S(1)}, u32[]{:S(2)}, u32[]{:S(2)}) collective-permute-start(f16[2,4,136,128]{3,2,1,0:T(8,128)(2,1)S(1)} %convert_element_type.38), channel_id=1, source_target_pairs={{0,2},{1,3},{2,0},{3,1},{4,6},{5,7},{6,4},{7,5},{8,10},{9,11},{10,... | collective-permute-start | bytes 835592 | tf_op jit(solution)/shard_map/ppermute | solution.py:25
  24.5 5.4 %shard_map.68 = f32[2,4,136,128]{3,2,1,0:T(8,128)S(1)} custom-call(s32[1]{0:T(128)} %bitcast.6.at_ref, bf16[1024,1024]{1,0:T(8,128)(2,1)S(1)} %get-tuple-element.36.q_ref, bf16[2048,512]{1,0:T(8,128)(2,1)S(1)} %get-tuple-element.26.refs_0_, bf16[512,2048]{1,0:T(8,128)(2,1)S(1)} %get-tuple-element.27.refs_1_, ...), custom_call_target="tpu_custom_call" | custom-call | flops 2147483648 | bytes 557056 | tf_op jit(solution)/shard_map/pallas_call | solution.py:232
  30.0 0.1 collective-permute-start.1
  30.1 5.2 %shard_map.69.own_ref = f32[2,4,136,128]{3,2,1,0:T(8,128)S(1)} custom-call(s32[1]{0:T(128)} %bitcast.at_ref, bf16[1024,1024]{1,0:T(8,128)(2,1)S(1)} %get-tuple-element.36.q_ref, bf16[2048,512]{1,0:T(8,128)(2,1)S(1)} %get-tuple-element.26.refs_0_, bf16[512,2048]{1,0:T(8,128)(2,1)S(1)} %get-tuple-element.27.refs_1_, ...), custom_call_target="tpu_custom_call" | custom-call | flops 2147483648 | bytes 557056 | tf_op jit(solution)/shard_map/pallas_call | solution.py:232
  35.3 0.0 collective-permute-done.2
  35.4 0.7 %shard_map.72 = f32[2,4,136,128]{3,2,1,0:T(8,128)S(1)} custom-call(f32[2,4,136,128]{3,2,1,0:T(8,128)S(1)} %shard_map.69.own_ref, f32[2,4,136,128]{3,2,1,0:T(8,128)S(1)} %convert_element_type.39.refs_0_), custom_call_target="tpu_custom_call" | custom-call | flops 2785280 | bytes 1671168 | tf_op jit(solution)/shard_map/pallas_call | solution.py:257
  36.1 2.1 %collective-permute-start.3 = (f16[2,4,136,128]{3,2,1,0:T(8,128)(2,1)S(1)}, f16[2,4,136,128]{3,2,1,0:T(8,128)(2,1)S(1)}, u32[]{:S(2)}, u32[]{:S(2)}) collective-permute-start(f16[2,4,136,128]{3,2,1,0:T(8,128)(2,1)S(1)} %convert_element_type.40), channel_id=1, source_target_pairs={{0,4},{1,5},{2,6},{3,7},{4,0},{5,1},{6,2},{7,3},{8,12},{9,13},{10,... | collective-permute-start | bytes 835592 | tf_op jit(solution)/shard_map/ppermute | solution.py:25
  38.2 5.4 %shard_map.70.own_ref = f32[2,4,136,128]{3,2,1,0:T(8,128)S(1)} custom-call(s32[1]{0:T(128)} %bitcast.at_ref, bf16[1024,1024]{1,0:T(8,128)(2,1)S(1)} %get-tuple-element.36.q_ref, bf16[2048,512]{1,0:T(8,128)(2,1)S(1)} %get-tuple-element.26.refs_0_, bf16[512,2048]{1,0:T(8,128)(2,1)S(1)} %get-tuple-element.27.refs_1_, ...), custom_call_target="tpu_custom_call" | custom-call | flops 2147483648 | bytes 557056 | tf_op jit(solution)/shard_map/pallas_call | solution.py:232
  43.6 0.0 collective-permute-done.1
  43.7 0.3 shard_map.71.own_ref
  44.0 0.0 copy-start
  44.0 1.0 %collective-permute-done.3 = f16[2,4,136,128]{3,2,1,0:T(8,128)(2,1)S(1)} collective-permute-done((f16[2,4,136,128]{3,2,1,0:T(8,128)(2,1)S(1)}, f16[2,4,136,128]{3,2,1,0:T(8,128)(2,1)S(1)}, u32[]{:S(2)}, u32[]{:S(2)}) %collective-permute-start.3) | collective-permute-done | bytes 278560 | tf_op jit(solution)/shard_map/ppermute | solution.py:25
  45.0 1.2 %shard_map.73 = (f32[2,136,128]{2,1,0:T(8,128)S(1)}, f32[2,136,128]{2,1,0:T(8,128)S(1)}, f32[2,136,128]{2,1,0:T(8,128)S(1)}, f32[2,136,128]{2,1,0:T(8,128)S(1)}) custom-call(s32[5]{0:T(128)S(1)} %stack.23.at_ref, f32[2,4,136,128]{3,2,1,0:T(8,128)S(1)} %shard_map.71.own_ref, f32[2,4,136,128]{3,2,1,0:T(8,128)S(1)} %convert_element_type.41.refs_0_), custom_call_target="tpu_custom_call" | custom-call | flops 2785280 | bytes 1671168 | tf_op jit(solution)/shard_map/pallas_call | solution.py:278
  46.3 3.9 %collective-permute-start.6 = (f16[2,136,128]{2,1,0:T(8,128)(2,1)S(1)}, f16[2,136,128]{2,1,0:T(8,128)(2,1)S(1)}, u32[]{:S(2)}, u32[]{:S(2)}) collective-permute-start(f16[2,136,128]{2,1,0:T(8,128)(2,1)S(1)} %convert_element_type.46), channel_id=1, source_target_pairs={{0,24},{1,25},{2,26},{3,27},{4,28},{5,29},{6,30},{7,31},{8,16},{9,... | collective-permute-start | bytes 208904 | tf_op jit(solution)/shard_map/ppermute | solution.py:25
  50.1 0.0 collective-permute-start.5
  50.1 0.7 %collective-permute-start.4 = (f16[2,136,128]{2,1,0:T(8,128)(2,1)S(1)}, f16[2,136,128]{2,1,0:T(8,128)(2,1)S(1)}, u32[]{:S(2)}, u32[]{:S(2)}) collective-permute-start(f16[2,136,128]{2,1,0:T(8,128)(2,1)S(1)} %convert_element_type.42), channel_id=1, source_target_pairs={{0,8},{1,9},{2,10},{3,11},{4,12},{5,13},{6,14},{7,15},{8,0},{9,1},... | collective-permute-start | bytes 208904 | tf_op jit(solution)/shard_map/ppermute | solution.py:25
  50.8 2.2 %collective-permute-done.6 = f16[2,136,128]{2,1,0:T(8,128)(2,1)S(1)} collective-permute-done((f16[2,136,128]{2,1,0:T(8,128)(2,1)S(1)}, f16[2,136,128]{2,1,0:T(8,128)(2,1)S(1)}, u32[]{:S(2)}, u32[]{:S(2)}) %collective-permute-start.6) | collective-permute-done | bytes 69664 | tf_op jit(solution)/shard_map/ppermute | solution.py:25
  53.1 2.5 %collective-permute-done.5 = f16[2,136,128]{2,1,0:T(8,128)(2,1)S(1)} collective-permute-done((f16[2,136,128]{2,1,0:T(8,128)(2,1)S(1)}, f16[2,136,128]{2,1,0:T(8,128)(2,1)S(1)}, u32[]{:S(2)}, u32[]{:S(2)}) %collective-permute-start.5) | collective-permute-done | bytes 69664 | tf_op jit(solution)/shard_map/ppermute | solution.py:25
  55.6 0.0 collective-permute-done.4
  55.7 0.2 shard_map.74.refs_0_
  55.9 1.5 %collective-permute-start.8 = (f32[256,128]{1,0:T(8,128)S(1)}, f32[256,128]{1,0:T(8,128)S(1)}, u32[]{:S(2)}, u32[]{:S(2)}) collective-permute-start(f32[256,128]{1,0:T(8,128)S(1)} %shard_map.74.refs_0_), channel_id=1, source_target_pairs={{0,2},{1,3},{2,0},{3,1},{4,6},{5,7},{6,4},{7,5},{8,10},{9,11},{10,... | collective-permute-start | bytes 393224 | tf_op jit(solution)/shard_map/ppermute | solution.py:25
  57.4 0.0 collective-permute-start.7
  57.4 3.5 %collective-permute-done.8.refs_2_ = f32[256,128]{1,0:T(8,128)S(1)} collective-permute-done((f32[256,128]{1,0:T(8,128)S(1)}, f32[256,128]{1,0:T(8,128)S(1)}, u32[]{:S(2)}, u32[]{:S(2)}) %collective-permute-start.8) | collective-permute-done | bytes 131104 | tf_op jit(solution)/shard_map/ppermute | solution.py:25
  61.0 0.0 collective-permute-start.9
  61.0 0.0 collective-permute-done.7.refs_1_
  61.0 1.3 %collective-permute-done.9.refs_3_ = f32[256,128]{1,0:T(8,128)S(1)} collective-permute-done((f32[256,128]{1,0:T(8,128)S(1)}, f32[256,128]{1,0:T(8,128)S(1)}, u32[]{:S(2)}, u32[]{:S(2)}) %collective-permute-start.9) | collective-permute-done | bytes 131104 | tf_op jit(solution)/shard_map/ppermute | solution.py:25
  62.3 0.0 copy-done
  62.3 1.5 %shard_map.75 = bf16[128,256]{1,0:T(8,128)(2,1)} custom-call(s32[5]{0:T(128)S(1)} %stack.23.at_ref, f32[256,128]{1,0:T(8,128)S(1)} %shard_map.74.refs_0_, f32[256,128]{1,0:T(8,128)S(1)} %collective-permute-done.7.refs_1_, f32[256,128]{1,0:T(8,128)S(1)} %collective-permute-done.8.refs_2_, f32[256,128]{1,0:T(8,128)S(1)} %collective-permute-done.9.refs_3_, ...), custom_call_target="tpu_custom_call" | custom-call | flops 67108864 | bytes 524288 | tf_op jit(solution)/shard_map/pallas_call | solution.py:326
  (12 shorter events, 0.3 us)
Async XLA Ops:
  0.0 12.1 %collective-permute-start = (bf16[2048,1024]{1,0:T(8,128)(2,1)}, bf16[2048,1024]{1,0:T(8,128)(2,1)}, u32[]{:S(2)}, u32[]{:S(2)}) collective-permute-start(bf16[2048,1024]{1,0:T(8,128)(2,1)} %t_hbm.1), channel_id=1, source_target_pairs={{0,1},{1,0},{2,3},{3,2},{4,5},{5,4},{6,7},{7,6},{8,9},{9,8},{10,11... | collective-permute-start | bytes 12582920 | tf_op jit(solution)/shard_map/ppermute | solution.py:25
  22.0 13.3 %collective-permute-start.2 = (f16[2,4,136,128]{3,2,1,0:T(8,128)(2,1)S(1)}, f16[2,4,136,128]{3,2,1,0:T(8,128)(2,1)S(1)}, u32[]{:S(2)}, u32[]{:S(2)}) collective-permute-start(f16[2,4,136,128]{3,2,1,0:T(8,128)(2,1)S(1)} %convert_element_type.38), channel_id=1, source_target_pairs={{0,2},{1,3},{2,0},{3,1},{4,6},{5,7},{6,4},{7,5},{8,10},{9,11},{10,... | collective-permute-start | bytes 835592 | tf_op jit(solution)/shard_map/ppermute | solution.py:25
  30.0 13.6 %collective-permute-start.1 = (f16[2,4,136,128]{3,2,1,0:T(8,128)(2,1)S(1)}, f16[2,4,136,128]{3,2,1,0:T(8,128)(2,1)S(1)}, u32[]{:S(2)}, u32[]{:S(2)}) collective-permute-start(f16[2,4,136,128]{3,2,1,0:T(8,128)(2,1)S(1)} %convert_element_type.36), channel_id=1, source_target_pairs={{0,2},{1,3},{2,0},{3,1},{4,6},{5,7},{6,4},{7,5},{8,10},{9,11},{10,... | collective-permute-start | bytes 835592 | tf_op jit(solution)/shard_map/ppermute | solution.py:25
  36.1 8.9 %collective-permute-start.3 = (f16[2,4,136,128]{3,2,1,0:T(8,128)(2,1)S(1)}, f16[2,4,136,128]{3,2,1,0:T(8,128)(2,1)S(1)}, u32[]{:S(2)}, u32[]{:S(2)}) collective-permute-start(f16[2,4,136,128]{3,2,1,0:T(8,128)(2,1)S(1)} %convert_element_type.40), channel_id=1, source_target_pairs={{0,4},{1,5},{2,6},{3,7},{4,0},{5,1},{6,2},{7,3},{8,12},{9,13},{10,... | collective-permute-start | bytes 835592 | tf_op jit(solution)/shard_map/ppermute | solution.py:25
  44.0 18.3 %copy-start = (bf16[1024,256]{1,0:T(8,128)(2,1)S(1)}, bf16[1024,256]{1,0:T(8,128)(2,1)}, u32[]{:S(2)}) copy-start(bf16[1024,256]{1,0:T(8,128)(2,1)} %refs_4_.1) | copy-start | bytes 1572868
  46.3 6.8 %collective-permute-start.6 = (f16[2,136,128]{2,1,0:T(8,128)(2,1)S(1)}, f16[2,136,128]{2,1,0:T(8,128)(2,1)S(1)}, u32[]{:S(2)}, u32[]{:S(2)}) collective-permute-start(f16[2,136,128]{2,1,0:T(8,128)(2,1)S(1)} %convert_element_type.46), channel_id=1, source_target_pairs={{0,24},{1,25},{2,26},{3,27},{4,28},{5,29},{6,30},{7,31},{8,16},{9,... | collective-permute-start | bytes 208904 | tf_op jit(solution)/shard_map/ppermute | solution.py:25
  50.1 5.5 %collective-permute-start.5 = (f16[2,136,128]{2,1,0:T(8,128)(2,1)S(1)}, f16[2,136,128]{2,1,0:T(8,128)(2,1)S(1)}, u32[]{:S(2)}, u32[]{:S(2)}) collective-permute-start(f16[2,136,128]{2,1,0:T(8,128)(2,1)S(1)} %convert_element_type.44), channel_id=1, source_target_pairs={{0,16},{1,17},{2,18},{3,19},{4,20},{5,21},{6,22},{7,23},{8,24},{9,... | collective-permute-start | bytes 208904 | tf_op jit(solution)/shard_map/ppermute | solution.py:25
  50.1 5.5 %collective-permute-start.4 = (f16[2,136,128]{2,1,0:T(8,128)(2,1)S(1)}, f16[2,136,128]{2,1,0:T(8,128)(2,1)S(1)}, u32[]{:S(2)}, u32[]{:S(2)}) collective-permute-start(f16[2,136,128]{2,1,0:T(8,128)(2,1)S(1)} %convert_element_type.42), channel_id=1, source_target_pairs={{0,8},{1,9},{2,10},{3,11},{4,12},{5,13},{6,14},{7,15},{8,0},{9,1},... | collective-permute-start | bytes 208904 | tf_op jit(solution)/shard_map/ppermute | solution.py:25
  55.9 5.0 %collective-permute-start.8 = (f32[256,128]{1,0:T(8,128)S(1)}, f32[256,128]{1,0:T(8,128)S(1)}, u32[]{:S(2)}, u32[]{:S(2)}) collective-permute-start(f32[256,128]{1,0:T(8,128)S(1)} %shard_map.74.refs_0_), channel_id=1, source_target_pairs={{0,2},{1,3},{2,0},{3,1},{4,6},{5,7},{6,4},{7,5},{8,10},{9,11},{10,... | collective-permute-start | bytes 393224 | tf_op jit(solution)/shard_map/ppermute | solution.py:25
  57.4 3.5 %collective-permute-start.7 = (f32[256,128]{1,0:T(8,128)S(1)}, f32[256,128]{1,0:T(8,128)S(1)}, u32[]{:S(2)}, u32[]{:S(2)}) collective-permute-start(f32[256,128]{1,0:T(8,128)S(1)} %shard_map.74.refs_0_), channel_id=1, source_target_pairs={{0,1},{1,0},{2,3},{3,2},{4,5},{5,4},{6,7},{7,6},{8,9},{9,8},{10,11... | collective-permute-start | bytes 393224 | tf_op jit(solution)/shard_map/ppermute | solution.py:25
  61.0 1.3 %collective-permute-start.9 = (f32[256,128]{1,0:T(8,128)S(1)}, f32[256,128]{1,0:T(8,128)S(1)}, u32[]{:S(2)}, u32[]{:S(2)}) collective-permute-start(f32[256,128]{1,0:T(8,128)S(1)} %collective-permute-done.8.refs_2_), channel_id=1, source_target_pairs={{0,1},{1,0},{2,3},{3,2},{4,5},{5,4},{6,7},{7,6},{8,9},{9,8},{10,11... | collective-permute-start | bytes 393224 | tf_op jit(solution)/shard_map/ppermute | solution.py:25

commit v7 on v5

--- a/solution.py
+++ b/solution.py
@@ -299,18 +299,19 @@
 
 
 def finish_kernel(at_ref, *refs):
-    pieces, (w_ref, o_ref, normed) = refs[:-3], refs[-3:]
+    pieces, (w_ref, o_ref) = refs[:-2], refs[-2:]
     feats, me = pieces[0].shape[0], at_ref[2]
     width = feats * len(pieces)
     squares = functools.reduce(lambda a, b: a + b, [jnp.square(p[...]) for p in pieces])
     scale = lax.rsqrt(jnp.sum(squares, axis=0, keepdims=True) * (1.0 / width) + 1e-06)
+    out = jnp.zeros(o_ref.shape, jnp.float32)
     for s, piece in enumerate(pieces):
         owner = me ^ s
         at = owner % CORES * (width // CORES) + owner // CORES * feats
-        normed[pl.ds(pl.multiple_of(at, feats), feats), :] = (piece[...] * scale).astype(jnp.bfloat16)
-    o_ref[...] = lax.dot_general(
-        normed[...], w_ref[...], (((0,), (0,)), ((), ())), preferred_element_type=jnp.float32
-    ).astype(jnp.bfloat16)
+        normed = (piece[...] * scale).astype(jnp.bfloat16)
+        rows = w_ref[pl.ds(pl.multiple_of(at, feats), feats), :]
+        out = out + lax.dot_general(normed, rows, (((0,), (0,)), ((), ())), preferred_element_type=jnp.float32)
+    o_ref[...] = out.astype(jnp.bfloat16)
 
 
 def finish(at, pieces, w_out):
@@ -320,7 +321,6 @@
         out_shape=jax.ShapeDtypeStruct((block, w_out.shape[1]), jnp.bfloat16),
         in_specs=[SMEM] + [VMEM] * (len(pieces) + 1),
         out_specs=VMEM,
-        scratch_shapes=[pltpu.VMEM((w_out.shape[0], block), jnp.bfloat16)],
         compiler_params=PARAMS,
         cost_estimate=pl.CostEstimate(flops=2 * block * w_out.size, bytes_accessed=2 * w_out.size, transcendentals=0),
     )(at, *pieces, w_out)

time: 64.5 us -> 64.4 us (level)
  no operation moved by 1% of the time
where the time goes in v7:
time: 64.4 us; the launch traced here: 64.3 us
  Pallas kernels  42.1 us (65%)
  starting transfers between devices  11.4 us (18%)
  waiting for transfers between devices  10.2 us (16%)
    pallas_call x5, Pallas kernels, attend(): pl.pallas_call(functools.partial(attend_kernel, chunk, half, len(blocks),...  23.2 us
    ppermute x10, starting transfers between devices, xor_permute(): return lax.ppermute(value, AXES, [(i, i ^ step) for i in range(n)])  11.4 us
    ppermute x10, waiting for transfers between devices, xor_permute(): return lax.ppermute(value, AXES, [(i, i ^ step) for i in range(n)])  10.2 us
    pallas_call x1, Pallas kernels, project_own(): pl.pallas_call(project_own_kernel, out_shape=[jax.ShapeDtypeStruct(s, jnp...  8.54 us
    pallas_call x1, Pallas kernels, project(): pl.pallas_call(project_kernel, out_shape=[jax.ShapeDtypeStruct(s, jnp.bfl...  6.39 us
    pallas_call x1, Pallas kernels, finish(): pl.pallas_call(finish_kernel, out_shape=jax.ShapeDtypeStruct((block, w_ou...  1.51 us
  transfers between devices with their start and end apart: 10, of which 5 were waited for; matrix products, arithmetic and copies ran while one was open for 0% of the time, Pallas kernels for 46%

profile of v7, /device:TPU:0, one launch (start us, length us, event | category | flops | bytes accessed | tf_op | source)
XLA Modules:
  0.0 64.3 jit_solution(17065218376845489301)
XLA Ops:
  0.0 0.5 collective-permute-start
  0.5 0.1 stack.23.at_ref
  0.5 8.5 %shard_map.64 = (bf16[2048,512]{1,0:T(8,128)(2,1)S(1)}, bf16[512,2048]{1,0:T(8,128)(2,1)S(1)}, bf16[512,1024]{1,0:T(8,128)(2,1)S(1)}, bf16[1024,512]{1,0:T(8,128)(2,1)S(1)}, bf16[1024,512]{1,0:T(8,128)(2,1)S(1)}) custom-call(s32[5]{0:T(128)S(1)} %stack.23.at_ref, bf16[2048,1024]{1,0:T(8,128)(2,1)} %t_hbm.1, bf16[4,2,128,1024]{3,2,1,0:T(8,128)(2,1)} %bitcast.7, ...), custom_call_target="tpu_custom_call" | custom-call | flops 5368709120 | bytes 9437184 | tf_op jit(solution)/shard_map/pallas_call | solution.py:74
  9.1 2.8 %shard_map.65.refs_2_ = f32[2,4,136,128]{3,2,1,0:T(8,128)S(1)} custom-call(s32[1]{0:T(128)} %bitcast.6.at_ref, bf16[512,1024]{1,0:T(8,128)(2,1)S(1)} %get-tuple-element.36.q_ref, bf16[2048,512]{1,0:T(8,128)(2,1)S(1)} %get-tuple-element.26.refs_0_, bf16[512,2048]{1,0:T(8,128)(2,1)S(1)} %get-tuple-element.27.refs_1_), custom_call_target="tpu_custom_call" | custom-call | flops 1073741824 | bytes 557056 | tf_op jit(solution)/shard_map/pallas_call | solution.py:224
  11.9 0.0 collective-permute-done.t_hbm
  11.9 6.4 %shard_map.66 = (bf16[2048,512]{1,0:T(8,128)(2,1)S(1)}, bf16[512,2048]{1,0:T(8,128)(2,1)S(1)}) custom-call(bf16[2048,1024]{1,0:T(8,128)(2,1)} %collective-permute-done.t_hbm, bf16[1024,512]{1,0:T(8,128)(2,1)S(1)} %get-tuple-element.29.wk_ref, bf16[1024,512]{1,0:T(8,128)(2,1)S(1)} %get-tuple-element.30.wv_ref), custom_call_target="tpu_custom_call" | custom-call | flops 4294967296 | bytes 6291456 | tf_op jit(solution)/shard_map/pallas_call | solution.py:106
  18.3 3.4 %shard_map.67 = f32[2,4,136,128]{3,2,1,0:T(8,128)S(1)} custom-call(s32[1]{0:T(128)} %bitcast.6.at_ref, bf16[512,1024]{1,0:T(8,128)(2,1)S(1)} %get-tuple-element.36.q_ref, bf16[2048,512]{1,0:T(8,128)(2,1)S(1)} %get-tuple-element.31.refs_0_.refs_2_, bf16[512,2048]{1,0:T(8,128)(2,1)S(1)} %get-tuple-element.32.refs_1_.refs_3_, ...), custom_call_target="tpu_custom_call" | custom-call | flops 1073741824 | bytes 557056 | tf_op jit(solution)/shard_map/pallas_call | solution.py:224
  21.8 2.6 %collective-permute-start.2 = (f16[2,4,136,128]{3,2,1,0:T(8,128)(2,1)S(1)}, f16[2,4,136,128]{3,2,1,0:T(8,128)(2,1)S(1)}, u32[]{:S(2)}, u32[]{:S(2)}) collective-permute-start(f16[2,4,136,128]{3,2,1,0:T(8,128)(2,1)S(1)} %convert_element_type.38), channel_id=1, source_target_pairs={{0,2},{1,3},{2,0},{3,1},{4,6},{5,7},{6,4},{7,5},{8,10},{9,11},{10,... | collective-permute-start | bytes 835592 | tf_op jit(solution)/shard_map/ppermute | solution.py:25
  24.3 5.8 %shard_map.68 = f32[2,4,136,128]{3,2,1,0:T(8,128)S(1)} custom-call(s32[1]{0:T(128)} %bitcast.6.at_ref, bf16[512,1024]{1,0:T(8,128)(2,1)S(1)} %get-tuple-element.36.q_ref, bf16[2048,512]{1,0:T(8,128)(2,1)S(1)} %get-tuple-element.26.refs_0_, bf16[512,2048]{1,0:T(8,128)(2,1)S(1)} %get-tuple-element.27.refs_1_, ...), custom_call_target="tpu_custom_call" | custom-call | flops 2147483648 | bytes 557056 | tf_op jit(solution)/shard_map/pallas_call | solution.py:224
  30.2 0.1 collective-permute-start.1
  30.3 5.5 %shard_map.69.own_ref = f32[2,4,136,128]{3,2,1,0:T(8,128)S(1)} custom-call(s32[1]{0:T(128)} %bitcast.at_ref, bf16[512,1024]{1,0:T(8,128)(2,1)S(1)} %get-tuple-element.36.q_ref, bf16[2048,512]{1,0:T(8,128)(2,1)S(1)} %get-tuple-element.26.refs_0_, bf16[512,2048]{1,0:T(8,128)(2,1)S(1)} %get-tuple-element.27.refs_1_, ...), custom_call_target="tpu_custom_call" | custom-call | flops 2147483648 | bytes 557056 | tf_op jit(solution)/shard_map/pallas_call | solution.py:224
  35.8 0.0 collective-permute-done.2
  35.8 0.7 %shard_map.72 = f32[2,4,136,128]{3,2,1,0:T(8,128)S(1)} custom-call(f32[2,4,136,128]{3,2,1,0:T(8,128)S(1)} %shard_map.69.own_ref, f32[2,4,136,128]{3,2,1,0:T(8,128)S(1)} %convert_element_type.39.refs_0_), custom_call_target="tpu_custom_call" | custom-call | flops 2785280 | bytes 1671168 | tf_op jit(solution)/shard_map/pallas_call | solution.py:249
  36.6 2.1 %collective-permute-start.3 = (f16[2,4,136,128]{3,2,1,0:T(8,128)(2,1)S(1)}, f16[2,4,136,128]{3,2,1,0:T(8,128)(2,1)S(1)}, u32[]{:S(2)}, u32[]{:S(2)}) collective-permute-start(f16[2,4,136,128]{3,2,1,0:T(8,128)(2,1)S(1)} %convert_element_type.40), channel_id=1, source_target_pairs={{0,4},{1,5},{2,6},{3,7},{4,0},{5,1},{6,2},{7,3},{8,12},{9,13},{10,... | collective-permute-start | bytes 835592 | tf_op jit(solution)/shard_map/ppermute | solution.py:25
  38.7 5.7 %shard_map.70.own_ref = f32[2,4,136,128]{3,2,1,0:T(8,128)S(1)} custom-call(s32[1]{0:T(128)} %bitcast.at_ref, bf16[512,1024]{1,0:T(8,128)(2,1)S(1)} %get-tuple-element.36.q_ref, bf16[2048,512]{1,0:T(8,128)(2,1)S(1)} %get-tuple-element.26.refs_0_, bf16[512,2048]{1,0:T(8,128)(2,1)S(1)} %get-tuple-element.27.refs_1_, ...), custom_call_target="tpu_custom_call" | custom-call | flops 2147483648 | bytes 557056 | tf_op jit(solution)/shard_map/pallas_call | solution.py:224
  44.4 0.0 collective-permute-done.1
  44.4 0.3 shard_map.71.own_ref
  44.8 0.0 copy-start
  44.8 0.7 %collective-permute-done.3 = f16[2,4,136,128]{3,2,1,0:T(8,128)(2,1)S(1)} collective-permute-done((f16[2,4,136,128]{3,2,1,0:T(8,128)(2,1)S(1)}, f16[2,4,136,128]{3,2,1,0:T(8,128)(2,1)S(1)}, u32[]{:S(2)}, u32[]{:S(2)}) %collective-permute-start.3) | collective-permute-done | bytes 278560 | tf_op jit(solution)/shard_map/ppermute | solution.py:25
  45.5 1.2 %shard_map.73 = (f32[2,136,128]{2,1,0:T(8,128)S(1)}, f32[2,136,128]{2,1,0:T(8,128)S(1)}, f32[2,136,128]{2,1,0:T(8,128)S(1)}, f32[2,136,128]{2,1,0:T(8,128)S(1)}) custom-call(s32[5]{0:T(128)S(1)} %stack.23.at_ref, f32[2,4,136,128]{3,2,1,0:T(8,128)S(1)} %shard_map.71.own_ref, f32[2,4,136,128]{3,2,1,0:T(8,128)S(1)} %convert_element_type.41.refs_0_), custom_call_target="tpu_custom_call" | custom-call | flops 2785280 | bytes 1671168 | tf_op jit(solution)/shard_map/pallas_call | solution.py:270
  46.7 3.9 %collective-permute-start.6 = (f16[2,136,128]{2,1,0:T(8,128)(2,1)S(1)}, f16[2,136,128]{2,1,0:T(8,128)(2,1)S(1)}, u32[]{:S(2)}, u32[]{:S(2)}) collective-permute-start(f16[2,136,128]{2,1,0:T(8,128)(2,1)S(1)} %convert_element_type.46), channel_id=1, source_target_pairs={{0,24},{1,25},{2,26},{3,27},{4,28},{5,29},{6,30},{7,31},{8,16},{9,... | collective-permute-start | bytes 208904 | tf_op jit(solution)/shard_map/ppermute | solution.py:25
  50.6 0.0 collective-permute-start.5
  50.6 0.7 %collective-permute-start.4 = (f16[2,136,128]{2,1,0:T(8,128)(2,1)S(1)}, f16[2,136,128]{2,1,0:T(8,128)(2,1)S(1)}, u32[]{:S(2)}, u32[]{:S(2)}) collective-permute-start(f16[2,136,128]{2,1,0:T(8,128)(2,1)S(1)} %convert_element_type.42), channel_id=1, source_target_pairs={{0,8},{1,9},{2,10},{3,11},{4,12},{5,13},{6,14},{7,15},{8,0},{9,1},... | collective-permute-start | bytes 208904 | tf_op jit(solution)/shard_map/ppermute | solution.py:25
  51.3 2.3 %collective-permute-done.6 = f16[2,136,128]{2,1,0:T(8,128)(2,1)S(1)} collective-permute-done((f16[2,136,128]{2,1,0:T(8,128)(2,1)S(1)}, f16[2,136,128]{2,1,0:T(8,128)(2,1)S(1)}, u32[]{:S(2)}, u32[]{:S(2)}) %collective-permute-start.6) | collective-permute-done | bytes 69664 | tf_op jit(solution)/shard_map/ppermute | solution.py:25
  53.6 2.5 %collective-permute-done.5 = f16[2,136,128]{2,1,0:T(8,128)(2,1)S(1)} collective-permute-done((f16[2,136,128]{2,1,0:T(8,128)(2,1)S(1)}, f16[2,136,128]{2,1,0:T(8,128)(2,1)S(1)}, u32[]{:S(2)}, u32[]{:S(2)}) %collective-permute-start.5) | collective-permute-done | bytes 69664 | tf_op jit(solution)/shard_map/ppermute | solution.py:25
  56.1 0.0 collective-permute-done.4
  56.1 0.2 shard_map.74.refs_0_
  56.4 1.6 %collective-permute-start.8 = (f32[256,128]{1,0:T(8,128)S(1)}, f32[256,128]{1,0:T(8,128)S(1)}, u32[]{:S(2)}, u32[]{:S(2)}) collective-permute-start(f32[256,128]{1,0:T(8,128)S(1)} %shard_map.74.refs_0_), channel_id=1, source_target_pairs={{0,2},{1,3},{2,0},{3,1},{4,6},{5,7},{6,4},{7,5},{8,10},{9,11},{10,... | collective-permute-start | bytes 393224 | tf_op jit(solution)/shard_map/ppermute | solution.py:25
  58.0 0.0 collective-permute-start.7
  58.0 3.4 %collective-permute-done.8.refs_2_ = f32[256,128]{1,0:T(8,128)S(1)} collective-permute-done((f32[256,128]{1,0:T(8,128)S(1)}, f32[256,128]{1,0:T(8,128)S(1)}, u32[]{:S(2)}, u32[]{:S(2)}) %collective-permute-start.8) | collective-permute-done | bytes 131104 | tf_op jit(solution)/shard_map/ppermute | solution.py:25
  61.4 0.0 collective-permute-start.9
  61.4 0.0 collective-permute-done.7.refs_1_
  61.4 1.3 %collective-permute-done.9.refs_3_ = f32[256,128]{1,0:T(8,128)S(1)} collective-permute-done((f32[256,128]{1,0:T(8,128)S(1)}, f32[256,128]{1,0:T(8,128)S(1)}, u32[]{:S(2)}, u32[]{:S(2)}) %collective-permute-start.9) | collective-permute-done | bytes 131104 | tf_op jit(solution)/shard_map/ppermute | solution.py:25
  62.8 0.0 copy-done
  62.8 1.5 %shard_map.75 = bf16[128,256]{1,0:T(8,128)(2,1)} custom-call(s32[5]{0:T(128)S(1)} %stack.23.at_ref, f32[256,128]{1,0:T(8,128)S(1)} %shard_map.74.refs_0_, f32[256,128]{1,0:T(8,128)S(1)} %collective-permute-done.7.refs_1_, f32[256,128]{1,0:T(8,128)S(1)} %collective-permute-done.8.refs_2_, f32[256,128]{1,0:T(8,128)S(1)} %collective-permute-done.9.refs_3_, ...), custom_call_target="tpu_custom_call" | custom-call | flops 67108864 | bytes 524288 | tf_op jit(solution)/shard_map/pallas_call | solution.py:319
  (12 shorter events, 0.3 us)
Async XLA Ops:
  0.0 11.9 %collective-permute-start = (bf16[2048,1024]{1,0:T(8,128)(2,1)}, bf16[2048,1024]{1,0:T(8,128)(2,1)}, u32[]{:S(2)}, u32[]{:S(2)}) collective-permute-start(bf16[2048,1024]{1,0:T(8,128)(2,1)} %t_hbm.1), channel_id=1, source_target_pairs={{0,1},{1,0},{2,3},{3,2},{4,5},{5,4},{6,7},{7,6},{8,9},{9,8},{10,11... | collective-permute-start | bytes 12582920 | tf_op jit(solution)/shard_map/ppermute | solution.py:25
  21.8 14.0 %collective-permute-start.2 = (f16[2,4,136,128]{3,2,1,0:T(8,128)(2,1)S(1)}, f16[2,4,136,128]{3,2,1,0:T(8,128)(2,1)S(1)}, u32[]{:S(2)}, u32[]{:S(2)}) collective-permute-start(f16[2,4,136,128]{3,2,1,0:T(8,128)(2,1)S(1)} %convert_element_type.38), channel_id=1, source_target_pairs={{0,2},{1,3},{2,0},{3,1},{4,6},{5,7},{6,4},{7,5},{8,10},{9,11},{10,... | collective-permute-start | bytes 835592 | tf_op jit(solution)/shard_map/ppermute | solution.py:25
  30.2 14.2 %collective-permute-start.1 = (f16[2,4,136,128]{3,2,1,0:T(8,128)(2,1)S(1)}, f16[2,4,136,128]{3,2,1,0:T(8,128)(2,1)S(1)}, u32[]{:S(2)}, u32[]{:S(2)}) collective-permute-start(f16[2,4,136,128]{3,2,1,0:T(8,128)(2,1)S(1)} %convert_element_type.36), channel_id=1, source_target_pairs={{0,2},{1,3},{2,0},{3,1},{4,6},{5,7},{6,4},{7,5},{8,10},{9,11},{10,... | collective-permute-start | bytes 835592 | tf_op jit(solution)/shard_map/ppermute | solution.py:25
  36.6 8.9 %collective-permute-start.3 = (f16[2,4,136,128]{3,2,1,0:T(8,128)(2,1)S(1)}, f16[2,4,136,128]{3,2,1,0:T(8,128)(2,1)S(1)}, u32[]{:S(2)}, u32[]{:S(2)}) collective-permute-start(f16[2,4,136,128]{3,2,1,0:T(8,128)(2,1)S(1)} %convert_element_type.40), channel_id=1, source_target_pairs={{0,4},{1,5},{2,6},{3,7},{4,0},{5,1},{6,2},{7,3},{8,12},{9,13},{10,... | collective-permute-start | bytes 835592 | tf_op jit(solution)/shard_map/ppermute | solution.py:25
  44.8 18.0 %copy-start = (bf16[1024,256]{1,0:T(8,128)(2,1)S(1)}, bf16[1024,256]{1,0:T(8,128)(2,1)}, u32[]{:S(2)}) copy-start(bf16[1024,256]{1,0:T(8,128)(2,1)} %refs_4_.1) | copy-start | bytes 1572868
  46.7 6.9 %collective-permute-start.6 = (f16[2,136,128]{2,1,0:T(8,128)(2,1)S(1)}, f16[2,136,128]{2,1,0:T(8,128)(2,1)S(1)}, u32[]{:S(2)}, u32[]{:S(2)}) collective-permute-start(f16[2,136,128]{2,1,0:T(8,128)(2,1)S(1)} %convert_element_type.46), channel_id=1, source_target_pairs={{0,24},{1,25},{2,26},{3,27},{4,28},{5,29},{6,30},{7,31},{8,16},{9,... | collective-permute-start | bytes 208904 | tf_op jit(solution)/shard_map/ppermute | solution.py:25
  50.6 5.5 %collective-permute-start.5 = (f16[2,136,128]{2,1,0:T(8,128)(2,1)S(1)}, f16[2,136,128]{2,1,0:T(8,128)(2,1)S(1)}, u32[]{:S(2)}, u32[]{:S(2)}) collective-permute-start(f16[2,136,128]{2,1,0:T(8,128)(2,1)S(1)} %convert_element_type.44), channel_id=1, source_target_pairs={{0,16},{1,17},{2,18},{3,19},{4,20},{5,21},{6,22},{7,23},{8,24},{9,... | collective-permute-start | bytes 208904 | tf_op jit(solution)/shard_map/ppermute | solution.py:25
  50.6 5.5 %collective-permute-start.4 = (f16[2,136,128]{2,1,0:T(8,128)(2,1)S(1)}, f16[2,136,128]{2,1,0:T(8,128)(2,1)S(1)}, u32[]{:S(2)}, u32[]{:S(2)}) collective-permute-start(f16[2,136,128]{2,1,0:T(8,128)(2,1)S(1)} %convert_element_type.42), channel_id=1, source_target_pairs={{0,8},{1,9},{2,10},{3,11},{4,12},{5,13},{6,14},{7,15},{8,0},{9,1},... | collective-permute-start | bytes 208904 | tf_op jit(solution)/shard_map/ppermute | solution.py:25
  56.4 5.0 %collective-permute-start.8 = (f32[256,128]{1,0:T(8,128)S(1)}, f32[256,128]{1,0:T(8,128)S(1)}, u32[]{:S(2)}, u32[]{:S(2)}) collective-permute-start(f32[256,128]{1,0:T(8,128)S(1)} %shard_map.74.refs_0_), channel_id=1, source_target_pairs={{0,2},{1,3},{2,0},{3,1},{4,6},{5,7},{6,4},{7,5},{8,10},{9,11},{10,... | collective-permute-start | bytes 393224 | tf_op jit(solution)/shard_map/ppermute | solution.py:25
  58.0 3.4 %collective-permute-start.7 = (f32[256,128]{1,0:T(8,128)S(1)}, f32[256,128]{1,0:T(8,128)S(1)}, u32[]{:S(2)}, u32[]{:S(2)}) collective-permute-start(f32[256,128]{1,0:T(8,128)S(1)} %shard_map.74.refs_0_), channel_id=1, source_target_pairs={{0,1},{1,0},{2,3},{3,2},{4,5},{5,4},{6,7},{7,6},{8,9},{9,8},{10,11... | collective-permute-start | bytes 393224 | tf_op jit(solution)/shard_map/ppermute | solution.py:25
  61.4 1.3 %collective-permute-start.9 = (f32[256,128]{1,0:T(8,128)S(1)}, f32[256,128]{1,0:T(8,128)S(1)}, u32[]{:S(2)}, u32[]{:S(2)}) collective-permute-start(f32[256,128]{1,0:T(8,128)S(1)} %collective-permute-done.8.refs_2_), channel_id=1, source_target_pairs={{0,1},{1,0},{2,3},{3,2},{4,5},{5,4},{6,7},{7,6},{8,9},{9,8},{10,11... | collective-permute-start | bytes 393224 | tf_op jit(solution)/shard_map/ppermute | solution.py:25
